TPU v7x, 256 devices: a whole 4x4x8 slice. The times are simulated.
256 devices in a mesh: row: 8 (over y, x_lo), col: 32 (over z, x_hi, core).
Axes of the slice: x: 4 (x_hi: 2, x_lo: 2; x = x_hi * 2 + x_lo), y: 4, z: 8, core: 2. Of those that a mesh axis runs over, the one named last changes fastest.
Arguments:
- weight_change: bfloat16 [8192, 28672], P('row', 'col'), may hold values from -6 to 6
- error_buffer: float32 [8192, 28672], P('row', 'col'), may hold values from -6 to 6
- basis: float32 [28672, 64], P('col'), may hold values from -6 to 6
- rollout_weight: bfloat16 [8192, 28672], P('col', 'row'), may hold values from -1.5 to 1.5
Outputs:
- new_error: float32 [8192, 28672], P('row', 'col')
- new_basis: float32 [28672, 64], P('col')
- new_rollout: bfloat16 [8192, 28672], P('col', 'row')
All inputs are finite; a program needn't handle non-finite values.
Results may differ from a plain program's by a relative error of at most 0.0057.
Values may be sent and summed in bfloat16 or wider, within the bound.
No kernel may reach another device: no remote copies, remote signals or barrier semaphores. Data moves between devices by JAX's collectives and lax.ppermute only.
A program may use at most 64 MiB of HBM per device.

v0:
```python
import jax
import jax.numpy as jnp
from jax import lax
from jax.sharding import PartitionSpec as P


def orthonormal(rows, gram):
    lower = jnp.linalg.cholesky(gram)
    return lax.linalg.triangular_solve(lower, rows, left_side=False, lower=True, transpose_a=True)


def gram_of(rows):
    return jnp.dot(
        rows.T, rows, precision=lax.Precision.HIGHEST, preferred_element_type=jnp.float32
    )


def local(weight_change, error_buffer, basis, rollout_weight):
    total = weight_change.astype(jnp.float32) + error_buffer
    partial_value = jnp.dot(
        total, basis, precision=lax.Precision.HIGHEST, preferred_element_type=jnp.float32
    )
    left = lax.psum(partial_value, "col")
    gram = lax.psum(gram_of(left), "row")
    left_round = orthonormal(left, gram).astype(jnp.bfloat16)
    right_part = lax.dot_general(
        total,
        left_round.astype(jnp.float32),
        (((0,), (0,)), ((), ())),
        precision=lax.Precision.HIGHEST,
        preferred_element_type=jnp.float32,
    )
    new_basis = lax.psum(right_part, "row")
    right_round = new_basis.astype(jnp.bfloat16)
    delta = lax.dot_general(
        left_round, right_round, (((1,), (1,)), ((), ())), preferred_element_type=jnp.float32
    )
    new_error = total - delta
    row_count = rollout_weight.shape[0]
    unit_count = rollout_weight.shape[1]
    all_left = lax.all_gather(left_round, "row", axis=0, tiled=True)
    all_right = lax.all_gather(right_round, "col", axis=0, tiled=True)
    my_left = lax.dynamic_slice_in_dim(all_left, lax.axis_index("col") * row_count, row_count, 0)
    my_right = lax.dynamic_slice_in_dim(
        all_right, lax.axis_index("row") * unit_count, unit_count, 0
    )
    rollout_delta = lax.dot_general(
        my_left, my_right, (((1,), (1,)), ((), ())), preferred_element_type=jnp.float32
    )
    new_rollout = (rollout_weight.astype(jnp.float32) + rollout_delta).astype(jnp.bfloat16)
    return (new_error, new_basis, new_rollout)


def solution(mesh):
    in_specs = (P("row", "col"), P("row", "col"), P("col", None), P("col", "row"))
    out_specs = (P("row", "col"), P("col", None), P("col", "row"))
    return jax.shard_map(local, mesh=mesh, in_specs=in_specs, out_specs=out_specs, check_vma=False)
```

profile of v0, /device:TPU:1, one launch (start us, length us, event | category | flops | bytes accessed | tf_op | source)
XLA Modules:
  0.0 557.0 jit_solution(9175333400143934756)
XLA Ops:
  7.2 0.0 copy-start
  7.2 0.0 copy-start.1
  7.2 0.0 all-reduce.3.cloned.1.call-start
  7.2 0.9 copy-done
  8.1 7.2 %fusion.2 = f32[1024,64]{0,1:T(8,128)} fusion(f32[896,64]{0,1:T(8,128)S(1)} %copy-done, f32[1024,896]{1,0:T(8,128)} %param.5, bf16[1024,896]{1,0:T(8,128)(2,1)} %param.4), kind=kOutput, calls=%fused_computation.5 | convolution fusion | flops 706478080 | bytes 5996544 | tf_op jit(solution)/shard_map/dot_general | solution.py:20
  15.3 0.0 all-reduce.3.cloned.1.call-update
  15.3 0.0 all-reduce.5.cloned.1.call-start
  15.4 270.1 %all-reduce.3.cloned.1.call-done = f32[1024,64]{0,1:T(8,128)} async-done(((f32[1024,64]{0,1:T(8,128)}), f32[1024,64]{0,1:T(8,128)}) %all-reduce.3.cloned.1.call-update) | async-done | bytes 262160 | tf_op jit(solution)/shard_map/psum | solution.py:23
  285.4 1.4 fusion.9
  286.8 26.3 %psum.22 = f32[64,64]{0,1:T(8,128)S(1)} all-reduce(f32[64,64]{0,1:T(8,128)S(1)} %fusion.9), channel_id=1, replica_groups=mesh['row'=8,'col'=32] {'row'}, use_global_device_ids=true, to_apply=%region_1.0 | all-reduce | flops 4096 | bytes 32768 | tf_op jit(solution)/shard_map/psum | solution.py:24
  313.1 0.1 copy.8
  313.2 5.8 %cholesky.16 = f32[64,64]{1,0:T(8,128)S(1)} custom-call(f32[64,64]{1,0:T(8,128)S(1)} %fusion.6), custom_call_target="Cholesky" | custom-call | tf_op jit(solution)/shard_map/jit(cholesky)/cholesky | solution.py:8
  319.1 0.6 compare_reduce_fusion
  319.8 0.7 fusion.4
  320.4 4.9 custom-call.6
  325.3 1.4 convolution_convert_fusion
  326.7 0.0 copy-start.2
  326.7 0.0 copy-done.1
  326.7 4.4 fusion.1
  331.1 0.0 all-reduce.5.cloned.1.call-update
  331.1 0.0 all-gather.3.cloned.1.call-start
  331.2 0.0 copy-done.2
  331.2 0.7 all-gather.3.cloned.1.call-update
  331.8 0.0 all-gather.5.cloned.1.call-start
  331.9 75.8 %all-reduce.5.cloned.1.call-done = f32[896,64]{0,1:T(8,128)} async-done(((f32[896,64]{0,1:T(8,128)}), f32[896,64]{0,1:T(8,128)}) %all-reduce.5.cloned.1.call-update) | async-done | bytes 229392 | tf_op jit(solution)/shard_map/psum | solution.py:33
  407.7 1.6 convert_element_type.18
  409.3 0.0 all-gather.5.cloned.1.call-update
  409.4 4.7 convolution_subtract_fusion
  414.1 39.4 %all-gather.3.cloned.1.call-done = bf16[8192,64]{0,1:T(8,128)(2,1)} async-done(((bf16[1024,64]{0,1:T(8,128)(2,1)}), bf16[8192,64]{0,1:T(8,128)(2,1)}) %all-gather.3.cloned.1.call-update) | async-done | bytes 1048592 | tf_op jit(solution)/shard_map/all_gather | solution.py:41
  453.4 92.8 %all-gather.5.cloned.1.call-done = bf16[28672,64]{0,1:T(8,128)(2,1)} async-done(((bf16[896,64]{0,1:T(8,128)(2,1)}), bf16[28672,64]{0,1:T(8,128)(2,1)}) %all-gather.5.cloned.1.call-update) | async-done | bytes 3670032 | tf_op jit(solution)/shard_map/all_gather | solution.py:42
  546.3 3.6 fusion
  549.8 0.7 copy.12
  (4 shorter events, 0.0 us)
Async XLA Ops:
  7.2 0.9 copy-start
  7.2 319.5 %copy-start.1 = (bf16[1024,896]{1,0:T(8,128)(2,1)S(1)}, bf16[1024,896]{1,0:T(8,128)(2,1)}, u32[]{:S(2)}) copy-start(bf16[1024,896]{1,0:T(8,128)(2,1)} %param.4) | copy-start | bytes 5505028
  7.2 278.3 %all-reduce.3.cloned.1.call-start = ((), (), s32[]{:S(2)}) async-start(), calls=%async_computation | async-start | bytes 524288 | tf_op jit(solution)/shard_map/psum | solution.py:23
  15.3 392.4 %all-reduce.5.cloned.1.call-start = ((), (), s32[]{:S(2)}) async-start(), calls=%async_computation.1 | async-start | bytes 458752 | tf_op jit(solution)/shard_map/psum | solution.py:33
  326.7 4.5 copy-start.2
  331.1 122.3 %all-gather.3.cloned.1.call-start = ((), (), s32[]{:S(2)}) async-start(), calls=%async_computation.2 | async-start | bytes 1179648 | tf_op jit(solution)/shard_map/all_gather | solution.py:41
  331.8 214.4 %all-gather.5.cloned.1.call-start = ((), (), s32[]{:S(2)}) async-start(), calls=%async_computation.3 | async-start | bytes 3784704 | tf_op jit(solution)/shard_map/all_gather | solution.py:42
  414.1 135.8 %copy-start.3 = (f32[896,64]{0,1:T(8,128)S(1)}, f32[896,64]{0,1:T(8,128)}, u32[]{:S(2)}) copy-start(f32[896,64]{0,1:T(8,128)} %all-reduce.5.cloned.1.call-done) | copy-start | bytes 688132
Sparse Core Ops, SparseCore 0:
  15.5 269.9 all-reduce.2
  331.2 76.4 all-reduce.4
  410.1 43.2 all-gather.2
  456.6 89.6 all-gather.4
where the time goes:
time: 557 us
  waiting for transfers between devices  479 us (86%)
  blocking collectives  26.3 us (5%)
  matrix products  22.6 us (4%)
  between operations  13.8 us (2%)
  other arithmetic  13.7 us (2%)
    psum x1, waiting for transfers between devices, local(): left = lax.psum(partial_value, 'col')  270 us
    all_gather x1, waiting for transfers between devices, local(): all_right = lax.all_gather(right_round, 'col', axis=0, tiled=True)  92.8 us
    psum x1, waiting for transfers between devices, local(): new_basis = lax.psum(right_part, 'row')  75.8 us
    all_gather x1, waiting for transfers between devices, local(): all_left = lax.all_gather(left_round, 'row', axis=0, tiled=True)  39.4 us
    psum x1, blocking collectives, local(): gram = lax.psum(gram_of(left), 'row')  26.3 us
  transfers between devices with their start and end apart: 4, of which 4 were waited for; matrix products, arithmetic and copies ran while one was open for 1% of the time, Pallas kernels for 0%

commit v1 on v0

v1 whole, which is shorter than its diff:
```python
import jax
import jax.numpy as jnp
from jax import lax
from jax.sharding import PartitionSpec as P

HIGHEST = lax.Precision.HIGHEST
ROWS, COLS, R = 8, 32, 64
AXES = ("row", "col")


def swap(flip):
    return [
        (r * COLS + c, (c // 4) * COLS + 4 * r + ((c % 4) ^ flip))
        for r in range(ROWS)
        for c in range(COLS)
    ]


def dot(a, b, ca, cb, precision=None):
    return lax.dot_general(
        a, b, (((ca,), (cb,)), ((), ())), precision=precision, preferred_element_type=jnp.float32
    )


def sum_then_share(parts, axis):
    n = parts.shape[0]
    mine = jnp.sum(lax.all_to_all(parts, axis, 0, 0), axis=0)
    return lax.all_to_all(jnp.broadcast_to(mine[None], (n,) + mine.shape), axis, 0, 0)


def local(weight_change, error_buffer, basis, rollout_weight):
    q = lax.axis_index("col") % 4
    total = weight_change.astype(jnp.float32) + error_buffer
    rows, units = total.shape
    part = dot(basis, total, 0, 1, HIGHEST)
    part = part.reshape(8, 8, 4, rows // 4).transpose(0, 2, 1, 3).reshape(COLS, 8, rows // 4)
    left = sum_then_share(part, "col")
    left = left.reshape(8, 4, 8, rows // 4).transpose(0, 2, 1, 3).reshape(R, rows)
    mine = lax.dynamic_slice_in_dim(left, q * (rows // 4), rows // 4, 1)
    my_left = lax.ppermute(mine, AXES, swap(0))
    gram_part = dot(left, left, 1, 1, HIGHEST)
    right_part = dot(left, total, 1, 0, HIGHEST)
    gram_lanes = gram_part.reshape(8, 8, R).transpose(1, 0, 2).reshape(8, 8 * R)
    sent = jnp.concatenate(
        [right_part.reshape(ROWS, 8, units), jnp.broadcast_to(gram_lanes[None], (ROWS, 8, 8 * R))], 2
    )
    got = jnp.sum(lax.all_to_all(sent, "row", 0, 0), axis=0)
    gram = got[:, units:].reshape(8, 8, R).transpose(1, 0, 2).reshape(R, R)
    mine = got[:, :units]
    right = lax.all_to_all(jnp.broadcast_to(mine[None], (ROWS, 8, units)), "row", 0, 0)
    right = right.reshape(R, units)
    lower = jnp.linalg.cholesky(gram)
    inverse = lax.linalg.triangular_solve(
        lower, jnp.eye(R, dtype=jnp.float32), left_side=True, lower=True
    )
    new_basis = dot(inverse, right, 1, 0, HIGHEST)
    right_round = new_basis.astype(jnp.bfloat16)
    blocks = [lax.ppermute(right_round, AXES, swap(k)) for k in range(4)]
    left_round = dot(inverse, left, 1, 0, HIGHEST).astype(jnp.bfloat16)
    delta = dot(left_round, right_round, 0, 0)
    new_error = total - delta
    my_left_round = dot(inverse, my_left, 1, 0, HIGHEST).astype(jnp.bfloat16)
    first = jnp.where((q & 1) == 0, jnp.stack(blocks), jnp.stack([blocks[k ^ 1] for k in range(4)]))
    both = jnp.where((q & 2) == 0, first, jnp.stack([first[k ^ 2] for k in range(4)]))
    my_right = both.transpose(1, 0, 2).reshape(R, 4 * units)
    rollout_delta = dot(my_left_round, my_right, 0, 0)
    new_rollout = (rollout_weight.astype(jnp.float32) + rollout_delta).astype(jnp.bfloat16)
    return (new_error, new_basis.T, new_rollout)


def solution(mesh):
    in_specs = (P("row", "col"), P("row", "col"), P("col", None), P("col", "row"))
    out_specs = (P("row", "col"), P("col", None), P("col", "row"))
    return jax.shard_map(local, mesh=mesh, in_specs=in_specs, out_specs=out_specs, check_vma=False)
```

time: 557 us -> 142 us (0.25)
  the two profiles are of different devices: /device:TPU:1 before, /device:TPU:225 now
where the time goes in v1:
time: 142 us; the launch traced here: 141 us
  waiting for transfers between devices  38.7 us (27%)
  blocking collectives  35.4 us (25%)
  starting transfers between devices  31.9 us (22%)
  matrix products  19.5 us (14%)
  other arithmetic  13.2 us (9%)
  local copies, waits for them, and re-layouts  2 us (1%)
    ppermute x4, waiting for transfers between devices, local(): blocks = [lax.ppermute(right_round, AXES, swap(k)) for k in range(4)]  33 us
    dot_general x8, matrix products, dot(): lax.dot_general(a, b, (((ca,), (cb,)), ((), ())), precision=precision, pr...  19.3 us
    all_to_all x1, blocking collectives, sum_then_share(): mine = jnp.sum(lax.all_to_all(parts, axis, 0, 0), axis=0)  18.5 us
    all_to_all x1, blocking collectives, sum_then_share(): lax.all_to_all(jnp.broadcast_to(mine[None], (n,) + mine.shape), axis, 0, 0)  16.9 us
    ppermute x4, starting transfers between devices, local(): blocks = [lax.ppermute(right_round, AXES, swap(k)) for k in range(4)]  16 us
    ppermute x1, starting transfers between devices, local(): my_left = lax.ppermute(mine, AXES, swap(0))  8.26 us
    another operation x3, other arithmetic, local(): lower = jnp.linalg.cholesky(gram)  6.52 us
    all_to_all x1, waiting for transfers between devices, local(): lax.all_to_all(jnp.broadcast_to(mine[None], (ROWS, 8, units)), 'row', 0, 0)  5.68 us
  transfers between devices with their start and end apart: 7, of which 5 were waited for; matrix products, arithmetic and copies ran while one was open for 13% of the time, Pallas kernels for 0%

profile of v1, /device:TPU:225, one launch (start us, length us, event | category | flops | bytes accessed | tf_op | source)
XLA Modules:
  0.0 141.5 jit_solution(11029389898280068678)
XLA Ops:
  0.7 0.9 copy-done
  1.6 6.5 %fusion.3 = f32[1024,64]{0,1:T(8,128)S(1)} fusion(f32[896,64]{0,1:T(8,128)S(1)} %copy-done, f32[1024,896]{1,0:T(8,128)} %param.5, bf16[1024,896]{1,0:T(8,128)(2,1)} %param.4), kind=kOutput, calls=%fused_computation.6 | convolution fusion | flops 706478080 | bytes 5996544 | tf_op jit(solution)/shard_map/dot_general | solution.py:20
  8.1 18.5 %all_to_all.20 = f32[32,8,256]{2,1,0:T(8,128)S(1)} all-to-all(f32[32,8,256]{2,1,0:T(8,128)S(1)} %bitcast.69), channel_id=1, replica_groups=mesh['row'=8,'col'=32] {'col'}, dimensions={0} | all-to-all | bytes 524288 | tf_op jit(solution)/shard_map/all_to_all | solution.py:27
  26.7 16.9 %all_to_all.21 = f32[32,8,256]{2,1,0:T(8,128)S(1)} all-to-all(f32[32,8,256]{2,1,0:T(8,128)S(1)} %broadcast_in_dim.9), channel_id=1, replica_groups=mesh['row'=8,'col'=32] {'col'}, dimensions={0} | all-to-all | bytes 524288 | tf_op jit(solution)/shard_map/all_to_all | solution.py:28
  43.5 4.4 %fusion.1 = f32[8,8,896]{2,1,0:T(8,128)S(1)} fusion(f32[8,8,1024]{2,1,0:T(8,128)S(1)} %bitcast.63, f32[1024,896]{1,0:T(8,128)} %param.5, bf16[1024,896]{1,0:T(8,128)(2,1)S(1)} %copy-done.1), kind=kOutput, calls=%fused_computation.2 | convolution fusion | flops 706478080 | bytes 5996544 | tf_op jit(solution)/shard_map/dot_general | solution.py:20
  47.9 0.4 convolution_bitcast_fusion
  48.4 0.8 pad_maximum_fusion
  49.2 4.2 %all-to-all-start.2 = ((f32[8,8,1408]{2,1,0:T(8,128)}), f32[8,8,1408]{2,1,0:T(8,128)S(1)}, u32[]{:S(2)}, u32[]{:S(2)}) async-start(f32[8,8,1408]{2,1,0:T(8,128)} %pad_maximum_fusion), calls=%async_computation.2 | async-start | bytes 720896 | tf_op jit(solution)/shard_map/all_to_all | solution.py:47
  53.4 8.3 %collective-permute-start = (f32[64,256]{1,0:T(8,128)S(1)}, f32[64,256]{1,0:T(8,128)S(1)}, u32[]{:S(2)}, u32[]{:S(2)}) collective-permute-start(f32[64,256]{1,0:T(8,128)S(1)} %constant_dynamic-slice_fusion), channel_id=1, source_target_pairs={{0,0},{1,1},{2,2},{3,3},{4,32},{5,33},{6,34},{7,35},{8,64},{9,65},... | collective-permute-start | bytes 196616 | tf_op jit(solution)/shard_map/ppermute | solution.py:40
  61.8 0.1 copy.10
  61.9 5.8 %cholesky.17 = f32[64,64]{1,0:T(8,128)S(1)} custom-call(f32[64,64]{1,0:T(8,128)S(1)} %fusion.10), custom_call_target="Cholesky" | custom-call | tf_op jit(solution)/shard_map/jit(cholesky)/cholesky | solution.py:52
  67.8 0.6 compare_reduce_fusion
  68.4 0.7 fusion.7
  69.1 4.9 %custom-call.6 = f32[1,64,64]{1,2,0:T(8,128)S(1)} custom-call(f32[1,64,64]{2,1,0:T(8,128)S(1)} %fusion.7), custom_call_target="InvertDiagBlocksLowerTriangular" | custom-call | tf_op jit(solution)/shard_map/triangular_solve | solution.py:53
  74.0 0.2 fusion.8
  74.2 0.4 convolution_convert_fusion
  74.6 0.7 broadcast_in_dim.24
  75.3 3.4 %all-to-all-start.3 = ((f32[8,8,896]{2,1,0:T(8,128)}), f32[8,8,896]{2,1,0:T(8,128)S(1)}, u32[]{:S(2)}, u32[]{:S(2)}) async-start(f32[8,8,896]{2,1,0:T(8,128)} %broadcast_in_dim.24), calls=%async_computation.3 | async-start | bytes 458752 | tf_op jit(solution)/shard_map/all_to_all | solution.py:50
  78.7 0.2 convolution_convert_fusion.1
  78.9 5.7 %all-to-all-done.3 = f32[8,8,896]{2,1,0:T(8,128)S(1)} async-done(((f32[8,8,896]{2,1,0:T(8,128)}), f32[8,8,896]{2,1,0:T(8,128)S(1)}, u32[]{:S(2)}, u32[]{:S(2)}) %all-to-all-start.3) | async-done | bytes 229408 | tf_op jit(solution)/shard_map/all_to_all | solution.py:50
  84.6 1.0 fusion.12
  85.6 6.6 %collective-permute-start.4 = (bf16[64,896]{1,0:T(8,128)(2,1)S(1)}, bf16[64,896]{1,0:T(8,128)(2,1)S(1)}, u32[]{:S(2)}, u32[]{:S(2)}) collective-permute-start(bf16[64,896]{1,0:T(8,128)(2,1)S(1)} %get-tuple-element.5), channel_id=1, source_target_pairs={{0,3},{1,2},{2,1},{3,0},{4,35},{5,34},{6,33},{7,32},{8,67},{9,66},... | collective-permute-start | bytes 344072 | tf_op jit(solution)/shard_map/ppermute | solution.py:58
  92.2 7.5 %collective-permute-start.3 = (bf16[64,896]{1,0:T(8,128)(2,1)S(1)}, bf16[64,896]{1,0:T(8,128)(2,1)S(1)}, u32[]{:S(2)}, u32[]{:S(2)}) collective-permute-start(bf16[64,896]{1,0:T(8,128)(2,1)S(1)} %get-tuple-element.5), channel_id=1, source_target_pairs={{0,2},{1,3},{2,0},{3,1},{4,34},{5,35},{6,32},{7,33},{8,66},{9,67},... | collective-permute-start | bytes 344072 | tf_op jit(solution)/shard_map/ppermute | solution.py:58
  99.8 1.9 %collective-permute-start.1 = (bf16[64,896]{1,0:T(8,128)(2,1)S(1)}, bf16[64,896]{1,0:T(8,128)(2,1)S(1)}, u32[]{:S(2)}, u32[]{:S(2)}) collective-permute-start(bf16[64,896]{1,0:T(8,128)(2,1)S(1)} %get-tuple-element.5), channel_id=1, source_target_pairs={{0,0},{1,1},{2,2},{3,3},{4,32},{5,33},{6,34},{7,35},{8,64},{9,65},... | collective-permute-start | bytes 344072 | tf_op jit(solution)/shard_map/ppermute | solution.py:58
  101.7 4.5 %convolution_subtract_fusion = f32[1024,896]{1,0:T(8,128)} fusion(bf16[64,1024]{1,0:T(8,128)(2,1)S(1)} %convolution_convert_fusion, bf16[64,896]{1,0:T(8,128)(2,1)S(1)} %get-tuple-element.5, f32[1024,896]{1,0:T(8,128)} %param.5, bf16[1024,896]{1,0:T(8,128)(2,1)S(1)} %copy-done.1), kind=kOutput, calls=%fused_computation.5 | convolution fusion | flops 120193024 | bytes 9420800 | tf_op jit(solution)/shard_map/dot_general | solution.py:20
  106.2 10.1 %collective-permute-done.4 = bf16[64,896]{1,0:T(8,128)(2,1)S(1)} collective-permute-done((bf16[64,896]{1,0:T(8,128)(2,1)S(1)}, bf16[64,896]{1,0:T(8,128)(2,1)S(1)}, u32[]{:S(2)}, u32[]{:S(2)}) %collective-permute-start.4) | collective-permute-done | bytes 114720 | tf_op jit(solution)/shard_map/ppermute | solution.py:58
  116.3 14.5 %collective-permute-done.3 = bf16[64,896]{1,0:T(8,128)(2,1)S(1)} collective-permute-done((bf16[64,896]{1,0:T(8,128)(2,1)S(1)}, bf16[64,896]{1,0:T(8,128)(2,1)S(1)}, u32[]{:S(2)}, u32[]{:S(2)}) %collective-permute-start.3) | collective-permute-done | bytes 114720 | tf_op jit(solution)/shard_map/ppermute | solution.py:58
  130.8 5.6 %collective-permute-done.2 = bf16[64,896]{1,0:T(8,128)(2,1)S(1)} collective-permute-done((bf16[64,896]{1,0:T(8,128)(2,1)S(1)}, bf16[64,896]{1,0:T(8,128)(2,1)S(1)}, u32[]{:S(2)}, u32[]{:S(2)}) %collective-permute-start.2) | collective-permute-done | bytes 114720 | tf_op jit(solution)/shard_map/ppermute | solution.py:58
  136.3 2.9 %collective-permute-done.1 = bf16[64,896]{1,0:T(8,128)(2,1)S(1)} collective-permute-done((bf16[64,896]{1,0:T(8,128)(2,1)S(1)}, bf16[64,896]{1,0:T(8,128)(2,1)S(1)}, u32[]{:S(2)}, u32[]{:S(2)}) %collective-permute-start.1) | collective-permute-done | bytes 114720 | tf_op jit(solution)/shard_map/ppermute | solution.py:58
  139.2 0.1 maximum_select_fusion
  139.4 0.2 fusion.4
  139.6 1.9 %fusion = bf16[256,3584]{1,0:T(8,128)(2,1)} fusion(bf16[64,256]{1,0:T(8,128)(2,1)S(1)} %convolution_convert_fusion.1, bf16[64,3584]{1,0:T(8,128)(2,1)S(1)} %bitcast.68, bf16[256,3584]{1,0:T(8,128)(2,1)S(1)} %copy-done.2), kind=kOutput, calls=%fused_computation.1 | convolution fusion | flops 120193024 | bytes 4161536 | tf_op jit(solution)/shard_map/dot_general | solution.py:20
  (23 shorter events, 0.4 us)
Async XLA Ops:
  0.6 0.9 copy-start
  0.6 42.9 %copy-start.1 = (bf16[1024,896]{1,0:T(8,128)(2,1)S(1)}, bf16[1024,896]{1,0:T(8,128)(2,1)}, u32[]{:S(2)}) copy-start(bf16[1024,896]{1,0:T(8,128)(2,1)} %param.4) | copy-start | bytes 5505028
  49.2 12.5 %all-to-all-start.2 = ((f32[8,8,1408]{2,1,0:T(8,128)}), f32[8,8,1408]{2,1,0:T(8,128)S(1)}, u32[]{:S(2)}, u32[]{:S(2)}) async-start(f32[8,8,1408]{2,1,0:T(8,128)} %pad_maximum_fusion), calls=%async_computation.2 | async-start | bytes 720896 | tf_op jit(solution)/shard_map/all_to_all | solution.py:47
  53.4 25.3 %collective-permute-start = (f32[64,256]{1,0:T(8,128)S(1)}, f32[64,256]{1,0:T(8,128)S(1)}, u32[]{:S(2)}, u32[]{:S(2)}) collective-permute-start(f32[64,256]{1,0:T(8,128)S(1)} %constant_dynamic-slice_fusion), channel_id=1, source_target_pairs={{0,0},{1,1},{2,2},{3,3},{4,32},{5,33},{6,34},{7,35},{8,64},{9,65},... | collective-permute-start | bytes 196616 | tf_op jit(solution)/shard_map/ppermute | solution.py:40
  75.3 9.3 %all-to-all-start.3 = ((f32[8,8,896]{2,1,0:T(8,128)}), f32[8,8,896]{2,1,0:T(8,128)S(1)}, u32[]{:S(2)}, u32[]{:S(2)}) async-start(f32[8,8,896]{2,1,0:T(8,128)} %broadcast_in_dim.24), calls=%async_computation.3 | async-start | bytes 458752 | tf_op jit(solution)/shard_map/all_to_all | solution.py:50
  85.6 30.7 %collective-permute-start.4 = (bf16[64,896]{1,0:T(8,128)(2,1)S(1)}, bf16[64,896]{1,0:T(8,128)(2,1)S(1)}, u32[]{:S(2)}, u32[]{:S(2)}) collective-permute-start(bf16[64,896]{1,0:T(8,128)(2,1)S(1)} %get-tuple-element.5), channel_id=1, source_target_pairs={{0,3},{1,2},{2,1},{3,0},{4,35},{5,34},{6,33},{7,32},{8,67},{9,66},... | collective-permute-start | bytes 344072 | tf_op jit(solution)/shard_map/ppermute | solution.py:58
  92.2 38.5 %collective-permute-start.3 = (bf16[64,896]{1,0:T(8,128)(2,1)S(1)}, bf16[64,896]{1,0:T(8,128)(2,1)S(1)}, u32[]{:S(2)}, u32[]{:S(2)}) collective-permute-start(bf16[64,896]{1,0:T(8,128)(2,1)S(1)} %get-tuple-element.5), channel_id=1, source_target_pairs={{0,2},{1,3},{2,0},{3,1},{4,34},{5,35},{6,32},{7,33},{8,66},{9,67},... | collective-permute-start | bytes 344072 | tf_op jit(solution)/shard_map/ppermute | solution.py:58
  99.7 36.6 %collective-permute-start.2 = (bf16[64,896]{1,0:T(8,128)(2,1)S(1)}, bf16[64,896]{1,0:T(8,128)(2,1)S(1)}, u32[]{:S(2)}, u32[]{:S(2)}) collective-permute-start(bf16[64,896]{1,0:T(8,128)(2,1)S(1)} %get-tuple-element.5), channel_id=1, source_target_pairs={{0,1},{1,0},{2,3},{3,2},{4,33},{5,32},{6,35},{7,34},{8,65},{9,64},... | collective-permute-start | bytes 344072 | tf_op jit(solution)/shard_map/ppermute | solution.py:58
  99.8 39.4 %collective-permute-start.1 = (bf16[64,896]{1,0:T(8,128)(2,1)S(1)}, bf16[64,896]{1,0:T(8,128)(2,1)S(1)}, u32[]{:S(2)}, u32[]{:S(2)}) collective-permute-start(bf16[64,896]{1,0:T(8,128)(2,1)S(1)} %get-tuple-element.5), channel_id=1, source_target_pairs={{0,0},{1,1},{2,2},{3,3},{4,32},{5,33},{6,34},{7,35},{8,64},{9,65},... | collective-permute-start | bytes 344072 | tf_op jit(solution)/shard_map/ppermute | solution.py:58
  106.2 33.4 %copy-start.2 = (bf16[256,3584]{1,0:T(8,128)(2,1)S(1)}, bf16[256,3584]{1,0:T(8,128)(2,1)}, u32[]{:S(2)}) copy-start(bf16[256,3584]{1,0:T(8,128)(2,1)} %param.7) | copy-start | bytes 5505028

commit v2 on v1

v2 whole, which is shorter than its diff:
```python
import jax
import jax.numpy as jnp
from jax import lax
from jax.sharding import PartitionSpec as P

HIGH = lax.Precision.HIGH
HIGHEST = lax.Precision.HIGHEST
ROWS, COLS, R = 8, 32, 64
AXES = ("row", "col")
SWAP = [(r * COLS + c, (c // 4) * COLS + 4 * r + c % 4) for r in range(ROWS) for c in range(COLS)]
SAME_CORE = [[c for c in range(COLS) if c % 2 == core] for core in range(2)]
PAIR = [(c, c ^ 1) for c in range(COLS)]


def dot(a, b, ca, cb, precision=None):
    return lax.dot_general(
        a, b, (((ca,), (cb,)), ((), ())), precision=precision, preferred_element_type=jnp.float32
    )


def exchange(parts, axis, groups=None):
    return lax.all_to_all(parts, axis, 0, 0, axis_index_groups=groups)


def share(mine, n, axis, groups=None):
    return exchange(jnp.broadcast_to(mine[None], (n,) + mine.shape), axis, groups)


def local(weight_change, error_buffer, basis, rollout_weight):
    q = lax.axis_index("col") % 4
    core = q % 2
    total = weight_change.astype(jnp.float32) + error_buffer
    rows, units = total.shape
    part = dot(basis, total, 0, 1, HIGH)
    part = part.reshape(8, 8, 4, rows // 4).transpose(0, 2, 1, 3).reshape(COLS, 8, rows // 4)
    left = share(jnp.sum(exchange(part, "col"), axis=0), COLS, "col")
    left = left.reshape(8, 4, 8, rows // 4).transpose(0, 2, 1, 3).reshape(R, rows)
    mine = lax.dynamic_slice_in_dim(left, q * (rows // 4), rows // 4, 1)
    my_left = lax.ppermute(mine, AXES, SWAP)
    gram_part = dot(left, left, 1, 1, HIGHEST)
    right_part = dot(left, total, 1, 0, HIGH)
    blocks = jnp.pad(right_part, ((0, 0), (0, 128 * ROWS - units))).reshape(R, ROWS, 128).transpose(1, 0, 2)
    gram_part = jnp.concatenate([gram_part[: R // 2], gram_part[R // 2 :]], 1)
    sent = jnp.concatenate([blocks, jnp.broadcast_to(gram_part[None], (ROWS, R // 2, 128))], 1)
    got = jnp.sum(exchange(sent, "row"), axis=0)
    gram = jnp.concatenate([got[R:, :R], got[R:, R:]], 0)
    my_block = got[:R]
    far_block = lax.ppermute(my_block, AXES, SWAP)
    lower = jnp.linalg.cholesky(gram)
    inverse = lax.linalg.triangular_solve(
        lower, jnp.eye(R, dtype=jnp.float32), left_side=True, lower=True
    )
    new_blocks = share(dot(inverse, my_block, 1, 0, HIGHEST), ROWS, "row")
    far_round = dot(inverse, far_block, 1, 0, HIGHEST).astype(jnp.bfloat16)
    near = share(far_round, COLS // 2, "col", SAME_CORE)
    other = lax.ppermute(near, "col", PAIR)
    new_basis = new_blocks.transpose(1, 0, 2).reshape(R, 128 * ROWS)[:, :units]
    left_round = dot(inverse, left, 1, 0, HIGHEST).astype(jnp.bfloat16)
    new_error = total - dot(left_round, new_basis.astype(jnp.bfloat16), 0, 0)
    my_left_round = dot(inverse, my_left, 1, 0, HIGHEST).astype(jnp.bfloat16)
    right = jnp.where(core == 0, jnp.stack([near, other]), jnp.stack([other, near]))
    right = right.reshape(2, 8, 2, R, 128)[:, : units // 128]
    right = right.transpose(3, 2, 0, 1, 4).reshape(R, 4 * units)
    rollout_delta = dot(my_left_round, right, 0, 0)
    new_rollout = (rollout_weight.astype(jnp.float32) + rollout_delta).astype(jnp.bfloat16)
    return (new_error, new_basis.T, new_rollout)


def solution(mesh):
    in_specs = (P("row", "col"), P("row", "col"), P("col", None), P("col", "row"))
    out_specs = (P("row", "col"), P("col", None), P("col", "row"))
    return jax.shard_map(local, mesh=mesh, in_specs=in_specs, out_specs=out_specs, check_vma=False)
```

time: 142 us -> 126 us (0.89)
  the two profiles are of different devices: /device:TPU:225 before, /device:TPU:1 now
where the time goes in v2:
time: 126 us; the launch traced here: 125 us
  blocking collectives  42.2 us (33%)
  starting transfers between devices  24.6 us (20%)
  waiting for transfers between devices  24 us (19%)
  matrix products  15.7 us (12%)
  other arithmetic  13.2 us (10%)
  local copies, waits for them, and re-layouts  4.91 us (4%)
    all_to_all x2, blocking collectives, exchange(): return lax.all_to_all(parts, axis, 0, 0, axis_index_groups=groups)  42.2 us
    all_to_all x3, waiting for transfers between devices, exchange(): return lax.all_to_all(parts, axis, 0, 0, axis_index_groups=groups)  24 us
    all_to_all x3, starting transfers between devices, exchange(): return lax.all_to_all(parts, axis, 0, 0, axis_index_groups=groups)  18 us
    dot_general x9, matrix products, dot(): lax.dot_general(a, b, (((ca,), (cb,)), ((), ())), precision=precision, pr...  15.4 us
    another operation x3, other arithmetic, local(): lower = jnp.linalg.cholesky(gram)  6.53 us
    another operation x2, other arithmetic, local(): lax.linalg.triangular_solve(lower, jnp.eye(R, dtype=jnp.float32), left_si...  5.55 us
    ppermute x1, starting transfers between devices, local(): other = lax.ppermute(near, 'col', PAIR)  5.28 us
  transfers between devices with their start and end apart: 6, of which 3 were waited for; matrix products, arithmetic and copies ran while one was open for 6% of the time, Pallas kernels for 0%

profile of v2, /device:TPU:1, one launch (start us, length us, event | category | flops | bytes accessed | tf_op | source)
XLA Modules:
  0.0 125.4 jit_solution(10510090769670533790)
XLA Ops:
  0.7 0.9 copy-done
  1.6 4.5 %fusion.2 = f32[1024,64]{0,1:T(8,128)S(1)} fusion(f32[896,64]{0,1:T(8,128)S(1)} %copy-done, f32[1024,896]{1,0:T(8,128)} %param.5, bf16[1024,896]{1,0:T(8,128)(2,1)} %param.4), kind=kOutput, calls=%fused_computation.5 | convolution fusion | flops 354156544 | bytes 5996544 | tf_op jit(solution)/shard_map/dot_general | solution.py:16
  6.1 25.3 %all_to_all.25 = f32[32,8,256]{2,1,0:T(8,128)S(1)} all-to-all(f32[32,8,256]{2,1,0:T(8,128)S(1)} %bitcast.59), channel_id=1, replica_groups=mesh['row'=8,'col'=32] {'col'}, dimensions={0} | all-to-all | bytes 524288 | tf_op jit(solution)/shard_map/all_to_all | solution.py:22
  31.4 16.9 %all_to_all.26 = f32[32,8,256]{2,1,0:T(8,128)S(1)} all-to-all(f32[32,8,256]{2,1,0:T(8,128)S(1)} %broadcast_in_dim.10), channel_id=1, replica_groups=mesh['row'=8,'col'=32] {'col'}, dimensions={0} | all-to-all | bytes 524288 | tf_op jit(solution)/shard_map/all_to_all | solution.py:22
  48.3 0.4 fusion.13
  48.7 3.3 %fusion.1 = f32[64,896]{1,0:T(8,128)S(1)} fusion(f32[64,1024]{1,0:T(8,128)S(1)} %bitcast.55, f32[1024,896]{1,0:T(8,128)} %param.5, bf16[1024,896]{1,0:T(8,128)(2,1)S(1)} %copy-done.1), kind=kOutput, calls=%fused_computation.4 | convolution fusion | flops 354156544 | bytes 5996544 | tf_op jit(solution)/shard_map/dot_general | solution.py:16
  52.1 0.8 pad_maximum_fusion.2
  52.9 4.2 %all-to-all-start.2 = ((f32[8,96,128]{2,1,0:T(8,128)}), f32[8,96,128]{2,1,0:T(8,128)S(1)}, u32[]{:S(2)}, u32[]{:S(2)}) async-start(f32[8,96,128]{2,1,0:T(8,128)} %pad_maximum_fusion.2), calls=%async_computation.2 | async-start | bytes 786432 | tf_op jit(solution)/shard_map/all_to_all | solution.py:22
  57.1 8.1 %all-to-all-done.2 = f32[8,96,128]{2,1,0:T(8,128)S(1)} async-done(((f32[8,96,128]{2,1,0:T(8,128)}), f32[8,96,128]{2,1,0:T(8,128)S(1)}, u32[]{:S(2)}, u32[]{:S(2)}) %all-to-all-start.2) | async-done | bytes 393248 | tf_op jit(solution)/shard_map/all_to_all | solution.py:22
  65.7 5.9 %cholesky.17 = f32[64,64]{1,0:T(8,128)S(1)} custom-call(f32[64,64]{1,0:T(8,128)S(1)} %fusion.8), custom_call_target="Cholesky" | custom-call | tf_op jit(solution)/shard_map/jit(cholesky)/cholesky | solution.py:49
  71.6 0.6 compare_reduce_fusion
  72.2 0.7 fusion.5
  72.9 4.9 %custom-call.6 = f32[1,64,64]{1,2,0:T(8,128)S(1)} custom-call(f32[1,64,64]{2,1,0:T(8,128)S(1)} %fusion.5), custom_call_target="InvertDiagBlocksLowerTriangular" | custom-call | tf_op jit(solution)/shard_map/triangular_solve | solution.py:50
  77.8 0.2 fusion.6
  78.0 0.7 collective-permute-start.1
  78.9 0.7 broadcast_in_dim.12
  79.6 7.8 %all-to-all-start.3 = ((f32[8,64,128]{2,1,0:T(8,128)}), f32[8,64,128]{2,1,0:T(8,128)S(1)}, u32[]{:S(2)}, u32[]{:S(2)}) async-start(f32[8,64,128]{2,1,0:T(8,128)} %broadcast_in_dim.12), calls=%async_computation.3 | async-start | bytes 524288 | tf_op jit(solution)/shard_map/all_to_all | solution.py:22
  87.4 0.7 collective-permute-start
  88.1 0.2 convolution_convert_fusion.2
  88.2 5.3 %all-to-all-done.3 = f32[8,64,128]{2,1,0:T(8,128)S(1)} async-done(((f32[8,64,128]{2,1,0:T(8,128)}), f32[8,64,128]{2,1,0:T(8,128)S(1)}, u32[]{:S(2)}, u32[]{:S(2)}) %all-to-all-start.3) | async-done | bytes 262176 | tf_op jit(solution)/shard_map/all_to_all | solution.py:22
  93.5 0.8 broadcast_in_dim.13
  94.3 6.0 %all-to-all-start.4 = ((bf16[16,64,128]{2,1,0:T(8,128)(2,1)}), bf16[16,64,128]{2,1,0:T(8,128)(2,1)S(1)}, u32[]{:S(2)}, u32[]{:S(2)}) async-start(bf16[16,64,128]{2,1,0:T(8,128)(2,1)} %broadcast_in_dim.13), calls=%async_computation.4 | async-start | bytes 524288 | tf_op jit(solution)/shard_map/all_to_all | solution.py:22
  100.3 0.2 convolution_convert_fusion.1
  100.5 0.4 convolution_convert_fusion
  100.9 10.6 %all-to-all-done.4 = bf16[16,64,128]{2,1,0:T(8,128)(2,1)S(1)} async-done(((bf16[16,64,128]{2,1,0:T(8,128)(2,1)}), bf16[16,64,128]{2,1,0:T(8,128)(2,1)S(1)}, u32[]{:S(2)}, u32[]{:S(2)}) %all-to-all-start.4) | async-done | bytes 262176 | tf_op jit(solution)/shard_map/all_to_all | solution.py:22
  111.5 5.3 %collective-permute-start.2 = (bf16[16,64,128]{2,1,0:T(8,128)(2,1)S(1)}, bf16[16,64,128]{2,1,0:T(8,128)(2,1)S(1)}, u32[]{:S(2)}, u32[]{:S(2)}) collective-permute-start(bf16[16,64,128]{2,1,0:T(8,128)(2,1)S(1)} %all-to-all-done.4), channel_id=1, source_target_pairs={{0,1},{1,0},{2,3},{3,2},{4,5},{5,4},{6,7},{7,6},{8,9},{9,8},{10,11... | collective-permute-start | bytes 786440 | tf_op jit(solution)/shard_map/ppermute | solution.py:56
  116.8 4.5 %convolution_subtract_fusion = f32[1024,896]{1,0:T(8,128)} fusion(bf16[64,1024]{1,0:T(8,128)(2,1)S(1)} %convolution_convert_fusion, f32[1024,896]{1,0:T(8,128)} %param.5, bf16[1024,896]{1,0:T(8,128)(2,1)S(1)} %copy-done.1, f32[64,1024]{1,0:T(8,128)S(1)} %copy_bitcast_fusion), kind=kOutput, calls=%fused_computation.3 | convolution fusion | flops 120193024 | bytes 9420800 | tf_op jit(solution)/shard_map/dot_general | solution.py:16
  121.3 0.7 slice_bitcast_fusion
  122.1 0.3 copy.23
  122.4 0.5 reshape.55
  122.9 0.6 copy-done.2
  123.5 1.9 %fusion = bf16[256,3584]{1,0:T(8,128)(2,1)} fusion(bf16[64,256]{1,0:T(8,128)(2,1)S(1)} %convolution_convert_fusion.1, bf16[64,3584]{1,0:T(8,128)(2,1)S(1)} %reshape.55, bf16[256,3584]{1,0:T(8,128)(2,1)S(1)} %copy-done.2), kind=kOutput, calls=%fused_computation.1 | convolution fusion | flops 120193024 | bytes 4161536 | tf_op jit(solution)/shard_map/dot_general | solution.py:16
  (26 shorter events, 1.0 us)
Async XLA Ops:
  0.6 0.9 copy-start
  0.6 48.0 %copy-start.1 = (bf16[1024,896]{1,0:T(8,128)(2,1)S(1)}, bf16[1024,896]{1,0:T(8,128)(2,1)}, u32[]{:S(2)}) copy-start(bf16[1024,896]{1,0:T(8,128)(2,1)} %param.4) | copy-start | bytes 5505028
  52.9 12.3 %all-to-all-start.2 = ((f32[8,96,128]{2,1,0:T(8,128)}), f32[8,96,128]{2,1,0:T(8,128)S(1)}, u32[]{:S(2)}, u32[]{:S(2)}) async-start(f32[8,96,128]{2,1,0:T(8,128)} %pad_maximum_fusion.2), calls=%async_computation.2 | async-start | bytes 786432 | tf_op jit(solution)/shard_map/all_to_all | solution.py:22
  78.0 10.0 %collective-permute-start.1 = (f32[64,128]{1,0:T(8,128)S(1)}, f32[64,128]{1,0:T(8,128)S(1)}, u32[]{:S(2)}, u32[]{:S(2)}) collective-permute-start(f32[64,128]{1,0:T(8,128)S(1)} %slice.42), channel_id=1, source_target_pairs={{0,0},{1,1},{2,2},{3,3},{4,32},{5,33},{6,34},{7,35},{8,64},{9,65},... | collective-permute-start | bytes 98312 | tf_op jit(solution)/shard_map/ppermute | solution.py:48
  79.6 13.9 %all-to-all-start.3 = ((f32[8,64,128]{2,1,0:T(8,128)}), f32[8,64,128]{2,1,0:T(8,128)S(1)}, u32[]{:S(2)}, u32[]{:S(2)}) async-start(f32[8,64,128]{2,1,0:T(8,128)} %broadcast_in_dim.12), calls=%async_computation.3 | async-start | bytes 524288 | tf_op jit(solution)/shard_map/all_to_all | solution.py:22
  87.4 12.9 %collective-permute-start = (f32[64,256]{1,0:T(8,128)S(1)}, f32[64,256]{1,0:T(8,128)S(1)}, u32[]{:S(2)}, u32[]{:S(2)}) collective-permute-start(f32[64,256]{1,0:T(8,128)S(1)} %constant_dynamic-slice_fusion), channel_id=1, source_target_pairs={{0,0},{1,1},{2,2},{3,3},{4,32},{5,33},{6,34},{7,35},{8,64},{9,65},... | collective-permute-start | bytes 196616 | tf_op jit(solution)/shard_map/ppermute | solution.py:39
  94.3 17.2 %all-to-all-start.4 = ((bf16[16,64,128]{2,1,0:T(8,128)(2,1)}), bf16[16,64,128]{2,1,0:T(8,128)(2,1)S(1)}, u32[]{:S(2)}, u32[]{:S(2)}) async-start(bf16[16,64,128]{2,1,0:T(8,128)(2,1)} %broadcast_in_dim.13), calls=%async_computation.4 | async-start | bytes 524288 | tf_op jit(solution)/shard_map/all_to_all | solution.py:22
  111.5 10.5 %collective-permute-start.2 = (bf16[16,64,128]{2,1,0:T(8,128)(2,1)S(1)}, bf16[16,64,128]{2,1,0:T(8,128)(2,1)S(1)}, u32[]{:S(2)}, u32[]{:S(2)}) collective-permute-start(bf16[16,64,128]{2,1,0:T(8,128)(2,1)S(1)} %all-to-all-done.4), channel_id=1, source_target_pairs={{0,1},{1,0},{2,3},{3,2},{4,5},{5,4},{6,7},{7,6},{8,9},{9,8},{10,11... | collective-permute-start | bytes 786440 | tf_op jit(solution)/shard_map/ppermute | solution.py:56
  122.0 1.5 %copy-start.2 = (bf16[256,3584]{1,0:T(8,128)(2,1)S(1)}, bf16[256,3584]{1,0:T(8,128)(2,1)}, u32[]{:S(2)}) copy-start(bf16[256,3584]{1,0:T(8,128)(2,1)} %param.7) | copy-start | bytes 5505028

commit v3 on v2

v3 whole, which is shorter than its diff:
```python
import jax
import jax.numpy as jnp
from jax import lax
from jax.experimental import pallas as pl
from jax.experimental.pallas import tpu as pltpu
from jax.sharding import PartitionSpec as P

HIGH = lax.Precision.HIGH
HIGHEST = lax.Precision.HIGHEST
ROWS, COLS, R, LANES, BLOCKS = 8, 32, 64, 128, 8
AXES = ("row", "col")
SWAP = [(r * COLS + c, (c // 4) * COLS + 4 * r + c % 4) for r in range(ROWS) for c in range(COLS)]
SAME_CORE = [[c for c in range(COLS) if c % 2 == core] for core in range(2)]
PAIR = [(c, c ^ 1) for c in range(COLS)]


def dot(a, b, ca, cb, precision=None):
    return lax.dot_general(
        a, b, (((ca,), (cb,)), ((), ())), precision=precision, preferred_element_type=jnp.float32
    )


def exchange(parts, axis, groups=None):
    return lax.all_to_all(parts, axis, 0, 0, axis_index_groups=groups)


def share(mine, n, axis, groups=None):
    return exchange(jnp.broadcast_to(mine[None], (n,) + mine.shape), axis, groups)


def inverse_factor(gram):
    n = R // 8
    lane = lax.broadcasted_iota(jnp.int32, (8, R), 1)
    sub = lax.broadcasted_iota(jnp.int32, (8, R), 0)
    wide = [
        jnp.concatenate([gram[8 * i : 8 * i + 8], (lane == sub + 8 * i).astype(jnp.float32)], 1)
        for i in range(n)
    ]
    row = lax.broadcasted_iota(jnp.int32, (8, LANES), 0)
    out = []

    def pick(x, k):
        return jnp.broadcast_to(x[k : k + 1], (8, LANES))

    for p in range(n):
        column = [
            [jnp.broadcast_to(wide[i][:, 8 * p + k : 8 * p + k + 1], (8, LANES)) for i in range(p, n)]
            for k in range(8)
        ]
        scale = jnp.zeros((8, LANES), jnp.float32)
        for k in range(8):
            pivot = pick(column[k][0], k)
            times = 1.0 / pivot
            scale = jnp.where(row == k, lax.rsqrt(pivot), scale)
            by = [c * times for c in column[k]]
            by[0] = jnp.where(row > k, by[0], 0.0)
            for l in range(k + 1, 8):
                value = pick(column[l][0], k)
                column[l] = [c - b * value for c, b in zip(column[l], by)]
            value = pick(wide[p], k)
            for i in range(p, n):
                wide[i] = wide[i] - by[i - p] * value
        out.append(wide[p][:, R:] * scale[:, R:])
    return jnp.concatenate(out, 0)


def factor_kernel(got_ref, inverse_ref, blocks_ref):
    packed = got_ref[R:]
    gram = jnp.concatenate([packed[:, :R], packed[:, R:]], 0)
    inverse = inverse_factor(gram)
    inverse_ref[...] = inverse
    block = dot(inverse, got_ref[:R], 1, 0, HIGHEST)
    for b in range(BLOCKS):
        blocks_ref[b] = block


def factor(got):
    return pl.pallas_call(
        factor_kernel,
        out_shape=[
            jax.ShapeDtypeStruct((R, R), jnp.float32),
            jax.ShapeDtypeStruct((BLOCKS, R, LANES), jnp.float32),
        ],
        cost_estimate=pl.CostEstimate(flops=10**7, bytes_accessed=20 * 10**6, transcendentals=0),
        name="factor",
    )(got)


def far_kernel(inverse_ref, block_ref, out_ref):
    block = dot(inverse_ref[...], block_ref[...], 1, 0, HIGHEST).astype(jnp.bfloat16)
    for b in range(out_ref.shape[0]):
        out_ref[b] = block


def far_blocks(inverse, block):
    return pl.pallas_call(
        far_kernel,
        out_shape=jax.ShapeDtypeStruct((COLS // 2, R, LANES), jnp.bfloat16),
        name="far_blocks",
    )(inverse, block)


def rollout_kernel(core_ref, inverse_ref, left_ref, near_ref, other_ref, weight_ref, out_ref, round_ref):
    i = pl.program_id(0)

    @pl.when(i == 0)
    def _():
        ortho = dot(left_ref[...], inverse_ref[...], 0, 1, HIGHEST)
        round_ref[...] = ortho.astype(jnp.bfloat16)

    def write(right_ref):
        half = i // 2
        for b in range(out_ref.shape[1] // LANES):
            lanes = pl.ds(b * LANES, LANES)
            delta = dot(round_ref[...], right_ref[b, half], 1, 0)
            out_ref[:, lanes] = (weight_ref[:, lanes].astype(jnp.float32) + delta).astype(jnp.bfloat16)

    @pl.when(i % 2 == core_ref[0])
    def _():
        write(near_ref)

    @pl.when(i % 2 != core_ref[0])
    def _():
        write(other_ref)


def rollout(core, inverse, left, near, other, weight):
    rows, units = weight.shape
    right = pl.BlockSpec((BLOCKS, 2, R, LANES), lambda i, core: (0, 0, 0, 0))
    block = pl.BlockSpec((rows, units // 4), lambda i, core: (0, i))
    return pl.pallas_call(
        rollout_kernel,
        grid_spec=pltpu.PrefetchScalarGridSpec(
            num_scalar_prefetch=1,
            grid=(4,),
            in_specs=[
                pl.BlockSpec((R, R), lambda i, core: (0, 0)),
                pl.BlockSpec((R, rows), lambda i, core: (0, 0)),
                right,
                right,
                block,
            ],
            out_specs=block,
            scratch_shapes=[pltpu.VMEM((rows, R), jnp.bfloat16)],
        ),
        out_shape=jax.ShapeDtypeStruct((rows, units), jnp.bfloat16),
        name="rollout",
    )(core, inverse, left, near, other, weight)


def local(weight_change, error_buffer, basis, rollout_weight):
    q = lax.axis_index("col") % 4
    core = q % 2
    total = weight_change.astype(jnp.float32) + error_buffer
    rows, units = total.shape
    part = dot(basis, total, 0, 1, HIGH)
    part = part.reshape(8, 8, 4, rows // 4).transpose(0, 2, 1, 3).reshape(COLS, 8, rows // 4)
    left = share(jnp.sum(exchange(part, "col"), axis=0), COLS, "col")
    left = left.reshape(8, 4, 8, rows // 4).transpose(0, 2, 1, 3).reshape(R, rows)
    mine = lax.dynamic_slice_in_dim(left, q * (rows // 4), rows // 4, 1)
    my_left = lax.ppermute(mine, AXES, SWAP)
    gram_part = dot(left, left, 1, 1, HIGHEST)
    right_part = dot(left, total, 1, 0, HIGH)
    blocks = jnp.pad(right_part, ((0, 0), (0, LANES * BLOCKS - units)))
    blocks = blocks.reshape(R, BLOCKS, LANES).transpose(1, 0, 2)
    gram_part = jnp.concatenate([gram_part[: R // 2], gram_part[R // 2 :]], 1)
    sent = jnp.concatenate([blocks, jnp.broadcast_to(gram_part[None], (BLOCKS, R // 2, LANES))], 1)
    got = jnp.sum(exchange(sent, "row"), axis=0)
    got, my_left = lax.optimization_barrier((got, my_left))
    far_block = lax.ppermute(got[:R], AXES, SWAP)
    inverse, new_blocks = factor(got)
    far = far_blocks(inverse, far_block)
    new_blocks, far = lax.optimization_barrier((new_blocks, far))
    near = exchange(far, "col", SAME_CORE)
    other = lax.ppermute(near, "col", PAIR)
    new_basis = exchange(new_blocks, "row").transpose(1, 0, 2).reshape(R, LANES * BLOCKS)[:, :units]
    left_round = dot(inverse, left, 1, 0, HIGHEST).astype(jnp.bfloat16)
    new_error = total - dot(left_round, new_basis.astype(jnp.bfloat16), 0, 0)
    halves = (BLOCKS, 2, R, LANES)
    new_rollout = rollout(
        core.astype(jnp.int32).reshape(1), inverse, my_left, near.reshape(halves), other.reshape(halves), rollout_weight
    )
    return (new_error, new_basis.T, new_rollout)


def solution(mesh):
    in_specs = (P("row", "col"), P("row", "col"), P("col", None), P("col", "row"))
    out_specs = (P("row", "col"), P("col", None), P("col", "row"))
    return jax.shard_map(local, mesh=mesh, in_specs=in_specs, out_specs=out_specs, check_vma=False)
```

time: 126 us -> 126 us (level)
  blocking collectives: 42.2 us -> 64.1 us
  other arithmetic: 13.2 us -> 0.91 us
  Pallas kernels: 0 us -> 9.89 us
  starting transfers between devices: 24.6 us -> 15.6 us
  waiting for transfers between devices: 24 us -> 17.4 us
  matrix products: 15.7 us -> 13.8 us
  local copies, waits for them, and re-layouts: 4.91 us -> 3.05 us
    all_to_all x2 -> x3, blocking collectives: 42.2 us -> 64.1 us  [exchange(): return lax.all_to_all(parts, axis, 0, 0, axis_index_groups=groups)]
    another operation x5 -> x0, other arithmetic: 12.1 us -> none  [the longest x3 6.53 us: local(): lower = jnp.linalg.cholesky(gram)]
    pallas_call x0 -> x3, Pallas kernels: none -> 9.89 us  [the longest x1 4.66 us: rollout(): pl.pallas_call(rollout_kernel, grid_spec=pltpu.PrefetchScalarGridSpec(num...]
    all_to_all x3 -> x2, starting transfers between devices: 18 us -> 8.28 us  [exchange(): return lax.all_to_all(parts, axis, 0, 0, axis_index_groups=groups)]
    all_to_all x3 -> x2, waiting for transfers between devices: 24 us -> 17.3 us  [exchange(): return lax.all_to_all(parts, axis, 0, 0, axis_index_groups=groups)]
    dot_general x9 -> x5, matrix products: 15.4 us -> 13.8 us  [dot(): lax.dot_general(a, b, (((ca,), (cb,)), ((), ())), precision=precision, pr...]
    broadcast_in_dim x3 -> x1, local copies, waits for them, and re-layouts: 1.49 us -> 0.02 us  [share(): jnp.broadcast_to(mine[None], (n,) + mine.shape)]
  transfers between devices with their start and end apart: 6 -> 5, of which waited for: 3 -> 2; matrix products, arithmetic and copies ran while one was open for 6% -> 5% of each run, Pallas kernels for 0% -> 3%
where the time goes in v3:
time: 126 us; the launch traced here: 125 us
  blocking collectives  64.1 us (51%)
  waiting for transfers between devices  17.4 us (14%)
  starting transfers between devices  15.6 us (12%)
  matrix products  13.8 us (11%)
  Pallas kernels  9.89 us (8%)
  local copies, waits for them, and re-layouts  3.05 us (2%)
    all_to_all x3, blocking collectives, exchange(): return lax.all_to_all(parts, axis, 0, 0, axis_index_groups=groups)  64.1 us
    all_to_all x2, waiting for transfers between devices, exchange(): return lax.all_to_all(parts, axis, 0, 0, axis_index_groups=groups)  17.3 us
    dot_general x5, matrix products, dot(): lax.dot_general(a, b, (((ca,), (cb,)), ((), ())), precision=precision, pr...  13.8 us
    all_to_all x2, starting transfers between devices, exchange(): return lax.all_to_all(parts, axis, 0, 0, axis_index_groups=groups)  8.28 us
    ppermute x1, starting transfers between devices, local(): other = lax.ppermute(near, 'col', PAIR)  6.02 us
    pallas_call x1, Pallas kernels, rollout(): pl.pallas_call(rollout_kernel, grid_spec=pltpu.PrefetchScalarGridSpec(num...  4.66 us
    pallas_call x1, Pallas kernels, factor(): pl.pallas_call(factor_kernel, out_shape=[jax.ShapeDtypeStruct((R, R), jnp...  3.57 us
  transfers between devices with their start and end apart: 5, of which 2 were waited for; matrix products, arithmetic and copies ran while one was open for 5% of the time, Pallas kernels for 3%

profile of v3, /device:TPU:1, one launch (start us, length us, event | category | flops | bytes accessed | tf_op | source)
XLA Modules:
  0.0 125.5 jit_solution(12656697683040541645)
XLA Ops:
  0.6 0.0 copy-start
  0.6 0.0 copy-start.1
  0.7 0.9 copy-done
  1.6 4.5 %fusion.1 = f32[1024,64]{0,1:T(8,128)S(1)} fusion(f32[896,64]{0,1:T(8,128)S(1)} %copy-done, f32[1024,896]{1,0:T(8,128)} %param.5, bf16[1024,896]{1,0:T(8,128)(2,1)} %param.4), kind=kOutput, calls=%fused_computation.3 | convolution fusion | flops 354156544 | bytes 5996544 | tf_op jit(solution)/shard_map/dot_general | solution.py:18
  6.1 25.3 %all_to_all.25 = f32[32,8,256]{2,1,0:T(8,128)S(1)} all-to-all(f32[32,8,256]{2,1,0:T(8,128)S(1)} %bitcast.42), channel_id=1, replica_groups=mesh['row'=8,'col'=32] {'col'}, dimensions={0} | all-to-all | bytes 524288 | tf_op jit(solution)/shard_map/all_to_all | solution.py:24
  31.4 16.9 %all_to_all.26 = f32[32,8,256]{2,1,0:T(8,128)S(1)} all-to-all(f32[32,8,256]{2,1,0:T(8,128)S(1)} %broadcast_in_dim.4), channel_id=1, replica_groups=mesh['row'=8,'col'=32] {'col'}, dimensions={0} | all-to-all | bytes 524288 | tf_op jit(solution)/shard_map/all_to_all | solution.py:24
  48.3 0.4 fusion.3
  48.7 0.0 copy-done.1
  48.7 3.3 %fusion = f32[64,896]{1,0:T(8,128)S(1)} fusion(f32[64,1024]{1,0:T(8,128)S(1)} %bitcast.38, f32[1024,896]{1,0:T(8,128)} %param.5, bf16[1024,896]{1,0:T(8,128)(2,1)S(1)} %copy-done.1), kind=kOutput, calls=%fused_computation.2 | convolution fusion | flops 354156544 | bytes 5996544 | tf_op jit(solution)/shard_map/dot_general | solution.py:18
  52.0 0.1 pad_maximum_fusion.1
  52.1 0.8 pad_maximum_fusion
  52.9 4.2 %all-to-all-start.2 = ((f32[8,96,128]{2,1,0:T(8,128)}), f32[8,96,128]{2,1,0:T(8,128)S(1)}, u32[]{:S(2)}, u32[]{:S(2)}) async-start(f32[8,96,128]{2,1,0:T(8,128)} %pad_maximum_fusion), calls=%async_computation.2 | async-start | bytes 786432 | tf_op jit(solution)/shard_map/all_to_all | solution.py:24
  57.1 0.7 collective-permute-start
  57.8 7.4 %all-to-all-done.2 = f32[8,96,128]{2,1,0:T(8,128)S(1)} async-done(((f32[8,96,128]{2,1,0:T(8,128)}), f32[8,96,128]{2,1,0:T(8,128)S(1)}, u32[]{:S(2)}, u32[]{:S(2)}) %all-to-all-start.2) | async-done | bytes 393248 | tf_op jit(solution)/shard_map/all_to_all | solution.py:24
  65.2 0.0 copy-start.3
  65.2 0.0 collective-permute-done.left_ref
  65.3 0.7 collective-permute-start.1
  65.9 3.6 %factor.1 = (f32[64,64]{1,0:T(8,128)}, f32[8,64,128]{2,1,0:T(8,128)}) custom-call(f32[96,128]{1,0:T(8,128)} %copy-done.3), custom_call_target="tpu_custom_call" | custom-call | flops 10000000 | bytes 20000000 | tf_op jit(solution)/shard_map/factor/pallas_call | solution.py:78
  69.5 0.0 collective-permute-done.1.block_ref
  69.5 0.6 copy-done.6
  70.1 1.7 %far_blocks.1 = bf16[16,64,128]{2,1,0:T(8,128)(2,1)} custom-call(f32[64,64]{1,0:T(8,128)} %get-tuple-element.10.inverse_ref, f32[64,128]{1,0:T(8,128)} %copy-done.6), custom_call_target="tpu_custom_call" | custom-call | tf_op jit(solution)/shard_map/far_blocks/pallas_call | solution.py:96
  71.8 21.9 %all_to_all.27 = f32[8,64,128]{2,1,0:T(8,128)S(1)} all-to-all(f32[8,64,128]{2,1,0:T(8,128)} %get-tuple-element.12), channel_id=1, replica_groups=mesh['row'=8,'col'=32] {'row'}, dimensions={0} | all-to-all | bytes 524288 | tf_op jit(solution)/shard_map/all_to_all | solution.py:24
  93.7 4.1 %all-to-all-start.4 = ((bf16[16,64,128]{2,1,0:T(8,128)(2,1)}), bf16[16,64,128]{2,1,0:T(8,128)(2,1)S(1)}, u32[]{:S(2)}, u32[]{:S(2)}) async-start(bf16[16,64,128]{2,1,0:T(8,128)(2,1)} %far_blocks.1), calls=%async_computation.4 | async-start | bytes 524288 | tf_op jit(solution)/shard_map/all_to_all | solution.py:24
  97.8 1.1 convolution_convert_fusion
  98.9 9.9 %all-to-all-done.4 = bf16[16,64,128]{2,1,0:T(8,128)(2,1)S(1)} async-done(((bf16[16,64,128]{2,1,0:T(8,128)(2,1)}), bf16[16,64,128]{2,1,0:T(8,128)(2,1)S(1)}, u32[]{:S(2)}, u32[]{:S(2)}) %all-to-all-start.4) | async-done | bytes 262176 | tf_op jit(solution)/shard_map/all_to_all | solution.py:24
  108.8 6.0 %collective-permute-start.2 = (bf16[16,64,128]{2,1,0:T(8,128)(2,1)S(1)}, bf16[16,64,128]{2,1,0:T(8,128)(2,1)S(1)}, u32[]{:S(2)}, u32[]{:S(2)}) collective-permute-start(bf16[16,64,128]{2,1,0:T(8,128)(2,1)S(1)} %all-to-all-done.4), channel_id=1, source_target_pairs={{0,1},{1,0},{2,3},{3,2},{4,5},{5,4},{6,7},{7,6},{8,9},{9,8},{10,11... | collective-permute-start | bytes 786440 | tf_op jit(solution)/shard_map/ppermute | solution.py:175
  114.9 4.5 %convolution_subtract_fusion = f32[1024,896]{1,0:T(8,128)} fusion(bf16[64,1024]{1,0:T(8,128)(2,1)S(1)} %convolution_convert_fusion, f32[1024,896]{1,0:T(8,128)} %param.5, bf16[1024,896]{1,0:T(8,128)(2,1)S(1)} %copy-done.1, f32[64,1024]{1,0:T(8,128)S(1)} %copy_bitcast_fusion), kind=kOutput, calls=%fused_computation.1 | convolution fusion | flops 120193024 | bytes 9420800 | tf_op jit(solution)/shard_map/dot_general | solution.py:18
  119.4 0.0 copy-done.2
  119.4 0.7 slice_bitcast_fusion
  120.1 0.0 collective-permute-done.2
  120.1 0.7 copy-done.4
  120.8 4.7 %rollout.1 = bf16[256,3584]{1,0:T(8,128)(2,1)} custom-call(s32[1]{0:T(128)} %bitcast.12.core_ref, f32[64,64]{1,0:T(8,128)} %get-tuple-element.10.inverse_ref, f32[64,256]{1,0:T(8,128)} %copy-done.5, bf16[8,2,64,128]{3,2,1,0:T(8,128)(2,1)} %bitcast.41, bf16[8,2,64,128]{3,2,1,0:T(8,128)(2,1)} %bitcast.43, bf16[256,3584]{1,0:T(8,128)(2,1)} %weight_ref.1), custom_call_target="tpu_custom_call" | custom-call | tf_op jit(solution)/shard_map/rollout/pallas_call | solution.py:131
  (15 shorter events, 0.2 us)
Async XLA Ops:
  0.6 0.9 copy-start
  0.6 48.0 %copy-start.1 = (bf16[1024,896]{1,0:T(8,128)(2,1)S(1)}, bf16[1024,896]{1,0:T(8,128)(2,1)}, u32[]{:S(2)}) copy-start(bf16[1024,896]{1,0:T(8,128)(2,1)} %param.4) | copy-start | bytes 5505028
  52.9 12.3 %all-to-all-start.2 = ((f32[8,96,128]{2,1,0:T(8,128)}), f32[8,96,128]{2,1,0:T(8,128)S(1)}, u32[]{:S(2)}, u32[]{:S(2)}) async-start(f32[8,96,128]{2,1,0:T(8,128)} %pad_maximum_fusion), calls=%async_computation.2 | async-start | bytes 786432 | tf_op jit(solution)/shard_map/all_to_all | solution.py:24
  57.1 8.1 %collective-permute-start = (f32[64,256]{1,0:T(8,128)S(1)}, f32[64,256]{1,0:T(8,128)S(1)}, u32[]{:S(2)}, u32[]{:S(2)}) collective-permute-start(f32[64,256]{1,0:T(8,128)S(1)} %constant_dynamic-slice_fusion), channel_id=1, source_target_pairs={{0,0},{1,1},{2,2},{3,3},{4,32},{5,33},{6,34},{7,35},{8,64},{9,65},... | collective-permute-start | bytes 196616 | tf_op jit(solution)/shard_map/ppermute | solution.py:161
  65.2 0.7 copy-start.3
  65.2 54.2 %copy-start.5 = (f32[64,256]{1,0:T(8,128)}, f32[64,256]{1,0:T(8,128)S(1)}, u32[]{:S(2)}) copy-start(f32[64,256]{1,0:T(8,128)S(1)} %collective-permute-done.left_ref) | copy-start | bytes 196612
  65.3 4.3 %collective-permute-start.1 = (f32[64,128]{1,0:T(8,128)S(1)}, f32[64,128]{1,0:T(8,128)S(1)}, u32[]{:S(2)}, u32[]{:S(2)}) collective-permute-start(f32[64,128]{1,0:T(8,128)S(1)} %slice.14), channel_id=1, source_target_pairs={{0,0},{1,1},{2,2},{3,3},{4,32},{5,33},{6,34},{7,35},{8,64},{9,65},... | collective-permute-start | bytes 98312 | tf_op jit(solution)/shard_map/ppermute | solution.py:170
  69.5 0.6 copy-start.6
  93.7 15.2 %all-to-all-start.4 = ((bf16[16,64,128]{2,1,0:T(8,128)(2,1)}), bf16[16,64,128]{2,1,0:T(8,128)(2,1)S(1)}, u32[]{:S(2)}, u32[]{:S(2)}) async-start(bf16[16,64,128]{2,1,0:T(8,128)(2,1)} %far_blocks.1), calls=%async_computation.4 | async-start | bytes 524288 | tf_op jit(solution)/shard_map/all_to_all | solution.py:24
  108.8 10.6 %copy-start.2 = (bf16[16,64,128]{2,1,0:T(8,128)(2,1)}, bf16[16,64,128]{2,1,0:T(8,128)(2,1)S(1)}, u32[]{:S(2)}) copy-start(bf16[16,64,128]{2,1,0:T(8,128)(2,1)S(1)} %all-to-all-done.4) | copy-start | bytes 786436
  108.8 11.3 %collective-permute-start.2 = (bf16[16,64,128]{2,1,0:T(8,128)(2,1)S(1)}, bf16[16,64,128]{2,1,0:T(8,128)(2,1)S(1)}, u32[]{:S(2)}, u32[]{:S(2)}) collective-permute-start(bf16[16,64,128]{2,1,0:T(8,128)(2,1)S(1)} %all-to-all-done.4), channel_id=1, source_target_pairs={{0,1},{1,0},{2,3},{3,2},{4,5},{5,4},{6,7},{7,6},{8,9},{9,8},{10,11... | collective-permute-start | bytes 786440 | tf_op jit(solution)/shard_map/ppermute | solution.py:175
  120.1 0.7 copy-start.4

commit v4 on v3

v4 whole, which is shorter than its diff:
```python
import jax
import jax.numpy as jnp
from jax import lax
from jax.experimental import pallas as pl
from jax.experimental.pallas import tpu as pltpu
from jax.sharding import PartitionSpec as P

HIGH = lax.Precision.HIGH
HIGHEST = lax.Precision.HIGHEST
ROWS, COLS, R, LANES, BLOCKS = 8, 32, 64, 128, 8
AXES = ("row", "col")
SWAP = [(r * COLS + c, (c // 4) * COLS + 4 * r + c % 4) for r in range(ROWS) for c in range(COLS)]
SAME_CORE = [[c for c in range(COLS) if c % 2 == core] for core in range(2)]
PAIR = [(c, c ^ 1) for c in range(COLS)]


def dot(a, b, ca, cb, precision=None):
    return lax.dot_general(
        a, b, (((ca,), (cb,)), ((), ())), precision=precision, preferred_element_type=jnp.float32
    )


def split(x):
    hi = x.astype(jnp.bfloat16)
    return hi, (x - hi.astype(jnp.float32)).astype(jnp.bfloat16)


def exchange(parts, axis, groups=None):
    return lax.all_to_all(parts, axis, 0, 0, axis_index_groups=groups)


def share(mine, n, axis, groups=None):
    return exchange(jnp.broadcast_to(mine[None], (n,) + mine.shape), axis, groups)


ANY = pl.BlockSpec(memory_space=pl.ANY)
VMEM = pl.BlockSpec(memory_space=pltpu.VMEM)
SMEM = pl.BlockSpec(memory_space=pltpu.SMEM)


def grant(mib):
    return pltpu.CompilerParams(vmem_limit_bytes=mib * 2**20)


def left_kernel(change_ref, error_ref, basis_ref, out_ref, change_buf, error_buf, basis_buf, sem, basis_sem):
    rows, width = change_ref.shape[0], out_ref.shape[3]
    block = rows // 2
    basis_copy = pltpu.make_async_copy(basis_ref, basis_buf, basis_sem)
    basis_copy.start()
    copies = []
    for i in range(2):
        part = pl.ds(i * block, block)
        pair = [
            pltpu.make_async_copy(change_ref.at[part], change_buf.at[part], sem.at[0, i]),
            pltpu.make_async_copy(error_ref.at[part], error_buf.at[part], sem.at[1, i]),
        ]
        for copy in pair:
            copy.start()
        copies.append(pair)
    basis_copy.wait()
    basis_hi, basis_lo = split(basis_buf[...])
    basis_both = jnp.concatenate([basis_hi, basis_lo], 0)
    for i in range(2):
        for copy in copies[i]:
            copy.wait()
        part = pl.ds(i * block, block)
        hi, lo = split(change_buf[part].astype(jnp.float32) + error_buf[part])
        both = dot(basis_both, hi, 1, 1)
        left = both[:R] + both[R:] + dot(basis_hi, lo, 1, 1)
        for j in range(block // width):
            out_ref[:, i * (block // width) + j] = left[:, j * width : (j + 1) * width].reshape(8, 8, width)


def left_part(change, error, basis):
    rows, units = change.shape
    return pl.pallas_call(
        left_kernel,
        in_specs=[ANY, ANY, ANY],
        out_specs=VMEM,
        out_shape=jax.ShapeDtypeStruct((8, 4, 8, rows // 4), jnp.float32),
        scratch_shapes=[
            pltpu.VMEM((rows, units), jnp.bfloat16),
            pltpu.VMEM((rows, units), jnp.float32),
            pltpu.VMEM((R, units), jnp.float32),
            pltpu.SemaphoreType.DMA((2, 2)),
            pltpu.SemaphoreType.DMA,
        ],
        compiler_params=grant(62),
        cost_estimate=pl.CostEstimate(flops=6 * rows * units * R, bytes_accessed=6 * rows * units, transcendentals=0),
        name="left_part",
    )(change, error, basis)


def right_kernel(hi_ref, lo_ref, left_ref, out_ref):
    left = jnp.concatenate([left_ref[:, i].reshape(R, -1) for i in range(4)], 1)
    left_hi, left_lo = split(left)
    both = dot(jnp.concatenate([left_hi, left_lo], 0), hi_ref[...], 1, 0)
    right = both[:R] + both[R:] + dot(left_hi, lo_ref[...], 1, 0)
    used = right.shape[1] // LANES
    for b in range(used):
        out_ref[b, :R] = right[:, b * LANES : (b + 1) * LANES]
    for b in range(used, BLOCKS):
        out_ref[b, :R] = jnp.zeros((R, LANES), jnp.float32)
    gram = dot(left, left, 1, 1, HIGHEST)
    for b in range(BLOCKS):
        out_ref[b, R:, :R] = gram[: R // 2]
        out_ref[b, R:, R:] = gram[R // 2 :]


def right_part(hi, lo, left):
    rows, units = hi.shape
    return pl.pallas_call(
        right_kernel,
        in_specs=[VMEM, VMEM, VMEM],
        out_specs=VMEM,
        out_shape=jax.ShapeDtypeStruct((BLOCKS, R + R // 2, LANES), jnp.float32),
        compiler_params=grant(12),
        cost_estimate=pl.CostEstimate(flops=6 * rows * units * R, bytes_accessed=4 * rows * units, transcendentals=0),
        name="right_part",
    )(hi, lo, left)


def inverse_factor(gram):
    n = R // 8
    lane = lax.broadcasted_iota(jnp.int32, (8, R), 1)
    sub = lax.broadcasted_iota(jnp.int32, (8, R), 0)
    wide = [
        jnp.concatenate([gram[8 * i : 8 * i + 8], (lane == sub + 8 * i).astype(jnp.float32)], 1)
        for i in range(n)
    ]
    row = lax.broadcasted_iota(jnp.int32, (8, LANES), 0)
    out = []

    def pick(x, k):
        return jnp.broadcast_to(x[k : k + 1], (8, LANES))

    for p in range(n):
        column = [
            [jnp.broadcast_to(wide[i][:, 8 * p + k : 8 * p + k + 1], (8, LANES)) for i in range(p, n)]
            for k in range(8)
        ]
        scale = jnp.zeros((8, LANES), jnp.float32)
        for k in range(8):
            pivot = pick(column[k][0], k)
            times = 1.0 / pivot
            scale = jnp.where(row == k, lax.rsqrt(pivot), scale)
            by = [c * times for c in column[k]]
            by[0] = jnp.where(row > k, by[0], 0.0)
            for l in range(k + 1, 8):
                value = pick(column[l][0], k)
                column[l] = [c - b * value for c, b in zip(column[l], by)]
            value = pick(wide[p], k)
            for i in range(p, n):
                wide[i] = wide[i] - by[i - p] * value
        out.append(wide[p][:, R:] * scale[:, R:])
    return jnp.concatenate(out, 0)


def settle_kernel(q_ref, parts_ref, left_ref, blocks_ref, sent_ref, gram_ref):
    got = parts_ref[0]
    for b in range(1, BLOCKS):
        got = got + parts_ref[b]
    sent_ref[:, :LANES] = got[:R]
    for b in range(BLOCKS):
        blocks_ref[b] = got[:R]
    gram_ref[...] = got[R:]
    sent_ref[:, LANES:] = left_ref[:, q_ref[0]].reshape(R, left_ref.shape[3])


def settle(q, parts, left):
    return pl.pallas_call(
        settle_kernel,
        in_specs=[SMEM, VMEM, VMEM],
        out_specs=[VMEM, VMEM, VMEM],
        out_shape=[
            jax.ShapeDtypeStruct((BLOCKS, R, LANES), jnp.float32),
            jax.ShapeDtypeStruct((R, LANES + left.shape[3]), jnp.float32),
            jax.ShapeDtypeStruct((R // 2, LANES), jnp.float32),
        ],
        compiler_params=grant(6),
        name="settle",
    )(q, parts, left)


def factor_kernel(gram_ref, inverse_ref, copies_ref):
    packed = gram_ref[...]
    inverse = inverse_factor(jnp.concatenate([packed[:, :R], packed[:, R:]], 0))
    inverse_ref[...] = inverse
    for b in range(copies_ref.shape[0] // R):
        copies_ref[b * R : (b + 1) * R] = inverse


def factor(gram):
    return pl.pallas_call(
        factor_kernel,
        in_specs=[VMEM],
        out_specs=[VMEM, VMEM],
        out_shape=[
            jax.ShapeDtypeStruct((R, R), jnp.float32),
            jax.ShapeDtypeStruct((COLS // 2 * R, R), jnp.float32),
        ],
        compiler_params=grant(6),
        cost_estimate=pl.CostEstimate(flops=10**7, bytes_accessed=20 * 10**6, transcendentals=0),
        name="factor",
    )(gram)


def rollout_kernel(core_ref, left_ref, near_ref, other_ref, weight_ref, out_ref, buf, sem):
    even = core_ref[0] == 0
    width = buf.shape[2]
    copies = []
    for q in range(4):
        first, second = (near_ref, other_ref) if q % 2 == 0 else (other_ref, near_ref)
        blocks = [jnp.where(even, first[b, q // 2], second[b, q // 2]) for b in range(width // LANES)]
        delta = dot(left_ref[...], jnp.concatenate(blocks, 1), 1, 0)
        buf[q] = (weight_ref[q].astype(jnp.float32) + delta).astype(jnp.bfloat16)
        copy = pltpu.make_async_copy(buf.at[q], out_ref.at[:, pl.ds(q * width, width)], sem.at[q])
        copy.start()
        copies.append(copy)
    for copy in copies:
        copy.wait()


def rollout(core, left, near, other, weight):
    quarters, rows, width = weight.shape
    return pl.pallas_call(
        rollout_kernel,
        in_specs=[SMEM, VMEM, VMEM, VMEM, VMEM],
        out_specs=ANY,
        out_shape=jax.ShapeDtypeStruct((rows, quarters * width), jnp.bfloat16),
        scratch_shapes=[
            pltpu.VMEM((quarters, rows, width), jnp.bfloat16),
            pltpu.SemaphoreType.DMA((4,)),
        ],
        compiler_params=grant(12),
        name="rollout",
    )(core, left, near, other, weight)


def local(weight_change, error_buffer, basis, rollout_weight):
    q = lax.axis_index("col") % 4
    core = q % 2
    rows, units = weight_change.shape
    part = left_part(weight_change, error_buffer, basis.T)
    part, change, error = lax.optimization_barrier((part, weight_change, error_buffer))
    hi, lo = split(change.astype(jnp.float32) + error)
    mine = jnp.sum(exchange(part.reshape(COLS, 8, rows // 4), "col"), axis=0)
    mine, hi, lo, weight = lax.optimization_barrier((mine, hi, lo, rollout_weight))
    weight = weight.reshape(weight.shape[0], 4, units).transpose(1, 0, 2)
    left = share(mine, COLS, "col").reshape(8, 4, 8, rows // 4)
    left, weight = lax.optimization_barrier((left, weight))
    parts = exchange(right_part(hi, lo, left), "row")
    blocks, sent, gram = settle(q.astype(jnp.int32).reshape(1), parts, left)
    far = lax.ppermute(sent, AXES, SWAP)
    blocks = exchange(blocks, "row")
    inverse, copies = factor(gram)
    far, blocks, copies = lax.optimization_barrier((far, blocks, copies))
    far_round = dot(copies, far[:, :LANES], 1, 0, HIGH).astype(jnp.bfloat16).reshape(COLS // 2, R, LANES)
    far_round, inverse = lax.optimization_barrier((far_round, inverse))
    near = exchange(far_round, "col", SAME_CORE)
    right = blocks.transpose(1, 0, 2).reshape(R, LANES * BLOCKS)[:, :units]
    new_basis = dot(inverse, right, 1, 0, HIGH)
    left_rows = left.transpose(0, 2, 1, 3).reshape(R, rows)
    left_round = dot(inverse, left_rows, 1, 0, HIGH).astype(jnp.bfloat16)
    total = weight_change.astype(jnp.float32) + error_buffer
    new_error = total - dot(left_round, new_basis.astype(jnp.bfloat16), 0, 0)
    far_left = dot(far[:, LANES:], inverse, 0, 1, HIGH).astype(jnp.bfloat16)
    near, new_error, far_left = lax.optimization_barrier((near, new_error, far_left))
    other = lax.ppermute(near, "col", PAIR)
    halves = (BLOCKS, 2, R, LANES)
    new_rollout = rollout(
        core.astype(jnp.int32).reshape(1), far_left, near.reshape(halves), other.reshape(halves), weight
    )
    return (new_error, new_basis.T, new_rollout)


def solution(mesh):
    in_specs = (P("row", "col"), P("row", "col"), P("col", None), P("col", "row"))
    out_specs = (P("row", "col"), P("col", None), P("col", "row"))
    return jax.shard_map(local, mesh=mesh, in_specs=in_specs, out_specs=out_specs, check_vma=False)
```

time: 126 us -> 108 us (0.86)
  blocking collectives: 64.1 us -> 0 us
  starting transfers between devices: 15.6 us -> 42 us
  waiting for transfers between devices: 17.4 us -> 32.7 us
  local copies, waits for them, and re-layouts: 3.05 us -> 10.5 us
  matrix products: 13.8 us -> 6.98 us
  other arithmetic: 0.91 us -> 4.43 us
    all_to_all x3 -> x0, blocking collectives: 64.1 us -> none  [exchange(): return lax.all_to_all(parts, axis, 0, 0, axis_index_groups=groups)]
    all_to_all x2 -> x5, starting transfers between devices: 8.28 us -> 35.6 us  [exchange(): return lax.all_to_all(parts, axis, 0, 0, axis_index_groups=groups)]
    all_to_all x2 -> x5, waiting for transfers between devices: 17.3 us -> 31.5 us  [exchange(): return lax.all_to_all(parts, axis, 0, 0, axis_index_groups=groups)]
    dot_general x5, matrix products: 13.8 us -> 6.98 us  [dot(): lax.dot_general(a, b, (((ca,), (cb,)), ((), ())), precision=precision, pr...]
    convert_element_type x0 -> x1, other arithmetic: none -> 4.4 us  [split(): return (hi, (x - hi.astype(jnp.float32)).astype(jnp.bfloat16))]
    optimization_barrier x0 -> x1, local copies, waits for them, and re-layouts: none -> 3.82 us  [local(): lax.optimization_barrier((mine, hi, lo, rollout_weight))]
    reshape x1 -> x2, local copies, waits for them, and re-layouts: 0.02 us -> 2.87 us  [the longest x1 2.85 us: local(): weight = weight.reshape(weight.shape[0], 4, units).transpose(1, 0, 2)]
    unnamed x14 -> x8, local copies, waits for them, and re-layouts: 2.26 us -> 3.01 us
  transfers between devices with their start and end apart: 5 -> 7, of which waited for: 2 -> 6; matrix products, arithmetic and copies ran while one was open for 5% -> 16% of each run, Pallas kernels for 3% -> 2%
where the time goes in v4:
time: 108 us
  starting transfers between devices  42 us (39%)
  waiting for transfers between devices  32.7 us (30%)
  local copies, waits for them, and re-layouts  10.5 us (10%)
  Pallas kernels  10.3 us (10%)
  matrix products  6.98 us (6%)
  other arithmetic  4.43 us (4%)
    all_to_all x5, starting transfers between devices, exchange(): return lax.all_to_all(parts, axis, 0, 0, axis_index_groups=groups)  35.6 us
    all_to_all x5, waiting for transfers between devices, exchange(): return lax.all_to_all(parts, axis, 0, 0, axis_index_groups=groups)  31.5 us
    dot_general x5, matrix products, dot(): lax.dot_general(a, b, (((ca,), (cb,)), ((), ())), precision=precision, pr...  6.98 us
    ppermute x1, starting transfers between devices, local(): other = lax.ppermute(near, 'col', PAIR)  5.73 us
    convert_element_type x1, other arithmetic, split(): return (hi, (x - hi.astype(jnp.float32)).astype(jnp.bfloat16))  4.4 us
    pallas_call x1, Pallas kernels, left_part(): pl.pallas_call(left_kernel, in_specs=[ANY, ANY, ANY], out_specs=VMEM, out...  4.36 us
    optimization_barrier x1, local copies, waits for them, and re-layouts, local(): lax.optimization_barrier((mine, hi, lo, rollout_weight))  3.82 us
    unnamed x8, local copies, waits for them, and re-layouts  3.01 us
  transfers between devices with their start and end apart: 7, of which 6 were waited for; matrix products, arithmetic and copies ran while one was open for 16% of the time, Pallas kernels for 2%

profile of v4, /device:TPU:1, one launch (start us, length us, event | category | flops | bytes accessed | tf_op | source)
XLA Modules:
  0.0 107.5 jit_solution(6174276771759289280)
XLA Ops:
  0.6 0.0 copy-start.2
  0.6 4.4 %left_part.1 = f32[8,4,8,256]{3,2,1,0:T(8,128)} custom-call(bf16[1024,896]{1,0:T(8,128)(2,1)} %change_ref.1, f32[1024,896]{1,0:T(8,128)} %error_ref.1, f32[64,896]{1,0:T(8,128)} %bitcast.35), custom_call_target="tpu_custom_call" | custom-call | flops 352321536 | bytes 5505024 | tf_op jit(solution)/shard_map/left_part/pallas_call | solution.py:76
  5.0 12.6 %all-to-all-start = ((f32[32,8,256]{2,1,0:T(8,128)}), f32[32,8,256]{2,1,0:T(8,128)S(1)}, u32[]{:S(2)}, u32[]{:S(2)}) async-start(f32[32,8,256]{2,1,0:T(8,128)} %bitcast.33), calls=%async_computation | async-start | bytes 524288 | tf_op jit(solution)/shard_map/all_to_all | solution.py:29
  17.6 4.4 %subtract_convert_fusion = (bf16[1024,896]{1,0:T(8,128)(2,1)}, bf16[1024,896]{1,0:T(8,128)(2,1)}) fusion(f32[1024,896]{1,0:T(8,128)} %error_ref.1, bf16[1024,896]{1,0:T(8,128)(2,1)S(1)} %copy-done.2), kind=kLoop, calls=%fused_computation.1 | loop fusion | flops 5505024 | bytes 9175040 | tf_op jit(solution)/shard_map/convert_element_type | solution.py:25
  22.0 8.5 %all-to-all-done = f32[32,8,256]{2,1,0:T(8,128)S(1)} async-done(((f32[32,8,256]{2,1,0:T(8,128)}), f32[32,8,256]{2,1,0:T(8,128)S(1)}, u32[]{:S(2)}, u32[]{:S(2)}) %all-to-all-start) | async-done | bytes 262176 | tf_op jit(solution)/shard_map/all_to_all | solution.py:29
  30.6 0.8 broadcast_in_dim.2
  31.4 4.1 %all-to-all-start.1 = ((f32[32,8,256]{2,1,0:T(8,128)}), f32[32,8,256]{2,1,0:T(8,128)S(1)}, u32[]{:S(2)}, u32[]{:S(2)}) async-start(f32[32,8,256]{2,1,0:T(8,128)} %broadcast_in_dim.2), calls=%async_computation.1 | async-start | bytes 524288 | tf_op jit(solution)/shard_map/all_to_all | solution.py:29
  35.5 3.8 %copy.8 = bf16[256,3584]{0,1:T(8,128)(2,1)} copy(bf16[256,3584]{1,0:T(8,128)(2,1)} %param.7) | data formatting | bytes 3670016 | tf_op jit(solution)/shard_map/optimization_barrier | solution.py:248
  39.3 2.9 %copy.9 = bf16[256,4,896]{2,0,1:T(8,128)(2,1)S(1)} copy(bf16[256,4,896]{0,2,1:T(8,128)(2,1)} %bitcast.32) | data formatting | bytes 3670016 | tf_op jit(solution)/shard_map/reshape | solution.py:249
  42.2 6.3 %all-to-all-done.1 = f32[32,8,256]{2,1,0:T(8,128)S(1)} async-done(((f32[32,8,256]{2,1,0:T(8,128)}), f32[32,8,256]{2,1,0:T(8,128)S(1)}, u32[]{:S(2)}, u32[]{:S(2)}) %all-to-all-start.1) | async-done | bytes 262176 | tf_op jit(solution)/shard_map/all_to_all | solution.py:29
  48.4 1.5 %copy-done = bf16[1024,896]{1,0:T(8,128)(2,1)S(1)} copy-done((bf16[1024,896]{1,0:T(8,128)(2,1)S(1)}, bf16[1024,896]{1,0:T(8,128)(2,1)}, u32[]{:S(2)}) %copy-start) | copy-done | bytes 1835032
  49.9 1.5 %copy-done.1 = bf16[1024,896]{1,0:T(8,128)(2,1)S(1)} copy-done((bf16[1024,896]{1,0:T(8,128)(2,1)S(1)}, bf16[1024,896]{1,0:T(8,128)(2,1)}, u32[]{:S(2)}) %copy-start.1) | copy-done | bytes 1835032
  51.4 1.7 %right_part.1 = f32[8,96,128]{2,1,0:T(8,128)} custom-call(bf16[1024,896]{1,0:T(8,128)(2,1)S(1)} %copy-done.1, bf16[1024,896]{1,0:T(8,128)(2,1)S(1)} %copy-done, f32[8,4,8,256]{3,2,1,0:T(8,128)S(1)} %bitcast.27), custom_call_target="tpu_custom_call" | custom-call | flops 352321536 | bytes 3670016 | tf_op jit(solution)/shard_map/right_part/pallas_call | solution.py:112
  53.2 4.2 %all-to-all-start.2 = ((f32[8,96,128]{2,1,0:T(8,128)}), f32[8,96,128]{2,1,0:T(8,128)S(1)}, u32[]{:S(2)}, u32[]{:S(2)}) async-start(f32[8,96,128]{2,1,0:T(8,128)} %right_part.1), calls=%async_computation.2 | async-start | bytes 786432 | tf_op jit(solution)/shard_map/all_to_all | solution.py:29
  57.4 8.1 %all-to-all-done.2.parts_ref = f32[8,96,128]{2,1,0:T(8,128)S(1)} async-done(((f32[8,96,128]{2,1,0:T(8,128)}), f32[8,96,128]{2,1,0:T(8,128)S(1)}, u32[]{:S(2)}, u32[]{:S(2)}) %all-to-all-start.2) | async-done | bytes 393248 | tf_op jit(solution)/shard_map/all_to_all | solution.py:29
  65.5 0.7 settle.1
  66.2 3.4 %all-to-all-start.3 = ((f32[8,64,128]{2,1,0:T(8,128)}), f32[8,64,128]{2,1,0:T(8,128)S(1)}, u32[]{:S(2)}, u32[]{:S(2)}) async-start(f32[8,64,128]{2,1,0:T(8,128)} %get-tuple-element.34), calls=%async_computation.3 | async-start | bytes 524288 | tf_op jit(solution)/shard_map/all_to_all | solution.py:29
  69.6 0.7 collective-permute-start
  70.3 1.9 %factor.1 = (f32[64,64]{1,0:T(8,128)S(1)}, f32[1024,64]{1,0:T(8,128)S(1)}) custom-call(f32[32,128]{1,0:T(8,128)S(1)} %get-tuple-element.35.gram_ref), custom_call_target="tpu_custom_call" | custom-call | flops 10000000 | bytes 20000000 | tf_op jit(solution)/shard_map/factor/pallas_call | solution.py:194
  72.2 0.0 collective-permute-done
  72.2 3.5 %all-to-all-done.3 = f32[8,64,128]{2,1,0:T(8,128)S(1)} async-done(((f32[8,64,128]{2,1,0:T(8,128)}), f32[8,64,128]{2,1,0:T(8,128)S(1)}, u32[]{:S(2)}, u32[]{:S(2)}) %all-to-all-start.3) | async-done | bytes 262176 | tf_op jit(solution)/shard_map/all_to_all | solution.py:29
  75.7 1.1 convolution_convert_fusion
  76.8 11.2 %all-to-all-start.4 = ((bf16[16,64,128]{2,1,0:T(8,128)(2,1)}), bf16[16,64,128]{2,1,0:T(8,128)(2,1)S(1)}, u32[]{:S(2)}, u32[]{:S(2)}) async-start(bf16[16,64,128]{2,1,0:T(8,128)(2,1)} %bitcast.6), calls=%async_computation.4 | async-start | bytes 524288 | tf_op jit(solution)/shard_map/all_to_all | solution.py:29
  88.0 0.3 convolution_convert_fusion.1
  88.3 0.2 fusion.1
  88.5 0.0 copy-start.3
  88.5 0.3 convolution_convert_fusion.2.left_ref
  88.8 5.1 %add_subtract_fusion = f32[1024,896]{1,0:T(8,128)} fusion(f32[1024,896]{1,0:T(8,128)} %error_ref.1, bf16[1024,896]{1,0:T(8,128)(2,1)} %change_ref.1, bf16[64,1024]{1,0:T(8,128)(2,1)S(1)} %convolution_convert_fusion.1, f32[64,896]{1,0:T(8,128)S(1)} %fusion.1), kind=kOutput, calls=%fused_computation | convolution fusion | flops 120250368 | bytes 9535488 | tf_op jit(solution)/shard_map/dot_general | solution.py:18
  94.0 5.1 %all-to-all-done.4 = bf16[16,64,128]{2,1,0:T(8,128)(2,1)S(1)} async-done(((bf16[16,64,128]{2,1,0:T(8,128)(2,1)}), bf16[16,64,128]{2,1,0:T(8,128)(2,1)S(1)}, u32[]{:S(2)}, u32[]{:S(2)}) %all-to-all-start.4) | async-done | bytes 262176 | tf_op jit(solution)/shard_map/all_to_all | solution.py:29
  99.1 5.7 %collective-permute-start.1 = (bf16[16,64,128]{2,1,0:T(8,128)(2,1)S(1)}, bf16[16,64,128]{2,1,0:T(8,128)(2,1)S(1)}, u32[]{:S(2)}, u32[]{:S(2)}) collective-permute-start(bf16[16,64,128]{2,1,0:T(8,128)(2,1)S(1)} %all-to-all-done.4), channel_id=1, source_target_pairs={{0,1},{1,0},{2,3},{3,2},{4,5},{5,4},{6,7},{7,6},{8,9},{9,8},{10,11... | collective-permute-start | bytes 786440 | tf_op jit(solution)/shard_map/ppermute | solution.py:269
  104.8 1.2 %collective-permute-done.1 = bf16[16,64,128]{2,1,0:T(8,128)(2,1)S(1)} collective-permute-done((bf16[16,64,128]{2,1,0:T(8,128)(2,1)S(1)}, bf16[16,64,128]{2,1,0:T(8,128)(2,1)S(1)}, u32[]{:S(2)}, u32[]{:S(2)}) %collective-permute-start.1) | collective-permute-done | bytes 262176 | tf_op jit(solution)/shard_map/ppermute | solution.py:269
  106.0 1.5 %rollout.1 = bf16[256,3584]{1,0:T(8,128)(2,1)} custom-call(s32[1]{0:T(128)} %bitcast.11.core_ref, bf16[256,64]{1,0:T(8,128)(2,1)S(1)} %convolution_convert_fusion.2.left_ref, bf16[8,2,64,128]{3,2,1,0:T(8,128)(2,1)S(1)} %bitcast.30, bf16[8,2,64,128]{3,2,1,0:T(8,128)(2,1)S(1)} %bitcast.31, bf16[4,256,896]{2,1,0:T(8,128)(2,1)S(1)} %bitcast.26), custom_call_target="tpu_custom_call" | custom-call | tf_op jit(solution)/shard_map/rollout/pallas_call | solution.py:226
  (6 shorter events, 0.1 us)
Async XLA Ops:
  0.6 17.0 %copy-start.2 = (bf16[1024,896]{1,0:T(8,128)(2,1)S(1)}, bf16[1024,896]{1,0:T(8,128)(2,1)}, u32[]{:S(2)}) copy-start(bf16[1024,896]{1,0:T(8,128)(2,1)} %change_ref.1) | copy-start | bytes 5505028
  5.0 25.5 %all-to-all-start = ((f32[32,8,256]{2,1,0:T(8,128)}), f32[32,8,256]{2,1,0:T(8,128)S(1)}, u32[]{:S(2)}, u32[]{:S(2)}) async-start(f32[32,8,256]{2,1,0:T(8,128)} %bitcast.33), calls=%async_computation | async-start | bytes 524288 | tf_op jit(solution)/shard_map/all_to_all | solution.py:29
  31.4 17.1 %all-to-all-start.1 = ((f32[32,8,256]{2,1,0:T(8,128)}), f32[32,8,256]{2,1,0:T(8,128)S(1)}, u32[]{:S(2)}, u32[]{:S(2)}) async-start(f32[32,8,256]{2,1,0:T(8,128)} %broadcast_in_dim.2), calls=%async_computation.1 | async-start | bytes 524288 | tf_op jit(solution)/shard_map/all_to_all | solution.py:29
  48.4 1.5 %copy-start = (bf16[1024,896]{1,0:T(8,128)(2,1)S(1)}, bf16[1024,896]{1,0:T(8,128)(2,1)}, u32[]{:S(2)}) copy-start(bf16[1024,896]{1,0:T(8,128)(2,1)} %get-tuple-element.29.lo_ref) | copy-start | bytes 5505028
  49.9 1.5 %copy-start.1 = (bf16[1024,896]{1,0:T(8,128)(2,1)S(1)}, bf16[1024,896]{1,0:T(8,128)(2,1)}, u32[]{:S(2)}) copy-start(bf16[1024,896]{1,0:T(8,128)(2,1)} %get-tuple-element.28.hi_ref) | copy-start | bytes 5505028
  53.2 12.3 %all-to-all-start.2 = ((f32[8,96,128]{2,1,0:T(8,128)}), f32[8,96,128]{2,1,0:T(8,128)S(1)}, u32[]{:S(2)}, u32[]{:S(2)}) async-start(f32[8,96,128]{2,1,0:T(8,128)} %right_part.1), calls=%async_computation.2 | async-start | bytes 786432 | tf_op jit(solution)/shard_map/all_to_all | solution.py:29
  66.2 9.5 %all-to-all-start.3 = ((f32[8,64,128]{2,1,0:T(8,128)}), f32[8,64,128]{2,1,0:T(8,128)S(1)}, u32[]{:S(2)}, u32[]{:S(2)}) async-start(f32[8,64,128]{2,1,0:T(8,128)} %get-tuple-element.34), calls=%async_computation.3 | async-start | bytes 524288 | tf_op jit(solution)/shard_map/all_to_all | solution.py:29
  69.6 2.6 %collective-permute-start = (f32[64,384]{1,0:T(8,128)S(1)}, f32[64,384]{1,0:T(8,128)S(1)}, u32[]{:S(2)}, u32[]{:S(2)}) collective-permute-start(f32[64,384]{1,0:T(8,128)S(1)} %get-tuple-element.33), channel_id=1, source_target_pairs={{0,0},{1,1},{2,2},{3,3},{4,32},{5,33},{6,34},{7,35},{8,64},{9,65},... | collective-permute-start | bytes 294920 | tf_op jit(solution)/shard_map/ppermute | solution.py:254
  76.8 22.3 %all-to-all-start.4 = ((bf16[16,64,128]{2,1,0:T(8,128)(2,1)}), bf16[16,64,128]{2,1,0:T(8,128)(2,1)S(1)}, u32[]{:S(2)}, u32[]{:S(2)}) async-start(bf16[16,64,128]{2,1,0:T(8,128)(2,1)} %bitcast.6), calls=%async_computation.4 | async-start | bytes 524288 | tf_op jit(solution)/shard_map/all_to_all | solution.py:29
  88.5 5.4 %copy-start.3 = (f32[64,896]{1,0:T(8,128)}, f32[64,896]{1,0:T(8,128)S(1)}, u32[]{:S(2)}) copy-start(f32[64,896]{1,0:T(8,128)S(1)} %fusion.1) | copy-start | bytes 688132
  99.1 6.9 %collective-permute-start.1 = (bf16[16,64,128]{2,1,0:T(8,128)(2,1)S(1)}, bf16[16,64,128]{2,1,0:T(8,128)(2,1)S(1)}, u32[]{:S(2)}, u32[]{:S(2)}) collective-permute-start(bf16[16,64,128]{2,1,0:T(8,128)(2,1)S(1)} %all-to-all-done.4), channel_id=1, source_target_pairs={{0,1},{1,0},{2,3},{3,2},{4,5},{5,4},{6,7},{7,6},{8,9},{9,8},{10,11... | collective-permute-start | bytes 786440 | tf_op jit(solution)/shard_map/ppermute | solution.py:269

commit v5 on v4

--- a/solution.py
+++ b/solution.py
@@ -9,7 +9,32 @@
 HIGHEST = lax.Precision.HIGHEST
 ROWS, COLS, R, LANES, BLOCKS = 8, 32, 64, 128, 8
 AXES = ("row", "col")
-SWAP = [(r * COLS + c, (c // 4) * COLS + 4 * r + c % 4) for r in range(ROWS) for c in range(COLS)]
+
+
+def row_hops(a, b):
+    y = abs(a // 2 - b // 2)
+    return min(y, 4 - y) + abs(a % 2 - b % 2)
+
+
+def partners(row):
+    rows = sorted(range(ROWS), key=lambda r: (row_hops(r, row), r))
+    places = sorted(range(8), key=lambda k: (-min(k, 8 - k), k))
+    return {r: (row + k) % 8 for r, k in zip(rows, places)}
+
+
+SLOTS = [[partners(z)[r] for r in range(ROWS)] for z in range(8)]
+SPREAD = [
+    (r * COLS + 4 * z + q, z * COLS + 4 * SLOTS[z][r] + q)
+    for r in range(ROWS)
+    for z in range(8)
+    for q in range(4)
+]
+FANOUT = [
+    (r * COLS + 4 * z + q, t * COLS + 4 * r + q)
+    for r in range(ROWS)
+    for t, z in partners(r).items()
+    for q in range(4)
+]
 SAME_CORE = [[c for c in range(COLS) if c % 2 == core] for core in range(2)]
 PAIR = [(c, c ^ 1) for c in range(COLS)]
 
@@ -27,10 +52,6 @@
 
 def exchange(parts, axis, groups=None):
     return lax.all_to_all(parts, axis, 0, 0, axis_index_groups=groups)
-
-
-def share(mine, n, axis, groups=None):
-    return exchange(jnp.broadcast_to(mine[None], (n,) + mine.shape), axis, groups)
 
 
 ANY = pl.BlockSpec(memory_space=pl.ANY)
@@ -91,11 +112,29 @@
     )(change, error, basis)
 
 
-def right_kernel(hi_ref, lo_ref, left_ref, out_ref):
+def sum_share_kernel(parts_ref, out_ref):
+    total = parts_ref[0]
+    for i in range(1, parts_ref.shape[0]):
+        total = total + parts_ref[i]
+    for i in range(out_ref.shape[0]):
+        out_ref[i] = total
+
+
+def sum_share(parts):
+    return pl.pallas_call(
+        sum_share_kernel,
+        in_specs=[VMEM],
+        out_specs=VMEM,
+        out_shape=jax.ShapeDtypeStruct(parts.shape, parts.dtype),
+        compiler_params=grant(6),
+        name="sum_share",
+    )(parts)
+
+
+def right_kernel(total_ref, left_ref, out_ref):
     left = jnp.concatenate([left_ref[:, i].reshape(R, -1) for i in range(4)], 1)
-    left_hi, left_lo = split(left)
-    both = dot(jnp.concatenate([left_hi, left_lo], 0), hi_ref[...], 1, 0)
-    right = both[:R] + both[R:] + dot(left_hi, lo_ref[...], 1, 0)
+    both = dot(jnp.concatenate(split(left), 0), total_ref[...], 1, 0)
+    right = both[:R] + both[R:]
     used = right.shape[1] // LANES
     for b in range(used):
         out_ref[b, :R] = right[:, b * LANES : (b + 1) * LANES]
@@ -107,17 +146,17 @@
         out_ref[b, R:, R:] = gram[R // 2 :]
 
 
-def right_part(hi, lo, left):
-    rows, units = hi.shape
+def right_part(total, left):
+    rows, units = total.shape
     return pl.pallas_call(
         right_kernel,
-        in_specs=[VMEM, VMEM, VMEM],
+        in_specs=[VMEM, VMEM],
         out_specs=VMEM,
         out_shape=jax.ShapeDtypeStruct((BLOCKS, R + R // 2, LANES), jnp.float32),
         compiler_params=grant(12),
-        cost_estimate=pl.CostEstimate(flops=6 * rows * units * R, bytes_accessed=4 * rows * units, transcendentals=0),
+        cost_estimate=pl.CostEstimate(flops=4 * rows * units * R, bytes_accessed=2 * rows * units, transcendentals=0),
         name="right_part",
-    )(hi, lo, left)
+    )(total, left)
 
 
 def inverse_factor(gram):
@@ -156,30 +195,26 @@
     return jnp.concatenate(out, 0)
 
 
-def settle_kernel(q_ref, parts_ref, left_ref, blocks_ref, sent_ref, gram_ref):
+def settle_kernel(parts_ref, block_ref, gram_ref):
     got = parts_ref[0]
     for b in range(1, BLOCKS):
         got = got + parts_ref[b]
-    sent_ref[:, :LANES] = got[:R]
-    for b in range(BLOCKS):
-        blocks_ref[b] = got[:R]
+    block_ref[...] = got[:R]
     gram_ref[...] = got[R:]
-    sent_ref[:, LANES:] = left_ref[:, q_ref[0]].reshape(R, left_ref.shape[3])
-
-
-def settle(q, parts, left):
+
+
+def settle(parts):
     return pl.pallas_call(
         settle_kernel,
-        in_specs=[SMEM, VMEM, VMEM],
-        out_specs=[VMEM, VMEM, VMEM],
+        in_specs=[VMEM],
+        out_specs=[VMEM, VMEM],
         out_shape=[
-            jax.ShapeDtypeStruct((BLOCKS, R, LANES), jnp.float32),
-            jax.ShapeDtypeStruct((R, LANES + left.shape[3]), jnp.float32),
+            jax.ShapeDtypeStruct((R, LANES), jnp.float32),
             jax.ShapeDtypeStruct((R // 2, LANES), jnp.float32),
         ],
         compiler_params=grant(6),
         name="settle",
-    )(q, parts, left)
+    )(parts)
 
 
 def factor_kernel(gram_ref, inverse_ref, copies_ref):
@@ -205,13 +240,45 @@
     )(gram)
 
 
-def rollout_kernel(core_ref, left_ref, near_ref, other_ref, weight_ref, out_ref, buf, sem):
+def basis_kernel(row_ref, inverse_ref, mine_ref, other_ref, basis_ref, round_ref):
+    y, odd = row_ref[0] // 2, row_ref[0] % 2
+    blocks = []
+    for b in range(basis_ref.shape[1] // LANES):
+        value = jnp.zeros((R, LANES), jnp.float32)
+        for k in range(4):
+            lanes = slice(k * LANES, (k + 1) * LANES)
+            picked = jnp.where(odd == b % 2, mine_ref[:, lanes], other_ref[:, lanes])
+            value = jnp.where((y + 4 - k) % 4 == b // 2, picked, value)
+        blocks.append(value)
+    basis = dot(inverse_ref[...], jnp.concatenate(blocks, 1), 1, 0, HIGHEST)
+    basis_ref[...] = basis
+    round_ref[...] = basis.astype(jnp.bfloat16)
+
+
+def basis_part(row, inverse, mine, other, units):
+    return pl.pallas_call(
+        basis_kernel,
+        in_specs=[SMEM] + [VMEM] * 3,
+        out_specs=[VMEM, VMEM],
+        out_shape=[
+            jax.ShapeDtypeStruct((R, units), jnp.float32),
+            jax.ShapeDtypeStruct((R, units), jnp.bfloat16),
+        ],
+        compiler_params=grant(6),
+        name="basis_part",
+    )(row, inverse, mine, other)
+
+
+def rollout_kernel(core_ref, slots_ref, left_ref, near_ref, other_ref, weight_ref, out_ref, buf, sem):
     even = core_ref[0] == 0
     width = buf.shape[2]
     copies = []
     for q in range(4):
         first, second = (near_ref, other_ref) if q % 2 == 0 else (other_ref, near_ref)
-        blocks = [jnp.where(even, first[b, q // 2], second[b, q // 2]) for b in range(width // LANES)]
+        blocks = []
+        for b in range(width // LANES):
+            slot = slots_ref[b]
+            blocks.append(jnp.where(even, first[slot, q // 2], second[slot, q // 2]))
         delta = dot(left_ref[...], jnp.concatenate(blocks, 1), 1, 0)
         buf[q] = (weight_ref[q].astype(jnp.float32) + delta).astype(jnp.bfloat16)
         copy = pltpu.make_async_copy(buf.at[q], out_ref.at[:, pl.ds(q * width, width)], sem.at[q])
@@ -221,11 +288,11 @@
         copy.wait()
 
 
-def rollout(core, left, near, other, weight):
+def rollout(core, slots, left, near, other, weight):
     quarters, rows, width = weight.shape
     return pl.pallas_call(
         rollout_kernel,
-        in_specs=[SMEM, VMEM, VMEM, VMEM, VMEM],
+        in_specs=[SMEM, SMEM, VMEM, VMEM, VMEM, VMEM],
         out_specs=ANY,
         out_shape=jax.ShapeDtypeStruct((rows, quarters * width), jnp.bfloat16),
         scratch_shapes=[
@@ -234,43 +301,45 @@
         ],
         compiler_params=grant(12),
         name="rollout",
-    )(core, left, near, other, weight)
+    )(core, slots, left, near, other, weight)
 
 
 def local(weight_change, error_buffer, basis, rollout_weight):
+    row = lax.axis_index("row")
     q = lax.axis_index("col") % 4
     core = q % 2
     rows, units = weight_change.shape
     part = left_part(weight_change, error_buffer, basis.T)
     part, change, error = lax.optimization_barrier((part, weight_change, error_buffer))
-    hi, lo = split(change.astype(jnp.float32) + error)
-    mine = jnp.sum(exchange(part.reshape(COLS, 8, rows // 4), "col"), axis=0)
-    mine, hi, lo, weight = lax.optimization_barrier((mine, hi, lo, rollout_weight))
-    weight = weight.reshape(weight.shape[0], 4, units).transpose(1, 0, 2)
-    left = share(mine, COLS, "col").reshape(8, 4, 8, rows // 4)
-    left, weight = lax.optimization_barrier((left, weight))
-    parts = exchange(right_part(hi, lo, left), "row")
-    blocks, sent, gram = settle(q.astype(jnp.int32).reshape(1), parts, left)
-    far = lax.ppermute(sent, AXES, SWAP)
-    blocks = exchange(blocks, "row")
+    total = (change.astype(jnp.float32) + error).astype(jnp.bfloat16)
+    parts = exchange(part.reshape(COLS, 8, rows // 4), "col")
+    parts, total = lax.optimization_barrier((parts, total))
+    left = exchange(sum_share(parts), "col").reshape(8, 4, 8, rows // 4)
+    sums, weight = lax.optimization_barrier((right_part(total, left), rollout_weight))
+    weight = jnp.stack([weight[:, i * units : (i + 1) * units] for i in range(4)])
+    mine = lax.dynamic_index_in_dim(left, q, 1, keepdims=False).reshape(R, rows // 4)
+    far_left = lax.ppermute(mine, AXES, FANOUT)
+    parts, weight, far_left = lax.optimization_barrier((exchange(sums, "row"), weight, far_left))
+    block, gram = settle(parts)
+    far = lax.ppermute(block, AXES, SPREAD)
+    blocks = [lax.ppermute(block, "row", [(r, (r + 2 * k) % ROWS) for r in range(ROWS)]) for k in (1, 2, 3)]
     inverse, copies = factor(gram)
-    far, blocks, copies = lax.optimization_barrier((far, blocks, copies))
-    far_round = dot(copies, far[:, :LANES], 1, 0, HIGH).astype(jnp.bfloat16).reshape(COLS // 2, R, LANES)
-    far_round, inverse = lax.optimization_barrier((far_round, inverse))
+    far_round = dot(copies, far, 1, 0, HIGH).astype(jnp.bfloat16).reshape(COLS // 2, R, LANES)
+    blocks = jnp.concatenate([block] + blocks, 1)
+    far_round, inverse, blocks = lax.optimization_barrier((far_round, inverse, blocks))
     near = exchange(far_round, "col", SAME_CORE)
-    right = blocks.transpose(1, 0, 2).reshape(R, LANES * BLOCKS)[:, :units]
-    new_basis = dot(inverse, right, 1, 0, HIGH)
+    other_blocks = lax.ppermute(blocks, "row", [(r, r ^ 1) for r in range(ROWS)])
     left_rows = left.transpose(0, 2, 1, 3).reshape(R, rows)
     left_round = dot(inverse, left_rows, 1, 0, HIGH).astype(jnp.bfloat16)
-    total = weight_change.astype(jnp.float32) + error_buffer
-    new_error = total - dot(left_round, new_basis.astype(jnp.bfloat16), 0, 0)
-    far_left = dot(far[:, LANES:], inverse, 0, 1, HIGH).astype(jnp.bfloat16)
-    near, new_error, far_left = lax.optimization_barrier((near, new_error, far_left))
+    far_left = dot(far_left, inverse, 0, 1, HIGH).astype(jnp.bfloat16)
+    new_basis, right_round = basis_part(row.astype(jnp.int32).reshape(1), inverse, blocks, other_blocks, units)
+    new_error = weight_change.astype(jnp.float32) + error_buffer - dot(left_round, right_round, 0, 0)
+    near, far_left, new_error = lax.optimization_barrier((near, far_left, new_error))
     other = lax.ppermute(near, "col", PAIR)
     halves = (BLOCKS, 2, R, LANES)
-    new_rollout = rollout(
-        core.astype(jnp.int32).reshape(1), far_left, near.reshape(halves), other.reshape(halves), weight
-    )
+    slots = jnp.asarray(SLOTS, jnp.int32)[row]
+    core = core.astype(jnp.int32).reshape(1)
+    new_rollout = rollout(core, slots, far_left, near.reshape(halves), other.reshape(halves), weight)
     return (new_error, new_basis.T, new_rollout)
 
 

time: 108 us -> 99.6 us (0.922)
  local copies, waits for them, and re-layouts: 10.5 us -> 2.28 us
  waiting for transfers between devices: 32.7 us -> 29.7 us
  starting transfers between devices: 42 us -> 44.9 us
  Pallas kernels: 10.3 us -> 11.5 us
  other arithmetic: 4.43 us -> 3.24 us
    ppermute x1 -> x6, starting transfers between devices: 0.67 us -> 15.7 us  [the longest x3 8.13 us: local(): lax.ppermute(block, 'row', [(r, (r + 2 * k) % ROWS) for r in range(ROWS)])]
    all_to_all x5 -> x4, starting transfers between devices: 35.6 us -> 24.5 us  [exchange(): return lax.all_to_all(parts, axis, 0, 0, axis_index_groups=groups)]
    all_to_all x5 -> x4, waiting for transfers between devices: 31.5 us -> 24.7 us  [exchange(): return lax.all_to_all(parts, axis, 0, 0, axis_index_groups=groups)]
    ppermute x1 -> x6, waiting for transfers between devices: 0.01 us -> 4.55 us  [the longest x1 2.03 us: local(): lax.ppermute(blocks, 'row', [(r, r ^ 1) for r in range(ROWS)])]
    optimization_barrier x1 -> x0, local copies, waits for them, and re-layouts: 3.82 us -> none  [local(): lax.optimization_barrier((mine, hi, lo, rollout_weight))]
    unnamed x8 -> x0, local copies, waits for them, and re-layouts: 3.01 us -> none
    reshape x2 -> x1, local copies, waits for them, and re-layouts: 2.87 us -> 0.01 us  [local(): lax.dynamic_index_in_dim(left, q, 1, keepdims=False).reshape(R, rows // 4)]
    another operation x0 -> x1, local copies, waits for them, and re-layouts: none -> 1.59 us  [local(): weight = jnp.stack([weight[:, i * units:(i + 1) * units] for i in range(4)])]
  transfers between devices with their start and end apart: 7 -> 11, of which waited for: 6 -> 8; matrix products, arithmetic and copies ran while one was open for 16% -> 12% of each run, Pallas kernels for 2% -> 3%
where the time goes in v5:
time: 99.6 us; the launch traced here: 99.1 us
  starting transfers between devices  44.9 us (45%)
  waiting for transfers between devices  29.7 us (30%)
  Pallas kernels  11.5 us (12%)
  matrix products  6.74 us (7%)
  other arithmetic  3.24 us (3%)
  local copies, waits for them, and re-layouts  2.28 us (2%)
    all_to_all x4, waiting for transfers between devices, exchange(): return lax.all_to_all(parts, axis, 0, 0, axis_index_groups=groups)  24.7 us
    all_to_all x4, starting transfers between devices, exchange(): return lax.all_to_all(parts, axis, 0, 0, axis_index_groups=groups)  24.5 us
    ppermute x3, starting transfers between devices, local(): lax.ppermute(block, 'row', [(r, (r + 2 * k) % ROWS) for r in range(ROWS)])  8.13 us
    dot_general x4, matrix products, dot(): lax.dot_general(a, b, (((ca,), (cb,)), ((), ())), precision=precision, pr...  6.74 us
    ppermute x1, starting transfers between devices, local(): other = lax.ppermute(near, 'col', PAIR)  4.68 us
    pallas_call x1, Pallas kernels, left_part(): pl.pallas_call(left_kernel, in_specs=[ANY, ANY, ANY], out_specs=VMEM, out...  4.24 us
    ppermute x1, starting transfers between devices, local(): far_left = lax.ppermute(mine, AXES, FANOUT)  3.94 us
    convert_element_type x1, other arithmetic, local(): total = (change.astype(jnp.float32) + error).astype(jnp.bfloat16)  2.95 us
  transfers between devices with their start and end apart: 11, of which 8 were waited for; matrix products, arithmetic and copies ran while one was open for 12% of the time, Pallas kernels for 3%

profile of v5, /device:TPU:1, one launch (start us, length us, event | category | flops | bytes accessed | tf_op | source)
XLA Modules:
  0.0 99.1 jit_solution(17874342845554201576)
XLA Ops:
  0.6 4.2 %left_part.1 = f32[8,4,8,256]{3,2,1,0:T(8,128)} custom-call(bf16[1024,896]{1,0:T(8,128)(2,1)} %change_ref.1, f32[1024,896]{1,0:T(8,128)} %error_ref.1, f32[64,896]{1,0:T(8,128)} %bitcast.39), custom_call_target="tpu_custom_call" | custom-call | flops 352321536 | bytes 5505024 | tf_op jit(solution)/shard_map/left_part/pallas_call | solution.py:97
  4.9 12.6 %all-to-all-start = ((f32[32,8,256]{2,1,0:T(8,128)}), f32[32,8,256]{2,1,0:T(8,128)S(1)}, u32[]{:S(2)}, u32[]{:S(2)}) async-start(f32[32,8,256]{2,1,0:T(8,128)} %bitcast.38), calls=%async_computation | async-start | bytes 524288 | tf_op jit(solution)/shard_map/all_to_all | solution.py:54
  17.5 3.0 %add_convert_fusion.total_ref = bf16[1024,896]{1,0:T(8,128)(2,1)S(1)} fusion(f32[1024,896]{1,0:T(8,128)} %error_ref.1, bf16[1024,896]{1,0:T(8,128)(2,1)} %change_ref.1), kind=kLoop, calls=%fused_computation.1 | loop fusion | flops 2752512 | bytes 7340032 | tf_op jit(solution)/shard_map/convert_element_type | solution.py:314
  20.4 10.0 %all-to-all-done.parts_ref = f32[32,8,256]{2,1,0:T(8,128)S(1)} async-done(((f32[32,8,256]{2,1,0:T(8,128)}), f32[32,8,256]{2,1,0:T(8,128)S(1)}, u32[]{:S(2)}, u32[]{:S(2)}) %all-to-all-start) | async-done | bytes 262176 | tf_op jit(solution)/shard_map/all_to_all | solution.py:54
  30.4 0.8 sum_share.1
  31.2 4.1 %all-to-all-start.1 = ((f32[32,8,256]{2,1,0:T(8,128)}), f32[32,8,256]{2,1,0:T(8,128)S(1)}, u32[]{:S(2)}, u32[]{:S(2)}) async-start(f32[32,8,256]{2,1,0:T(8,128)} %sum_share.1), calls=%async_computation.1 | async-start | bytes 524288 | tf_op jit(solution)/shard_map/all_to_all | solution.py:54
  35.3 12.9 %all-to-all-done.1 = f32[32,8,256]{2,1,0:T(8,128)S(1)} async-done(((f32[32,8,256]{2,1,0:T(8,128)}), f32[32,8,256]{2,1,0:T(8,128)S(1)}, u32[]{:S(2)}, u32[]{:S(2)}) %all-to-all-start.1) | async-done | bytes 262176 | tf_op jit(solution)/shard_map/all_to_all | solution.py:54
  48.3 1.5 %right_part.1 = f32[8,96,128]{2,1,0:T(8,128)} custom-call(bf16[1024,896]{1,0:T(8,128)(2,1)S(1)} %add_convert_fusion.total_ref, f32[8,4,8,256]{3,2,1,0:T(8,128)S(1)} %bitcast.33), custom_call_target="tpu_custom_call" | custom-call | flops 234881024 | bytes 1835008 | tf_op jit(solution)/shard_map/right_part/pallas_call | solution.py:151
  49.7 4.2 %all-to-all-start.2 = ((f32[8,96,128]{2,1,0:T(8,128)}), f32[8,96,128]{2,1,0:T(8,128)S(1)}, u32[]{:S(2)}, u32[]{:S(2)}) async-start(f32[8,96,128]{2,1,0:T(8,128)} %right_part.1), calls=%async_computation.2 | async-start | bytes 786432 | tf_op jit(solution)/shard_map/all_to_all | solution.py:54
  53.9 3.9 %collective-permute-start = (f32[64,256]{1,0:T(8,128)S(1)}, f32[64,256]{1,0:T(8,128)S(1)}, u32[]{:S(2)}, u32[]{:S(2)}) collective-permute-start(f32[64,256]{1,0:T(8,128)S(1)} %dynamic-slice_bitcast_fusion), channel_id=1, source_target_pairs={{16,0},{17,1},{18,2},{19,3},{12,32},{13,33},{14,34},{15,35},{20,64... | collective-permute-start | bytes 196616 | tf_op jit(solution)/shard_map/ppermute | solution.py:321
  57.9 1.6 %slice_bitcast_fusion.3 = (bf16[1,256,896]{2,1,0:T(8,128)(2,1)S(1)}, bf16[1,256,896]{2,1,0:T(8,128)(2,1)S(1)}, bf16[1,256,896]{2,1,0:T(8,128)(2,1)S(1)}, bf16[1,256,896]{2,1,0:T(8,128)(2,1)S(1)}) fusion(bf16[256,3584]{1,0:T(8,128)(2,1)} %param.8), kind=kLoop, calls=%fused_computation.9 | loop fusion | bytes 3670016 | tf_op jit(solution)/shard_map/stack | solution.py:319
  59.5 0.3 pad_maximum_fusion.weight_ref
  59.8 1.5 %collective-permute-done = f32[64,256]{1,0:T(8,128)S(1)} collective-permute-done((f32[64,256]{1,0:T(8,128)S(1)}, f32[64,256]{1,0:T(8,128)S(1)}, u32[]{:S(2)}, u32[]{:S(2)}) %collective-permute-start) | collective-permute-done | bytes 65568 | tf_op jit(solution)/shard_map/ppermute | solution.py:321
  61.3 0.7 all-to-all-done.2.parts_ref
  62.0 2.3 %collective-permute-start.1 = (f32[64,128]{1,0:T(8,128)S(1)}, f32[64,128]{1,0:T(8,128)S(1)}, u32[]{:S(2)}, u32[]{:S(2)}) collective-permute-start(f32[64,128]{1,0:T(8,128)S(1)} %get-tuple-element.35), channel_id=1, source_target_pairs={{0,16},{1,17},{2,18},{3,19},{4,48},{5,49},{6,50},{7,51},{8,84},{9,... | collective-permute-start | bytes 98312 | tf_op jit(solution)/shard_map/ppermute | solution.py:324
  64.3 1.5 %collective-permute-start.4 = (f32[64,128]{1,0:T(8,128)S(1)}, f32[64,128]{1,0:T(8,128)S(1)}, u32[]{:S(2)}, u32[]{:S(2)}) collective-permute-start(f32[64,128]{1,0:T(8,128)S(1)} %get-tuple-element.35), channel_id=1, source_target_pairs={{0,192},{32,224},{64,0},{96,32},{128,64},{160,96},{192,128},{224,1... | collective-permute-start | bytes 98312 | tf_op jit(solution)/shard_map/ppermute | solution.py:325
  65.8 6.6 %collective-permute-start.3 = (f32[64,128]{1,0:T(8,128)S(1)}, f32[64,128]{1,0:T(8,128)S(1)}, u32[]{:S(2)}, u32[]{:S(2)}) collective-permute-start(f32[64,128]{1,0:T(8,128)S(1)} %get-tuple-element.35), channel_id=1, source_target_pairs={{0,128},{32,160},{64,192},{96,224},{128,0},{160,32},{192,64},{224,... | collective-permute-start | bytes 98312 | tf_op jit(solution)/shard_map/ppermute | solution.py:325
  72.4 1.9 %factor.1 = (f32[64,64]{1,0:T(8,128)S(1)}, f32[1024,64]{1,0:T(8,128)S(1)}) custom-call(f32[32,128]{1,0:T(8,128)S(1)} %get-tuple-element.33.gram_ref), custom_call_target="tpu_custom_call" | custom-call | flops 10000000 | bytes 20000000 | tf_op jit(solution)/shard_map/factor/pallas_call | solution.py:229
  74.3 1.1 %convolution_convert_fusion = bf16[1024,128]{1,0:T(8,128)(2,1)} fusion(f32[1024,64]{1,0:T(8,128)S(1)} %get-tuple-element.34, f32[64,128]{1,0:T(8,128)S(1)} %collective-permute-done.1), kind=kOutput, calls=%fused_computation.3 | convolution fusion | flops 50462720 | bytes 557056 | tf_op jit(solution)/shard_map/dot_general | solution.py:43
  75.4 1.0 collective-permute-done.2
  76.4 3.5 %all-to-all-start.3 = ((bf16[16,64,128]{2,1,0:T(8,128)(2,1)}), bf16[16,64,128]{2,1,0:T(8,128)(2,1)S(1)}, u32[]{:S(2)}, u32[]{:S(2)}) async-start(bf16[16,64,128]{2,1,0:T(8,128)(2,1)} %bitcast.8), calls=%async_computation.3 | async-start | bytes 524288 | tf_op jit(solution)/shard_map/all_to_all | solution.py:54
  80.0 1.4 %collective-permute-start.5 = (f32[64,512]{1,0:T(8,128)S(1)}, f32[64,512]{1,0:T(8,128)S(1)}, u32[]{:S(2)}, u32[]{:S(2)}) collective-permute-start(f32[64,512]{1,0:T(8,128)S(1)} %pad_maximum_fusion.1.mine_ref), channel_id=1, source_target_pairs={{0,32},{32,0},{64,96},{96,64},{128,160},{160,128},{192,224},{224,1... | collective-permute-start | bytes 393224 | tf_op jit(solution)/shard_map/ppermute | solution.py:331
  81.3 0.2 convolution_convert_fusion.1
  81.6 0.3 convolution_convert_fusion.2.left_ref
  81.9 2.0 %collective-permute-done.5.other_ref = f32[64,512]{1,0:T(8,128)S(1)} collective-permute-done((f32[64,512]{1,0:T(8,128)S(1)}, f32[64,512]{1,0:T(8,128)S(1)}, u32[]{:S(2)}, u32[]{:S(2)}) %collective-permute-start.5) | collective-permute-done | bytes 131104 | tf_op jit(solution)/shard_map/ppermute | solution.py:331
  83.9 1.1 %basis_part.1 = (f32[64,896]{1,0:T(8,128)}, bf16[64,896]{1,0:T(8,128)(2,1)S(1)}) custom-call(s32[1]{0:T(128)} %bitcast.11.row_ref, f32[64,64]{1,0:T(8,128)S(1)} %get-tuple-element.39.inverse_ref, f32[64,512]{1,0:T(8,128)S(1)} %pad_maximum_fusion.1.mine_ref, f32[64,512]{1,0:T(8,128)S(1)} %collective-permute-done.5.other_ref), custom_call_target="tpu_custom_call" | custom-call | tf_op jit(solution)/shard_map/basis_part/pallas_call | solution.py:259
  85.0 5.1 %add_subtract_fusion = f32[1024,896]{1,0:T(8,128)} fusion(f32[1024,896]{1,0:T(8,128)} %error_ref.1, bf16[1024,896]{1,0:T(8,128)(2,1)} %change_ref.1, bf16[64,1024]{1,0:T(8,128)(2,1)S(1)} %convolution_convert_fusion.1, bf16[64,896]{1,0:T(8,128)(2,1)S(1)} %get-tuple-element.41), kind=kOutput, calls=%fused_computation | convolution fusion | flops 120193024 | bytes 9420800 | tf_op jit(solution)/shard_map/dot_general | solution.py:43
  90.1 1.1 %all-to-all-done.3 = bf16[16,64,128]{2,1,0:T(8,128)(2,1)S(1)} async-done(((bf16[16,64,128]{2,1,0:T(8,128)(2,1)}), bf16[16,64,128]{2,1,0:T(8,128)(2,1)S(1)}, u32[]{:S(2)}, u32[]{:S(2)}) %all-to-all-start.3) | async-done | bytes 262176 | tf_op jit(solution)/shard_map/all_to_all | solution.py:54
  91.2 4.7 %collective-permute-start.6 = (bf16[16,64,128]{2,1,0:T(8,128)(2,1)S(1)}, bf16[16,64,128]{2,1,0:T(8,128)(2,1)S(1)}, u32[]{:S(2)}, u32[]{:S(2)}) collective-permute-start(bf16[16,64,128]{2,1,0:T(8,128)(2,1)S(1)} %all-to-all-done.3), channel_id=1, source_target_pairs={{0,1},{1,0},{2,3},{3,2},{4,5},{5,4},{6,7},{7,6},{8,9},{9,8},{10,11... | collective-permute-start | bytes 786440 | tf_op jit(solution)/shard_map/ppermute | solution.py:338
  95.9 0.7 dynamic-slice_bitcast_fusion.1.slots_ref
  96.5 0.5 collective-permute-done.6
  97.0 2.1 %rollout.1 = bf16[256,3584]{1,0:T(8,128)(2,1)} custom-call(s32[1]{0:T(128)} %bitcast.13.core_ref, s32[8]{0:T(128)S(1)} %dynamic-slice_bitcast_fusion.1.slots_ref, bf16[256,64]{1,0:T(8,128)(2,1)S(1)} %convolution_convert_fusion.2.left_ref, bf16[8,2,64,128]{3,2,1,0:T(8,128)(2,1)S(1)} %bitcast.36, bf16[8,2,64,128]{3,2,1,0:T(8,128)(2,1)S(1)} %bitcast.37, ...), custom_call_target="tpu_custom_call" | custom-call | tf_op jit(solution)/shard_map/rollout/pallas_call | solution.py:293
  (7 shorter events, 0.0 us)
Async XLA Ops:
  4.9 25.5 %all-to-all-start = ((f32[32,8,256]{2,1,0:T(8,128)}), f32[32,8,256]{2,1,0:T(8,128)S(1)}, u32[]{:S(2)}, u32[]{:S(2)}) async-start(f32[32,8,256]{2,1,0:T(8,128)} %bitcast.38), calls=%async_computation | async-start | bytes 524288 | tf_op jit(solution)/shard_map/all_to_all | solution.py:54
  31.2 17.1 %all-to-all-start.1 = ((f32[32,8,256]{2,1,0:T(8,128)}), f32[32,8,256]{2,1,0:T(8,128)S(1)}, u32[]{:S(2)}, u32[]{:S(2)}) async-start(f32[32,8,256]{2,1,0:T(8,128)} %sum_share.1), calls=%async_computation.1 | async-start | bytes 524288 | tf_op jit(solution)/shard_map/all_to_all | solution.py:54
  49.7 12.3 %all-to-all-start.2 = ((f32[8,96,128]{2,1,0:T(8,128)}), f32[8,96,128]{2,1,0:T(8,128)S(1)}, u32[]{:S(2)}, u32[]{:S(2)}) async-start(f32[8,96,128]{2,1,0:T(8,128)} %right_part.1), calls=%async_computation.2 | async-start | bytes 786432 | tf_op jit(solution)/shard_map/all_to_all | solution.py:54
  53.9 7.4 %collective-permute-start = (f32[64,256]{1,0:T(8,128)S(1)}, f32[64,256]{1,0:T(8,128)S(1)}, u32[]{:S(2)}, u32[]{:S(2)}) collective-permute-start(f32[64,256]{1,0:T(8,128)S(1)} %dynamic-slice_bitcast_fusion), channel_id=1, source_target_pairs={{16,0},{17,1},{18,2},{19,3},{12,32},{13,33},{14,34},{15,35},{20,64... | collective-permute-start | bytes 196616 | tf_op jit(solution)/shard_map/ppermute | solution.py:321
  62.0 12.3 %collective-permute-start.1 = (f32[64,128]{1,0:T(8,128)S(1)}, f32[64,128]{1,0:T(8,128)S(1)}, u32[]{:S(2)}, u32[]{:S(2)}) collective-permute-start(f32[64,128]{1,0:T(8,128)S(1)} %get-tuple-element.35), channel_id=1, source_target_pairs={{0,16},{1,17},{2,18},{3,19},{4,48},{5,49},{6,50},{7,51},{8,84},{9,... | collective-permute-start | bytes 98312 | tf_op jit(solution)/shard_map/ppermute | solution.py:324
  64.3 11.1 %collective-permute-start.4 = (f32[64,128]{1,0:T(8,128)S(1)}, f32[64,128]{1,0:T(8,128)S(1)}, u32[]{:S(2)}, u32[]{:S(2)}) collective-permute-start(f32[64,128]{1,0:T(8,128)S(1)} %get-tuple-element.35), channel_id=1, source_target_pairs={{0,192},{32,224},{64,0},{96,32},{128,64},{160,96},{192,128},{224,1... | collective-permute-start | bytes 98312 | tf_op jit(solution)/shard_map/ppermute | solution.py:325
  65.8 9.6 %collective-permute-start.3 = (f32[64,128]{1,0:T(8,128)S(1)}, f32[64,128]{1,0:T(8,128)S(1)}, u32[]{:S(2)}, u32[]{:S(2)}) collective-permute-start(f32[64,128]{1,0:T(8,128)S(1)} %get-tuple-element.35), channel_id=1, source_target_pairs={{0,128},{32,160},{64,192},{96,224},{128,0},{160,32},{192,64},{224,... | collective-permute-start | bytes 98312 | tf_op jit(solution)/shard_map/ppermute | solution.py:325
  72.4 4.0 %collective-permute-start.2 = (f32[64,128]{1,0:T(8,128)S(1)}, f32[64,128]{1,0:T(8,128)S(1)}, u32[]{:S(2)}, u32[]{:S(2)}) collective-permute-start(f32[64,128]{1,0:T(8,128)S(1)} %get-tuple-element.35), channel_id=1, source_target_pairs={{0,64},{32,96},{64,128},{96,160},{128,192},{160,224},{192,0},{224,... | collective-permute-start | bytes 98312 | tf_op jit(solution)/shard_map/ppermute | solution.py:325
  76.4 14.8 %all-to-all-start.3 = ((bf16[16,64,128]{2,1,0:T(8,128)(2,1)}), bf16[16,64,128]{2,1,0:T(8,128)(2,1)S(1)}, u32[]{:S(2)}, u32[]{:S(2)}) async-start(bf16[16,64,128]{2,1,0:T(8,128)(2,1)} %bitcast.8), calls=%async_computation.3 | async-start | bytes 524288 | tf_op jit(solution)/shard_map/all_to_all | solution.py:54
  80.0 3.9 %collective-permute-start.5 = (f32[64,512]{1,0:T(8,128)S(1)}, f32[64,512]{1,0:T(8,128)S(1)}, u32[]{:S(2)}, u32[]{:S(2)}) collective-permute-start(f32[64,512]{1,0:T(8,128)S(1)} %pad_maximum_fusion.1.mine_ref), channel_id=1, source_target_pairs={{0,32},{32,0},{64,96},{96,64},{128,160},{160,128},{192,224},{224,1... | collective-permute-start | bytes 393224 | tf_op jit(solution)/shard_map/ppermute | solution.py:331
  91.2 5.8 %collective-permute-start.6 = (bf16[16,64,128]{2,1,0:T(8,128)(2,1)S(1)}, bf16[16,64,128]{2,1,0:T(8,128)(2,1)S(1)}, u32[]{:S(2)}, u32[]{:S(2)}) collective-permute-start(bf16[16,64,128]{2,1,0:T(8,128)(2,1)S(1)} %all-to-all-done.3), channel_id=1, source_target_pairs={{0,1},{1,0},{2,3},{3,2},{4,5},{5,4},{6,7},{7,6},{8,9},{9,8},{10,11... | collective-permute-start | bytes 786440 | tf_op jit(solution)/shard_map/ppermute | solution.py:338

commit v6 on v5

--- a/solution.py
+++ b/solution.py
@@ -8,6 +8,7 @@
 HIGH = lax.Precision.HIGH
 HIGHEST = lax.Precision.HIGHEST
 ROWS, COLS, R, LANES, BLOCKS = 8, 32, 64, 128, 8
+GRAM_END = R + R // 2
 AXES = ("row", "col")
 
 
@@ -29,13 +30,12 @@
     for z in range(8)
     for q in range(4)
 ]
-FANOUT = [
-    (r * COLS + 4 * z + q, t * COLS + 4 * r + q)
-    for r in range(ROWS)
-    for t, z in partners(r).items()
-    for q in range(4)
+SWAP = [(r * COLS + 4 * z + q, z * COLS + 4 * r + q) for r in range(ROWS) for z in range(8) for q in range(4)]
+SAME_CORE = [
+    [row * COLS + 4 * SLOTS[row][b] + 2 * half + core for b in range(ROWS) for half in range(2)]
+    for row in range(ROWS)
+    for core in range(2)
 ]
-SAME_CORE = [[c for c in range(COLS) if c % 2 == core] for core in range(2)]
 PAIR = [(c, c ^ 1) for c in range(COLS)]
 
 
@@ -131,7 +131,7 @@
     )(parts)
 
 
-def right_kernel(total_ref, left_ref, out_ref):
+def right_kernel(total_ref, left_ref, rows_ref, out_ref):
     left = jnp.concatenate([left_ref[:, i].reshape(R, -1) for i in range(4)], 1)
     both = dot(jnp.concatenate(split(left), 0), total_ref[...], 1, 0)
     right = both[:R] + both[R:]
@@ -142,21 +142,23 @@
         out_ref[b, :R] = jnp.zeros((R, LANES), jnp.float32)
     gram = dot(left, left, 1, 1, HIGHEST)
     for b in range(BLOCKS):
-        out_ref[b, R:, :R] = gram[: R // 2]
-        out_ref[b, R:, R:] = gram[R // 2 :]
-
-
-def right_part(total, left):
+        out_ref[b, R : GRAM_END, :R] = gram[: R // 2]
+        out_ref[b, R : GRAM_END, R:] = gram[R // 2 :]
+        for i in range(rows_ref.shape[1] // LANES):
+            out_ref[b, GRAM_END + 8 * i : GRAM_END + 8 * i + 8] = rows_ref[:, i * LANES : (i + 1) * LANES]
+
+
+def right_part(total, left, some_rows):
     rows, units = total.shape
     return pl.pallas_call(
         right_kernel,
-        in_specs=[VMEM, VMEM],
+        in_specs=[VMEM, VMEM, VMEM],
         out_specs=VMEM,
-        out_shape=jax.ShapeDtypeStruct((BLOCKS, R + R // 2, LANES), jnp.float32),
+        out_shape=jax.ShapeDtypeStruct((BLOCKS, GRAM_END + some_rows.size // LANES, LANES), jnp.float32),
         compiler_params=grant(12),
         cost_estimate=pl.CostEstimate(flops=4 * rows * units * R, bytes_accessed=2 * rows * units, transcendentals=0),
         name="right_part",
-    )(total, left)
+    )(total, left, some_rows)
 
 
 def inverse_factor(gram):
@@ -195,49 +197,57 @@
     return jnp.concatenate(out, 0)
 
 
-def settle_kernel(parts_ref, block_ref, gram_ref):
-    got = parts_ref[0]
+def settle_kernel(parts_ref, block_ref, gram_ref, rows_ref):
+    got = parts_ref[0, :GRAM_END]
     for b in range(1, BLOCKS):
-        got = got + parts_ref[b]
+        got = got + parts_ref[b, :GRAM_END]
     block_ref[...] = got[:R]
     gram_ref[...] = got[R:]
+    for b in range(BLOCKS):
+        for i in range(rows_ref.shape[1] // LANES):
+            piece = parts_ref[b, GRAM_END + 8 * i : GRAM_END + 8 * i + 8]
+            rows_ref[8 * b : 8 * b + 8, i * LANES : (i + 1) * LANES] = piece
 
 
 def settle(parts):
+    width = (parts.shape[1] - GRAM_END) // 8 * LANES
     return pl.pallas_call(
         settle_kernel,
         in_specs=[VMEM],
-        out_specs=[VMEM, VMEM],
+        out_specs=[VMEM, VMEM, VMEM],
         out_shape=[
             jax.ShapeDtypeStruct((R, LANES), jnp.float32),
             jax.ShapeDtypeStruct((R // 2, LANES), jnp.float32),
+            jax.ShapeDtypeStruct((R, width), jnp.float32),
         ],
         compiler_params=grant(6),
         name="settle",
     )(parts)
 
 
-def factor_kernel(gram_ref, inverse_ref, copies_ref):
+def factor_kernel(gram_ref, block_ref, inverse_ref, copies_ref, same_ref):
     packed = gram_ref[...]
+    same_ref[...] = block_ref[...]
     inverse = inverse_factor(jnp.concatenate([packed[:, :R], packed[:, R:]], 0))
     inverse_ref[...] = inverse
     for b in range(copies_ref.shape[0] // R):
         copies_ref[b * R : (b + 1) * R] = inverse
 
 
-def factor(gram):
+def factor(gram, block):
     return pl.pallas_call(
         factor_kernel,
-        in_specs=[VMEM],
-        out_specs=[VMEM, VMEM],
+        in_specs=[VMEM, VMEM],
+        out_specs=[VMEM, VMEM, VMEM],
         out_shape=[
             jax.ShapeDtypeStruct((R, R), jnp.float32),
             jax.ShapeDtypeStruct((COLS // 2 * R, R), jnp.float32),
+            jax.ShapeDtypeStruct((R, LANES), jnp.float32),
         ],
         compiler_params=grant(6),
-        cost_estimate=pl.CostEstimate(flops=10**7, bytes_accessed=20 * 10**6, transcendentals=0),
+        cost_estimate=pl.CostEstimate(flops=1, bytes_accessed=1, transcendentals=0),
         name="factor",
-    )(gram)
+    )(gram, block)
 
 
 def basis_kernel(row_ref, inverse_ref, mine_ref, other_ref, basis_ref, round_ref):
@@ -269,16 +279,13 @@
     )(row, inverse, mine, other)
 
 
-def rollout_kernel(core_ref, slots_ref, left_ref, near_ref, other_ref, weight_ref, out_ref, buf, sem):
+def rollout_kernel(core_ref, left_ref, near_ref, other_ref, weight_ref, out_ref, buf, sem):
     even = core_ref[0] == 0
     width = buf.shape[2]
     copies = []
     for q in range(4):
         first, second = (near_ref, other_ref) if q % 2 == 0 else (other_ref, near_ref)
-        blocks = []
-        for b in range(width // LANES):
-            slot = slots_ref[b]
-            blocks.append(jnp.where(even, first[slot, q // 2], second[slot, q // 2]))
+        blocks = [jnp.where(even, first[b, q // 2], second[b, q // 2]) for b in range(width // LANES)]
         delta = dot(left_ref[...], jnp.concatenate(blocks, 1), 1, 0)
         buf[q] = (weight_ref[q].astype(jnp.float32) + delta).astype(jnp.bfloat16)
         copy = pltpu.make_async_copy(buf.at[q], out_ref.at[:, pl.ds(q * width, width)], sem.at[q])
@@ -288,11 +295,11 @@
         copy.wait()
 
 
-def rollout(core, slots, left, near, other, weight):
+def rollout(core, left, near, other, weight):
     quarters, rows, width = weight.shape
     return pl.pallas_call(
         rollout_kernel,
-        in_specs=[SMEM, SMEM, VMEM, VMEM, VMEM, VMEM],
+        in_specs=[SMEM, VMEM, VMEM, VMEM, VMEM],
         out_specs=ANY,
         out_shape=jax.ShapeDtypeStruct((rows, quarters * width), jnp.bfloat16),
         scratch_shapes=[
@@ -301,33 +308,32 @@
         ],
         compiler_params=grant(12),
         name="rollout",
-    )(core, slots, left, near, other, weight)
+    )(core, left, near, other, weight)
 
 
 def local(weight_change, error_buffer, basis, rollout_weight):
     row = lax.axis_index("row")
-    q = lax.axis_index("col") % 4
-    core = q % 2
+    core = lax.axis_index("col") % 2
     rows, units = weight_change.shape
     part = left_part(weight_change, error_buffer, basis.T)
     part, change, error = lax.optimization_barrier((part, weight_change, error_buffer))
     total = (change.astype(jnp.float32) + error).astype(jnp.bfloat16)
     parts = exchange(part.reshape(COLS, 8, rows // 4), "col")
     parts, total = lax.optimization_barrier((parts, total))
-    left = exchange(sum_share(parts), "col").reshape(8, 4, 8, rows // 4)
-    sums, weight = lax.optimization_barrier((right_part(total, left), rollout_weight))
+    chunks = sum_share(parts)
+    some_rows = lax.ppermute(chunks[0], AXES, SWAP)
+    left = exchange(chunks, "col").reshape(8, 4, 8, rows // 4)
+    sums, weight = lax.optimization_barrier((right_part(total, left, some_rows), rollout_weight))
     weight = jnp.stack([weight[:, i * units : (i + 1) * units] for i in range(4)])
-    mine = lax.dynamic_index_in_dim(left, q, 1, keepdims=False).reshape(R, rows // 4)
-    far_left = lax.ppermute(mine, AXES, FANOUT)
-    parts, weight, far_left = lax.optimization_barrier((exchange(sums, "row"), weight, far_left))
-    block, gram = settle(parts)
+    parts, weight = lax.optimization_barrier((exchange(sums, "row"), weight))
+    block, gram, far_left = settle(parts)
     far = lax.ppermute(block, AXES, SPREAD)
+    inverse, copies, block = factor(gram, block)
     blocks = [lax.ppermute(block, "row", [(r, (r + 2 * k) % ROWS) for r in range(ROWS)]) for k in (1, 2, 3)]
-    inverse, copies = factor(gram)
     far_round = dot(copies, far, 1, 0, HIGH).astype(jnp.bfloat16).reshape(COLS // 2, R, LANES)
+    far_round, inverse = lax.optimization_barrier((far_round, inverse))
+    near = exchange(far_round, AXES, SAME_CORE)
     blocks = jnp.concatenate([block] + blocks, 1)
-    far_round, inverse, blocks = lax.optimization_barrier((far_round, inverse, blocks))
-    near = exchange(far_round, "col", SAME_CORE)
     other_blocks = lax.ppermute(blocks, "row", [(r, r ^ 1) for r in range(ROWS)])
     left_rows = left.transpose(0, 2, 1, 3).reshape(R, rows)
     left_round = dot(inverse, left_rows, 1, 0, HIGH).astype(jnp.bfloat16)
@@ -337,9 +343,8 @@
     near, far_left, new_error = lax.optimization_barrier((near, far_left, new_error))
     other = lax.ppermute(near, "col", PAIR)
     halves = (BLOCKS, 2, R, LANES)
-    slots = jnp.asarray(SLOTS, jnp.int32)[row]
     core = core.astype(jnp.int32).reshape(1)
-    new_rollout = rollout(core, slots, far_left, near.reshape(halves), other.reshape(halves), weight)
+    new_rollout = rollout(core, far_left, near.reshape(halves), other.reshape(halves), weight)
     return (new_error, new_basis.T, new_rollout)
 
 

time: 99.6 us -> 97.8 us (0.982)
  starting transfers between devices: 44.9 us -> 39.8 us
  waiting for transfers between devices: 29.7 us -> 33.5 us
    ppermute x3, starting transfers between devices: 8.13 us -> 2.08 us  [local(): lax.ppermute(block, 'row', [(r, (r + 2 * k) % ROWS) for r in range(ROWS)])]
    all_to_all x4, starting transfers between devices: 24.5 us -> 30 us  [exchange(): return lax.all_to_all(parts, axis, 0, 0, axis_index_groups=groups)]
    all_to_all x4, waiting for transfers between devices: 24.7 us -> 28.5 us  [exchange(): return lax.all_to_all(parts, axis, 0, 0, axis_index_groups=groups)]
    ppermute x1, starting transfers between devices: 3.94 us -> 0.65 us  [local(): some_rows = lax.ppermute(chunks[0], AXES, SWAP)]
    ppermute x1, waiting for transfers between devices: 2.03 us -> 3.85 us  [local(): lax.ppermute(blocks, 'row', [(r, r ^ 1) for r in range(ROWS)])]
    ppermute x1, waiting for transfers between devices: 1.54 us -> 0.01 us  [local(): some_rows = lax.ppermute(chunks[0], AXES, SWAP)]
    ppermute x1, starting transfers between devices: 1.36 us -> 0.09 us  [local(): lax.ppermute(blocks, 'row', [(r, r ^ 1) for r in range(ROWS)])]
  transfers between devices with their start and end apart: 11 -> 11, of which waited for: 8 -> 5; matrix products, arithmetic and copies ran while one was open for 12% -> 13% of each run, Pallas kernels for 3% -> 3%
where the time goes in v6:
time: 97.8 us; the launch traced here: 97.3 us
  starting transfers between devices  39.8 us (41%)
  waiting for transfers between devices  33.5 us (34%)
  Pallas kernels  11 us (11%)
  matrix products  6.72 us (7%)
  other arithmetic  3.23 us (3%)
  local copies, waits for them, and re-layouts  2.31 us (2%)
    all_to_all x4, starting transfers between devices, exchange(): return lax.all_to_all(parts, axis, 0, 0, axis_index_groups=groups)  30 us
    all_to_all x4, waiting for transfers between devices, exchange(): return lax.all_to_all(parts, axis, 0, 0, axis_index_groups=groups)  28.5 us
    dot_general x4, matrix products, dot(): lax.dot_general(a, b, (((ca,), (cb,)), ((), ())), precision=precision, pr...  6.72 us
    ppermute x1, starting transfers between devices, local(): other = lax.ppermute(near, 'col', PAIR)  4.68 us
    pallas_call x1, Pallas kernels, left_part(): pl.pallas_call(left_kernel, in_specs=[ANY, ANY, ANY], out_specs=VMEM, out...  4.24 us
    ppermute x1, waiting for transfers between devices, local(): lax.ppermute(blocks, 'row', [(r, r ^ 1) for r in range(ROWS)])  3.85 us
    convert_element_type x1, other arithmetic, local(): total = (change.astype(jnp.float32) + error).astype(jnp.bfloat16)  2.95 us
    ppermute x1, starting transfers between devices, local(): far = lax.ppermute(block, AXES, SPREAD)  2.33 us
  transfers between devices with their start and end apart: 11, of which 5 were waited for; matrix products, arithmetic and copies ran while one was open for 13% of the time, Pallas kernels for 3%

profile of v6, /device:TPU:1, one launch (start us, length us, event | category | flops | bytes accessed | tf_op | source)
XLA Modules:
  0.0 97.3 jit_solution(17912425454931973303)
XLA Ops:
  0.6 4.2 %left_part.1 = f32[8,4,8,256]{3,2,1,0:T(8,128)} custom-call(bf16[1024,896]{1,0:T(8,128)(2,1)} %change_ref.1, f32[1024,896]{1,0:T(8,128)} %error_ref.1, f32[64,896]{1,0:T(8,128)} %bitcast.36), custom_call_target="tpu_custom_call" | custom-call | flops 352321536 | bytes 5505024 | tf_op jit(solution)/shard_map/left_part/pallas_call | solution.py:97
  4.9 12.6 %all-to-all-start = ((f32[32,8,256]{2,1,0:T(8,128)}), f32[32,8,256]{2,1,0:T(8,128)S(1)}, u32[]{:S(2)}, u32[]{:S(2)}) async-start(f32[32,8,256]{2,1,0:T(8,128)} %bitcast.35), calls=%async_computation | async-start | bytes 524288 | tf_op jit(solution)/shard_map/all_to_all | solution.py:54
  17.5 3.0 %add_convert_fusion.total_ref = bf16[1024,896]{1,0:T(8,128)(2,1)S(1)} fusion(f32[1024,896]{1,0:T(8,128)} %error_ref.1, bf16[1024,896]{1,0:T(8,128)(2,1)} %change_ref.1), kind=kLoop, calls=%fused_computation.1 | loop fusion | flops 2752512 | bytes 7340032 | tf_op jit(solution)/shard_map/convert_element_type | solution.py:320
  20.4 10.0 %all-to-all-done.parts_ref = f32[32,8,256]{2,1,0:T(8,128)S(1)} async-done(((f32[32,8,256]{2,1,0:T(8,128)}), f32[32,8,256]{2,1,0:T(8,128)S(1)}, u32[]{:S(2)}, u32[]{:S(2)}) %all-to-all-start) | async-done | bytes 262176 | tf_op jit(solution)/shard_map/all_to_all | solution.py:54
  30.4 0.8 sum_share.1
  31.2 4.1 %all-to-all-start.1 = ((f32[32,8,256]{2,1,0:T(8,128)}), f32[32,8,256]{2,1,0:T(8,128)S(1)}, u32[]{:S(2)}, u32[]{:S(2)}) async-start(f32[32,8,256]{2,1,0:T(8,128)} %sum_share.1), calls=%async_computation.1 | async-start | bytes 524288 | tf_op jit(solution)/shard_map/all_to_all | solution.py:54
  35.3 0.7 slice_bitcast_fusion.4
  36.0 0.6 collective-permute-start
  36.7 0.0 collective-permute-done.rows_ref
  36.7 11.6 %all-to-all-done.1 = f32[32,8,256]{2,1,0:T(8,128)S(1)} async-done(((f32[32,8,256]{2,1,0:T(8,128)}), f32[32,8,256]{2,1,0:T(8,128)S(1)}, u32[]{:S(2)}, u32[]{:S(2)}) %all-to-all-start.1) | async-done | bytes 262176 | tf_op jit(solution)/shard_map/all_to_all | solution.py:54
  48.3 1.5 %right_part.1 = f32[8,112,128]{2,1,0:T(8,128)} custom-call(bf16[1024,896]{1,0:T(8,128)(2,1)S(1)} %add_convert_fusion.total_ref, f32[8,4,8,256]{3,2,1,0:T(8,128)S(1)} %bitcast.31, f32[8,256]{1,0:T(8,128)S(1)} %collective-permute-done.rows_ref), custom_call_target="tpu_custom_call" | custom-call | flops 234881024 | bytes 1835008 | tf_op jit(solution)/shard_map/right_part/pallas_call | solution.py:153
  49.7 4.2 %all-to-all-start.2 = ((f32[8,112,128]{2,1,0:T(8,128)}), f32[8,112,128]{2,1,0:T(8,128)S(1)}, u32[]{:S(2)}, u32[]{:S(2)}) async-start(f32[8,112,128]{2,1,0:T(8,128)} %right_part.1), calls=%async_computation.2 | async-start | bytes 917504 | tf_op jit(solution)/shard_map/all_to_all | solution.py:54
  54.0 1.6 %slice_bitcast_fusion.3 = (bf16[1,256,896]{2,1,0:T(8,128)(2,1)S(1)}, bf16[1,256,896]{2,1,0:T(8,128)(2,1)S(1)}, bf16[1,256,896]{2,1,0:T(8,128)(2,1)S(1)}, bf16[1,256,896]{2,1,0:T(8,128)(2,1)S(1)}) fusion(bf16[256,3584]{1,0:T(8,128)(2,1)} %param.7), kind=kLoop, calls=%fused_computation.9 | loop fusion | bytes 3670016 | tf_op jit(solution)/shard_map/stack | solution.py:327
  55.5 0.3 pad_maximum_fusion.weight_ref
  55.8 6.9 %all-to-all-done.2.parts_ref = f32[8,112,128]{2,1,0:T(8,128)S(1)} async-done(((f32[8,112,128]{2,1,0:T(8,128)}), f32[8,112,128]{2,1,0:T(8,128)S(1)}, u32[]{:S(2)}, u32[]{:S(2)}) %all-to-all-start.2) | async-done | bytes 458784 | tf_op jit(solution)/shard_map/all_to_all | solution.py:54
  62.8 2.3 %collective-permute-start.1 = (f32[64,128]{1,0:T(8,128)S(1)}, f32[64,128]{1,0:T(8,128)S(1)}, u32[]{:S(2)}, u32[]{:S(2)}) collective-permute-start(f32[64,128]{1,0:T(8,128)S(1)} %get-tuple-element.34.block_ref), channel_id=1, source_target_pairs={{0,16},{1,17},{2,18},{3,19},{4,48},{5,49},{6,50},{7,51},{8,84},{9,... | collective-permute-start | bytes 98312 | tf_op jit(solution)/shard_map/ppermute | solution.py:330
  65.1 1.9 %factor.1 = (f32[64,64]{1,0:T(8,128)S(1)}, f32[1024,64]{1,0:T(8,128)S(1)}, f32[64,128]{1,0:T(8,128)S(1)}) custom-call(f32[32,128]{1,0:T(8,128)S(1)} %get-tuple-element.33.gram_ref, f32[64,128]{1,0:T(8,128)S(1)} %get-tuple-element.34.block_ref), custom_call_target="tpu_custom_call" | custom-call | flops 1 | bytes 1 | tf_op jit(solution)/shard_map/factor/pallas_call | solution.py:238
  67.0 0.7 collective-permute-start.4
  67.7 1.4 %collective-permute-start.3 = (f32[64,128]{1,0:T(8,128)S(1)}, f32[64,128]{1,0:T(8,128)S(1)}, u32[]{:S(2)}, u32[]{:S(2)}) collective-permute-start(f32[64,128]{1,0:T(8,128)S(1)} %get-tuple-element.40), channel_id=1, source_target_pairs={{0,128},{32,160},{64,192},{96,224},{128,0},{160,32},{192,64},{224,... | collective-permute-start | bytes 98312 | tf_op jit(solution)/shard_map/ppermute | solution.py:332
  69.1 0.0 collective-permute-start.2
  69.1 0.0 collective-permute-done.1
  69.1 1.1 %convolution_convert_fusion = bf16[1024,128]{1,0:T(8,128)(2,1)} fusion(f32[1024,64]{1,0:T(8,128)S(1)} %get-tuple-element.35, f32[64,128]{1,0:T(8,128)S(1)} %collective-permute-done.1), kind=kOutput, calls=%fused_computation.3 | convolution fusion | flops 50462720 | bytes 557056 | tf_op jit(solution)/shard_map/dot_general | solution.py:43
  70.2 9.0 %all-to-all-start.3 = ((bf16[16,64,128]{2,1,0:T(8,128)(2,1)}), bf16[16,64,128]{2,1,0:T(8,128)(2,1)S(1)}, u32[]{:S(2)}, u32[]{:S(2)}) async-start(bf16[16,64,128]{2,1,0:T(8,128)(2,1)} %bitcast.8), calls=%async_computation.3 | async-start | bytes 524288 | tf_op jit(solution)/shard_map/all_to_all | solution.py:54
  79.3 0.1 collective-permute-start.5
  79.4 0.2 convolution_convert_fusion.1
  79.6 0.3 convolution_convert_fusion.2.left_ref
  79.9 3.8 %collective-permute-done.5.other_ref = f32[64,512]{1,0:T(8,128)S(1)} collective-permute-done((f32[64,512]{1,0:T(8,128)S(1)}, f32[64,512]{1,0:T(8,128)S(1)}, u32[]{:S(2)}, u32[]{:S(2)}) %collective-permute-start.5) | collective-permute-done | bytes 131104 | tf_op jit(solution)/shard_map/ppermute | solution.py:337
  83.8 1.1 %basis_part.1 = (f32[64,896]{1,0:T(8,128)}, bf16[64,896]{1,0:T(8,128)(2,1)S(1)}) custom-call(s32[1]{0:T(128)} %bitcast.11.row_ref, f32[64,64]{1,0:T(8,128)S(1)} %get-tuple-element.39.inverse_ref, f32[64,512]{1,0:T(8,128)S(1)} %constant_dynamic-update-slice_fusion.mine_ref, f32[64,512]{1,0:T(8,128)S(1)} %collective-permute-done.5.other_ref), custom_call_target="tpu_custom_call" | custom-call | tf_op jit(solution)/shard_map/basis_part/pallas_call | solution.py:269
  84.8 5.1 %add_subtract_fusion = f32[1024,896]{1,0:T(8,128)} fusion(f32[1024,896]{1,0:T(8,128)} %error_ref.1, bf16[1024,896]{1,0:T(8,128)(2,1)} %change_ref.1, bf16[64,1024]{1,0:T(8,128)(2,1)S(1)} %convolution_convert_fusion.1, bf16[64,896]{1,0:T(8,128)(2,1)S(1)} %get-tuple-element.41), kind=kOutput, calls=%fused_computation | convolution fusion | flops 120193024 | bytes 9420800 | tf_op jit(solution)/shard_map/dot_general | solution.py:43
  90.0 4.7 %collective-permute-start.6 = (bf16[16,64,128]{2,1,0:T(8,128)(2,1)S(1)}, bf16[16,64,128]{2,1,0:T(8,128)(2,1)S(1)}, u32[]{:S(2)}, u32[]{:S(2)}) collective-permute-start(bf16[16,64,128]{2,1,0:T(8,128)(2,1)S(1)} %all-to-all-done.3), channel_id=1, source_target_pairs={{0,1},{1,0},{2,3},{3,2},{4,5},{5,4},{6,7},{7,6},{8,9},{9,8},{10,11... | collective-permute-start | bytes 786440 | tf_op jit(solution)/shard_map/ppermute | solution.py:344
  94.6 1.2 %collective-permute-done.6 = bf16[16,64,128]{2,1,0:T(8,128)(2,1)S(1)} collective-permute-done((bf16[16,64,128]{2,1,0:T(8,128)(2,1)S(1)}, bf16[16,64,128]{2,1,0:T(8,128)(2,1)S(1)}, u32[]{:S(2)}, u32[]{:S(2)}) %collective-permute-start.6) | collective-permute-done | bytes 262176 | tf_op jit(solution)/shard_map/ppermute | solution.py:344
  95.8 1.5 %rollout.1 = bf16[256,3584]{1,0:T(8,128)(2,1)} custom-call(s32[1]{0:T(128)} %bitcast.13.core_ref, bf16[256,64]{1,0:T(8,128)(2,1)S(1)} %convolution_convert_fusion.2.left_ref, bf16[8,2,64,128]{3,2,1,0:T(8,128)(2,1)S(1)} %bitcast.33, bf16[8,2,64,128]{3,2,1,0:T(8,128)(2,1)S(1)} %bitcast.34, bf16[4,256,896]{2,1,0:T(8,128)(2,1)S(1)} %pad_maximum_fusion.weight_ref), custom_call_target="tpu_custom_call" | custom-call | tf_op jit(solution)/shard_map/rollout/pallas_call | solution.py:300
  (9 shorter events, 0.1 us)
Async XLA Ops:
  4.9 25.5 %all-to-all-start = ((f32[32,8,256]{2,1,0:T(8,128)}), f32[32,8,256]{2,1,0:T(8,128)S(1)}, u32[]{:S(2)}, u32[]{:S(2)}) async-start(f32[32,8,256]{2,1,0:T(8,128)} %bitcast.35), calls=%async_computation | async-start | bytes 524288 | tf_op jit(solution)/shard_map/all_to_all | solution.py:54
  31.2 17.1 %all-to-all-start.1 = ((f32[32,8,256]{2,1,0:T(8,128)}), f32[32,8,256]{2,1,0:T(8,128)S(1)}, u32[]{:S(2)}, u32[]{:S(2)}) async-start(f32[32,8,256]{2,1,0:T(8,128)} %sum_share.1), calls=%async_computation.1 | async-start | bytes 524288 | tf_op jit(solution)/shard_map/all_to_all | solution.py:54
  36.0 0.7 collective-permute-start
  49.7 13.0 %all-to-all-start.2 = ((f32[8,112,128]{2,1,0:T(8,128)}), f32[8,112,128]{2,1,0:T(8,128)S(1)}, u32[]{:S(2)}, u32[]{:S(2)}) async-start(f32[8,112,128]{2,1,0:T(8,128)} %right_part.1), calls=%async_computation.2 | async-start | bytes 917504 | tf_op jit(solution)/shard_map/all_to_all | solution.py:54
  62.8 6.3 %collective-permute-start.1 = (f32[64,128]{1,0:T(8,128)S(1)}, f32[64,128]{1,0:T(8,128)S(1)}, u32[]{:S(2)}, u32[]{:S(2)}) collective-permute-start(f32[64,128]{1,0:T(8,128)S(1)} %get-tuple-element.34.block_ref), channel_id=1, source_target_pairs={{0,16},{1,17},{2,18},{3,19},{4,48},{5,49},{6,50},{7,51},{8,84},{9,... | collective-permute-start | bytes 98312 | tf_op jit(solution)/shard_map/ppermute | solution.py:330
  67.0 12.2 %collective-permute-start.4 = (f32[64,128]{1,0:T(8,128)S(1)}, f32[64,128]{1,0:T(8,128)S(1)}, u32[]{:S(2)}, u32[]{:S(2)}) collective-permute-start(f32[64,128]{1,0:T(8,128)S(1)} %get-tuple-element.40), channel_id=1, source_target_pairs={{0,192},{32,224},{64,0},{96,32},{128,64},{160,96},{192,128},{224,1... | collective-permute-start | bytes 98312 | tf_op jit(solution)/shard_map/ppermute | solution.py:332
  67.7 11.5 %collective-permute-start.3 = (f32[64,128]{1,0:T(8,128)S(1)}, f32[64,128]{1,0:T(8,128)S(1)}, u32[]{:S(2)}, u32[]{:S(2)}) collective-permute-start(f32[64,128]{1,0:T(8,128)S(1)} %get-tuple-element.40), channel_id=1, source_target_pairs={{0,128},{32,160},{64,192},{96,224},{128,0},{160,32},{192,64},{224,... | collective-permute-start | bytes 98312 | tf_op jit(solution)/shard_map/ppermute | solution.py:332
  69.1 10.1 %collective-permute-start.2 = (f32[64,128]{1,0:T(8,128)S(1)}, f32[64,128]{1,0:T(8,128)S(1)}, u32[]{:S(2)}, u32[]{:S(2)}) collective-permute-start(f32[64,128]{1,0:T(8,128)S(1)} %get-tuple-element.40), channel_id=1, source_target_pairs={{0,64},{32,96},{64,128},{96,160},{128,192},{160,224},{192,0},{224,... | collective-permute-start | bytes 98312 | tf_op jit(solution)/shard_map/ppermute | solution.py:332
  70.2 19.8 %all-to-all-start.3 = ((bf16[16,64,128]{2,1,0:T(8,128)(2,1)}), bf16[16,64,128]{2,1,0:T(8,128)(2,1)S(1)}, u32[]{:S(2)}, u32[]{:S(2)}) async-start(bf16[16,64,128]{2,1,0:T(8,128)(2,1)} %bitcast.8), calls=%async_computation.3 | async-start | bytes 524288 | tf_op jit(solution)/shard_map/all_to_all | solution.py:54
  79.3 4.5 %collective-permute-start.5 = (f32[64,512]{1,0:T(8,128)S(1)}, f32[64,512]{1,0:T(8,128)S(1)}, u32[]{:S(2)}, u32[]{:S(2)}) collective-permute-start(f32[64,512]{1,0:T(8,128)S(1)} %constant_dynamic-update-slice_fusion.mine_ref), channel_id=1, source_target_pairs={{0,32},{32,0},{64,96},{96,64},{128,160},{160,128},{192,224},{224,1... | collective-permute-start | bytes 393224 | tf_op jit(solution)/shard_map/ppermute | solution.py:337
  90.0 5.8 %collective-permute-start.6 = (bf16[16,64,128]{2,1,0:T(8,128)(2,1)S(1)}, bf16[16,64,128]{2,1,0:T(8,128)(2,1)S(1)}, u32[]{:S(2)}, u32[]{:S(2)}) collective-permute-start(bf16[16,64,128]{2,1,0:T(8,128)(2,1)S(1)} %all-to-all-done.3), channel_id=1, source_target_pairs={{0,1},{1,0},{2,3},{3,2},{4,5},{5,4},{6,7},{7,6},{8,9},{9,8},{10,11... | collective-permute-start | bytes 786440 | tf_op jit(solution)/shard_map/ppermute | solution.py:344

commit v7 on v6

--- a/solution.py
+++ b/solution.py
@@ -225,50 +225,47 @@
     )(parts)
 
 
-def factor_kernel(gram_ref, block_ref, inverse_ref, copies_ref, same_ref):
+def factor_kernel(gram_ref, inverse_ref, copies_ref):
     packed = gram_ref[...]
-    same_ref[...] = block_ref[...]
     inverse = inverse_factor(jnp.concatenate([packed[:, :R], packed[:, R:]], 0))
     inverse_ref[...] = inverse
     for b in range(copies_ref.shape[0] // R):
         copies_ref[b * R : (b + 1) * R] = inverse
 
 
-def factor(gram, block):
+def factor(gram):
     return pl.pallas_call(
         factor_kernel,
-        in_specs=[VMEM, VMEM],
-        out_specs=[VMEM, VMEM, VMEM],
+        in_specs=[VMEM],
+        out_specs=[VMEM, VMEM],
         out_shape=[
             jax.ShapeDtypeStruct((R, R), jnp.float32),
             jax.ShapeDtypeStruct((COLS // 2 * R, R), jnp.float32),
-            jax.ShapeDtypeStruct((R, LANES), jnp.float32),
         ],
         compiler_params=grant(6),
         cost_estimate=pl.CostEstimate(flops=1, bytes_accessed=1, transcendentals=0),
         name="factor",
-    )(gram, block)
-
-
-def basis_kernel(row_ref, inverse_ref, mine_ref, other_ref, basis_ref, round_ref):
-    y, odd = row_ref[0] // 2, row_ref[0] % 2
+    )(gram)
+
+
+def basis_kernel(row_ref, inverse_ref, pair0_ref, pair1_ref, pair2_ref, pair3_ref, basis_ref, round_ref):
+    y = row_ref[0] // 2
     blocks = []
     for b in range(basis_ref.shape[1] // LANES):
-        value = jnp.zeros((R, LANES), jnp.float32)
-        for k in range(4):
-            lanes = slice(k * LANES, (k + 1) * LANES)
-            picked = jnp.where(odd == b % 2, mine_ref[:, lanes], other_ref[:, lanes])
-            value = jnp.where((y + 4 - k) % 4 == b // 2, picked, value)
+        lanes = slice(b % 2 * LANES, (b % 2 + 1) * LANES)
+        value = pair0_ref[:, lanes]
+        for k, ref in enumerate((pair1_ref, pair2_ref, pair3_ref), 1):
+            value = jnp.where((y + 4 - k) % 4 == b // 2, ref[:, lanes], value)
         blocks.append(value)
     basis = dot(inverse_ref[...], jnp.concatenate(blocks, 1), 1, 0, HIGHEST)
     basis_ref[...] = basis
     round_ref[...] = basis.astype(jnp.bfloat16)
 
 
-def basis_part(row, inverse, mine, other, units):
+def basis_part(row, inverse, pairs, units):
     return pl.pallas_call(
         basis_kernel,
-        in_specs=[SMEM] + [VMEM] * 3,
+        in_specs=[SMEM] + [VMEM] * 5,
         out_specs=[VMEM, VMEM],
         out_shape=[
             jax.ShapeDtypeStruct((R, units), jnp.float32),
@@ -276,7 +273,7 @@
         ],
         compiler_params=grant(6),
         name="basis_part",
-    )(row, inverse, mine, other)
+    )(row, inverse, *pairs)
 
 
 def rollout_kernel(core_ref, left_ref, near_ref, other_ref, weight_ref, out_ref, buf, sem):
@@ -323,24 +320,24 @@
     chunks = sum_share(parts)
     some_rows = lax.ppermute(chunks[0], AXES, SWAP)
     left = exchange(chunks, "col").reshape(8, 4, 8, rows // 4)
-    sums, weight = lax.optimization_barrier((right_part(total, left, some_rows), rollout_weight))
-    weight = jnp.stack([weight[:, i * units : (i + 1) * units] for i in range(4)])
-    parts, weight = lax.optimization_barrier((exchange(sums, "row"), weight))
+    parts = exchange(right_part(total, left, some_rows), "row")
     block, gram, far_left = settle(parts)
     far = lax.ppermute(block, AXES, SPREAD)
-    inverse, copies, block = factor(gram, block)
-    blocks = [lax.ppermute(block, "row", [(r, (r + 2 * k) % ROWS) for r in range(ROWS)]) for k in (1, 2, 3)]
+    other_block = lax.ppermute(block, "row", [(r, r ^ 1) for r in range(ROWS)])
+    inverse, copies = factor(gram)
+    odd = row % 2 == 1
+    pair = jnp.concatenate([jnp.where(odd, other_block, block), jnp.where(odd, block, other_block)], 1)
+    pairs = [lax.ppermute(pair, "row", [(r, (r + 2 * k) % ROWS) for r in range(ROWS)]) for k in (1, 2, 3)]
     far_round = dot(copies, far, 1, 0, HIGH).astype(jnp.bfloat16).reshape(COLS // 2, R, LANES)
-    far_round, inverse = lax.optimization_barrier((far_round, inverse))
+    far_round, inverse, weight = lax.optimization_barrier((far_round, inverse, rollout_weight))
     near = exchange(far_round, AXES, SAME_CORE)
-    blocks = jnp.concatenate([block] + blocks, 1)
-    other_blocks = lax.ppermute(blocks, "row", [(r, r ^ 1) for r in range(ROWS)])
+    weight = jnp.stack([weight[:, i * units : (i + 1) * units] for i in range(4)])
     left_rows = left.transpose(0, 2, 1, 3).reshape(R, rows)
     left_round = dot(inverse, left_rows, 1, 0, HIGH).astype(jnp.bfloat16)
     far_left = dot(far_left, inverse, 0, 1, HIGH).astype(jnp.bfloat16)
-    new_basis, right_round = basis_part(row.astype(jnp.int32).reshape(1), inverse, blocks, other_blocks, units)
+    new_basis, right_round = basis_part(row.astype(jnp.int32).reshape(1), inverse, [pair] + pairs, units)
     new_error = weight_change.astype(jnp.float32) + error_buffer - dot(left_round, right_round, 0, 0)
-    near, far_left, new_error = lax.optimization_barrier((near, far_left, new_error))
+    near, far_left, new_error, weight = lax.optimization_barrier((near, far_left, new_error, weight))
     other = lax.ppermute(near, "col", PAIR)
     halves = (BLOCKS, 2, R, LANES)
     core = core.astype(jnp.int32).reshape(1)

time: 97.8 us -> 94.4 us (0.965); the launches traced: 97.3 us -> 92.7 us
  blocking collectives: 0 us -> 12.8 us
  waiting for transfers between devices: 33.5 us -> 22.7 us
  starting transfers between devices: 39.8 us -> 35.5 us
  matrix products: 6.72 us -> 4.11 us
    all_to_all x0 -> x1, blocking collectives: none -> 12.8 us  [exchange(): return lax.all_to_all(parts, axis, 0, 0, axis_index_groups=groups)]
    all_to_all x4 -> x3, waiting for transfers between devices: 28.5 us -> 21.5 us  [exchange(): return lax.all_to_all(parts, axis, 0, 0, axis_index_groups=groups)]
    all_to_all x4 -> x3, starting transfers between devices: 30 us -> 24.7 us  [exchange(): return lax.all_to_all(parts, axis, 0, 0, axis_index_groups=groups)]
    ppermute x4, waiting for transfers between devices: 3.86 us -> 0.01 us  [the longest x3 0.01 us: local(): lax.ppermute(pair, 'row', [(r, (r + 2 * k) % ROWS) for r in range(ROWS)])]
    dot_general x4, matrix products: 6.72 us -> 4.11 us  [dot(): lax.dot_general(a, b, (((ca,), (cb,)), ((), ())), precision=precision, pr...]
    ppermute x4, starting transfers between devices: 2.17 us -> 4 us  [the longest x3 3.22 us: local(): lax.ppermute(pair, 'row', [(r, (r + 2 * k) % ROWS) for r in range(ROWS)])]
    ppermute x1, starting transfers between devices: 2.33 us -> 0.88 us  [local(): far = lax.ppermute(block, AXES, SPREAD)]
  transfers between devices with their start and end apart: 11 -> 10, of which waited for: 5 -> 3; matrix products, arithmetic and copies ran while one was open for 13% -> 11% of each run, Pallas kernels for 3% -> 3%
where the time goes in v7:
time: 94.4 us; the launch traced here: 92.7 us
  starting transfers between devices  35.5 us (38%)
  waiting for transfers between devices  22.7 us (24%)
  blocking collectives  12.8 us (14%)
  Pallas kernels  10.2 us (11%)
  matrix products  4.11 us (4%)
  other arithmetic  3.26 us (3%)
  local copies, waits for them, and re-layouts  3.26 us (3%)
    all_to_all x3, starting transfers between devices, exchange(): return lax.all_to_all(parts, axis, 0, 0, axis_index_groups=groups)  24.7 us
    all_to_all x3, waiting for transfers between devices, exchange(): return lax.all_to_all(parts, axis, 0, 0, axis_index_groups=groups)  21.5 us
    all_to_all x1, blocking collectives, exchange(): return lax.all_to_all(parts, axis, 0, 0, axis_index_groups=groups)  12.8 us
    ppermute x1, starting transfers between devices, local(): other = lax.ppermute(near, 'col', PAIR)  5.3 us
    pallas_call x1, Pallas kernels, left_part(): pl.pallas_call(left_kernel, in_specs=[ANY, ANY, ANY], out_specs=VMEM, out...  4.24 us
    dot_general x4, matrix products, dot(): lax.dot_general(a, b, (((ca,), (cb,)), ((), ())), precision=precision, pr...  4.11 us
    ppermute x3, starting transfers between devices, local(): lax.ppermute(pair, 'row', [(r, (r + 2 * k) % ROWS) for r in range(ROWS)])  3.22 us
    convert_element_type x1, other arithmetic, local(): total = (change.astype(jnp.float32) + error).astype(jnp.bfloat16)  2.95 us
  transfers between devices with their start and end apart: 10, of which 3 were waited for; matrix products, arithmetic and copies ran while one was open for 11% of the time, Pallas kernels for 3%

profile of v7, /device:TPU:1, one launch (start us, length us, event | category | flops | bytes accessed | tf_op | source)
XLA Modules:
  0.0 92.7 jit_solution(168883611187994771)
XLA Ops:
  0.6 4.2 %left_part.1 = f32[8,4,8,256]{3,2,1,0:T(8,128)} custom-call(bf16[1024,896]{1,0:T(8,128)(2,1)} %change_ref.1, f32[1024,896]{1,0:T(8,128)} %error_ref.1, f32[64,896]{1,0:T(8,128)} %bitcast.36), custom_call_target="tpu_custom_call" | custom-call | flops 352321536 | bytes 5505024 | tf_op jit(solution)/shard_map/left_part/pallas_call | solution.py:97
  4.9 12.6 %all-to-all-start = ((f32[32,8,256]{2,1,0:T(8,128)}), f32[32,8,256]{2,1,0:T(8,128)S(1)}, u32[]{:S(2)}, u32[]{:S(2)}) async-start(f32[32,8,256]{2,1,0:T(8,128)} %bitcast.35), calls=%async_computation | async-start | bytes 524288 | tf_op jit(solution)/shard_map/all_to_all | solution.py:54
  17.5 3.0 %add_convert_fusion.total_ref = bf16[1024,896]{1,0:T(8,128)(2,1)S(1)} fusion(f32[1024,896]{1,0:T(8,128)} %error_ref.1, bf16[1024,896]{1,0:T(8,128)(2,1)} %change_ref.1), kind=kLoop, calls=%fused_computation.1 | loop fusion | flops 2752512 | bytes 7340032 | tf_op jit(solution)/shard_map/convert_element_type | solution.py:317
  20.4 10.0 %all-to-all-done.parts_ref = f32[32,8,256]{2,1,0:T(8,128)S(1)} async-done(((f32[32,8,256]{2,1,0:T(8,128)}), f32[32,8,256]{2,1,0:T(8,128)S(1)}, u32[]{:S(2)}, u32[]{:S(2)}) %all-to-all-start) | async-done | bytes 262176 | tf_op jit(solution)/shard_map/all_to_all | solution.py:54
  30.4 0.8 sum_share.1
  31.2 4.1 %all-to-all-start.1 = ((f32[32,8,256]{2,1,0:T(8,128)}), f32[32,8,256]{2,1,0:T(8,128)S(1)}, u32[]{:S(2)}, u32[]{:S(2)}) async-start(f32[32,8,256]{2,1,0:T(8,128)} %sum_share.1), calls=%async_computation.1 | async-start | bytes 524288 | tf_op jit(solution)/shard_map/all_to_all | solution.py:54
  35.3 0.7 slice_bitcast_fusion.4
  36.0 0.6 collective-permute-start
  36.7 0.0 collective-permute-done.rows_ref
  36.7 11.6 %all-to-all-done.1 = f32[32,8,256]{2,1,0:T(8,128)S(1)} async-done(((f32[32,8,256]{2,1,0:T(8,128)}), f32[32,8,256]{2,1,0:T(8,128)S(1)}, u32[]{:S(2)}, u32[]{:S(2)}) %all-to-all-start.1) | async-done | bytes 262176 | tf_op jit(solution)/shard_map/all_to_all | solution.py:54
  48.2 0.7 right_part.1
  49.0 12.8 %all_to_all.20.parts_ref = f32[8,112,128]{2,1,0:T(8,128)S(1)} all-to-all(f32[8,112,128]{2,1,0:T(8,128)S(1)} %right_part.1), channel_id=1, replica_groups=mesh['row'=8,'col'=32] {'row'}, dimensions={0} | all-to-all | bytes 917504 | tf_op jit(solution)/shard_map/all_to_all | solution.py:54
  61.8 0.8 collective-permute-start.2
  62.6 0.9 collective-permute-start.1
  63.5 1.9 %factor.1 = (f32[64,64]{1,0:T(8,128)S(1)}, f32[1024,64]{1,0:T(8,128)S(1)}) custom-call(f32[32,128]{1,0:T(8,128)S(1)} %get-tuple-element.27.gram_ref), custom_call_target="tpu_custom_call" | custom-call | flops 1 | bytes 1 | tf_op jit(solution)/shard_map/factor/pallas_call | solution.py:237
  65.4 1.6 %collective-permute-start.5 = (f32[64,256]{1,0:T(8,128)S(1)}, f32[64,256]{1,0:T(8,128)S(1)}, u32[]{:S(2)}, u32[]{:S(2)}) collective-permute-start(f32[64,256]{1,0:T(8,128)S(1)} %pad_maximum_fusion.1.pair0_ref), channel_id=1, source_target_pairs={{0,192},{32,224},{64,0},{96,32},{128,64},{160,96},{192,128},{224,1... | collective-permute-start | bytes 196616 | tf_op jit(solution)/shard_map/ppermute | solution.py:330
  67.0 1.6 %collective-permute-start.4 = (f32[64,256]{1,0:T(8,128)S(1)}, f32[64,256]{1,0:T(8,128)S(1)}, u32[]{:S(2)}, u32[]{:S(2)}) collective-permute-start(f32[64,256]{1,0:T(8,128)S(1)} %pad_maximum_fusion.1.pair0_ref), channel_id=1, source_target_pairs={{0,128},{32,160},{64,192},{96,224},{128,0},{160,32},{192,64},{224,... | collective-permute-start | bytes 196616 | tf_op jit(solution)/shard_map/ppermute | solution.py:330
  68.7 0.0 collective-permute-start.3
  68.7 1.1 %convolution_convert_fusion = bf16[1024,128]{1,0:T(8,128)(2,1)} fusion(f32[1024,64]{1,0:T(8,128)S(1)} %get-tuple-element.28, f32[64,128]{1,0:T(8,128)S(1)} %collective-permute-done.1), kind=kOutput, calls=%fused_computation.3 | convolution fusion | flops 50462720 | bytes 557056 | tf_op jit(solution)/shard_map/dot_general | solution.py:43
  69.7 0.2 convolution_convert_fusion.1
  70.0 0.3 convolution_convert_fusion.2.left_ref
  70.3 8.0 %all-to-all-start.3 = ((bf16[16,64,128]{2,1,0:T(8,128)(2,1)}), bf16[16,64,128]{2,1,0:T(8,128)(2,1)S(1)}, u32[]{:S(2)}, u32[]{:S(2)}) async-start(bf16[16,64,128]{2,1,0:T(8,128)(2,1)} %bitcast.4), calls=%async_computation.3 | async-start | bytes 524288 | tf_op jit(solution)/shard_map/all_to_all | solution.py:54
  78.3 1.7 %slice_bitcast_fusion.3 = (bf16[1,256,896]{2,1,0:T(8,128)(2,1)S(1)}, bf16[1,256,896]{2,1,0:T(8,128)(2,1)S(1)}, bf16[1,256,896]{2,1,0:T(8,128)(2,1)S(1)}, bf16[1,256,896]{2,1,0:T(8,128)(2,1)S(1)}) fusion(bf16[256,3584]{1,0:T(8,128)(2,1)} %param.7), kind=kLoop, calls=%fused_computation.9 | loop fusion | bytes 3670016 | tf_op jit(solution)/shard_map/stack | solution.py:334
  80.0 0.0 copy-start
  80.0 0.3 pad_maximum_fusion.weight_ref
  80.3 0.0 collective-permute-done.4.pair2_ref
  80.3 1.0 %basis_part.1 = (f32[64,896]{1,0:T(8,128)}, bf16[64,896]{1,0:T(8,128)(2,1)S(1)}) custom-call(s32[1]{0:T(128)} %bitcast.7.row_ref, f32[64,64]{1,0:T(8,128)S(1)} %get-tuple-element.33.inverse_ref, f32[64,256]{1,0:T(8,128)S(1)} %pad_maximum_fusion.1.pair0_ref, f32[64,256]{1,0:T(8,128)S(1)} %collective-permute-done.3.pair1_ref, ...), custom_call_target="tpu_custom_call" | custom-call | tf_op jit(solution)/shard_map/basis_part/pallas_call | solution.py:266
  81.4 0.8 copy-done
  82.2 2.5 %add_subtract_fusion = f32[1024,896]{1,0:T(8,128)} fusion(f32[1024,896]{1,0:T(8,128)S(1)} %copy-done, bf16[1024,896]{1,0:T(8,128)(2,1)S(1)} %copy-done.1, bf16[64,1024]{1,0:T(8,128)(2,1)S(1)} %convolution_convert_fusion.1, bf16[64,896]{1,0:T(8,128)(2,1)S(1)} %get-tuple-element.34), kind=kOutput, calls=%fused_computation | convolution fusion | flops 120193024 | bytes 9420800 | tf_op jit(solution)/shard_map/dot_general | solution.py:43
  84.7 5.3 %collective-permute-start.6 = (bf16[16,64,128]{2,1,0:T(8,128)(2,1)S(1)}, bf16[16,64,128]{2,1,0:T(8,128)(2,1)S(1)}, u32[]{:S(2)}, u32[]{:S(2)}) collective-permute-start(bf16[16,64,128]{2,1,0:T(8,128)(2,1)S(1)} %all-to-all-done.3), channel_id=1, source_target_pairs={{0,1},{1,0},{2,3},{3,2},{4,5},{5,4},{6,7},{7,6},{8,9},{9,8},{10,11... | collective-permute-start | bytes 786440 | tf_op jit(solution)/shard_map/ppermute | solution.py:341
  90.0 1.2 %collective-permute-done.6 = bf16[16,64,128]{2,1,0:T(8,128)(2,1)S(1)} collective-permute-done((bf16[16,64,128]{2,1,0:T(8,128)(2,1)S(1)}, bf16[16,64,128]{2,1,0:T(8,128)(2,1)S(1)}, u32[]{:S(2)}, u32[]{:S(2)}) %collective-permute-start.6) | collective-permute-done | bytes 262176 | tf_op jit(solution)/shard_map/ppermute | solution.py:341
  91.2 1.5 %rollout.1 = bf16[256,3584]{1,0:T(8,128)(2,1)} custom-call(s32[1]{0:T(128)} %bitcast.13.core_ref, bf16[256,64]{1,0:T(8,128)(2,1)S(1)} %convolution_convert_fusion.2.left_ref, bf16[8,2,64,128]{3,2,1,0:T(8,128)(2,1)S(1)} %bitcast.33, bf16[8,2,64,128]{3,2,1,0:T(8,128)(2,1)S(1)} %bitcast.34, bf16[4,256,896]{2,1,0:T(8,128)(2,1)S(1)} %pad_maximum_fusion.weight_ref), custom_call_target="tpu_custom_call" | custom-call | tf_op jit(solution)/shard_map/rollout/pallas_call | solution.py:297
  (10 shorter events, 0.1 us)
Async XLA Ops:
  4.9 25.5 %all-to-all-start = ((f32[32,8,256]{2,1,0:T(8,128)}), f32[32,8,256]{2,1,0:T(8,128)S(1)}, u32[]{:S(2)}, u32[]{:S(2)}) async-start(f32[32,8,256]{2,1,0:T(8,128)} %bitcast.35), calls=%async_computation | async-start | bytes 524288 | tf_op jit(solution)/shard_map/all_to_all | solution.py:54
  31.2 17.1 %all-to-all-start.1 = ((f32[32,8,256]{2,1,0:T(8,128)}), f32[32,8,256]{2,1,0:T(8,128)S(1)}, u32[]{:S(2)}, u32[]{:S(2)}) async-start(f32[32,8,256]{2,1,0:T(8,128)} %sum_share.1), calls=%async_computation.1 | async-start | bytes 524288 | tf_op jit(solution)/shard_map/all_to_all | solution.py:54
  36.0 0.7 collective-permute-start
  61.8 3.6 %collective-permute-start.2 = (f32[64,128]{1,0:T(8,128)S(1)}, f32[64,128]{1,0:T(8,128)S(1)}, u32[]{:S(2)}, u32[]{:S(2)}) collective-permute-start(f32[64,128]{1,0:T(8,128)S(1)} %get-tuple-element.29), channel_id=1, source_target_pairs={{0,32},{32,0},{64,96},{96,64},{128,160},{160,128},{192,224},{224,1... | collective-permute-start | bytes 98312 | tf_op jit(solution)/shard_map/ppermute | solution.py:326
  62.6 6.1 %collective-permute-start.1 = (f32[64,128]{1,0:T(8,128)S(1)}, f32[64,128]{1,0:T(8,128)S(1)}, u32[]{:S(2)}, u32[]{:S(2)}) collective-permute-start(f32[64,128]{1,0:T(8,128)S(1)} %get-tuple-element.29), channel_id=1, source_target_pairs={{0,16},{1,17},{2,18},{3,19},{4,48},{5,49},{6,50},{7,51},{8,84},{9,... | collective-permute-start | bytes 98312 | tf_op jit(solution)/shard_map/ppermute | solution.py:325
  65.4 14.9 %collective-permute-start.5 = (f32[64,256]{1,0:T(8,128)S(1)}, f32[64,256]{1,0:T(8,128)S(1)}, u32[]{:S(2)}, u32[]{:S(2)}) collective-permute-start(f32[64,256]{1,0:T(8,128)S(1)} %pad_maximum_fusion.1.pair0_ref), channel_id=1, source_target_pairs={{0,192},{32,224},{64,0},{96,32},{128,64},{160,96},{192,128},{224,1... | collective-permute-start | bytes 196616 | tf_op jit(solution)/shard_map/ppermute | solution.py:330
  67.0 13.3 %collective-permute-start.4 = (f32[64,256]{1,0:T(8,128)S(1)}, f32[64,256]{1,0:T(8,128)S(1)}, u32[]{:S(2)}, u32[]{:S(2)}) collective-permute-start(f32[64,256]{1,0:T(8,128)S(1)} %pad_maximum_fusion.1.pair0_ref), channel_id=1, source_target_pairs={{0,128},{32,160},{64,192},{96,224},{128,0},{160,32},{192,64},{224,... | collective-permute-start | bytes 196616 | tf_op jit(solution)/shard_map/ppermute | solution.py:330
  68.7 11.7 %collective-permute-start.3 = (f32[64,256]{1,0:T(8,128)S(1)}, f32[64,256]{1,0:T(8,128)S(1)}, u32[]{:S(2)}, u32[]{:S(2)}) collective-permute-start(f32[64,256]{1,0:T(8,128)S(1)} %pad_maximum_fusion.1.pair0_ref), channel_id=1, source_target_pairs={{0,64},{32,96},{64,128},{96,160},{128,192},{160,224},{192,0},{224,... | collective-permute-start | bytes 196616 | tf_op jit(solution)/shard_map/ppermute | solution.py:330
  70.3 14.4 %all-to-all-start.3 = ((bf16[16,64,128]{2,1,0:T(8,128)(2,1)}), bf16[16,64,128]{2,1,0:T(8,128)(2,1)S(1)}, u32[]{:S(2)}, u32[]{:S(2)}) async-start(bf16[16,64,128]{2,1,0:T(8,128)(2,1)} %bitcast.4), calls=%async_computation.3 | async-start | bytes 524288 | tf_op jit(solution)/shard_map/all_to_all | solution.py:54
  78.3 3.1 %copy-start.1 = (bf16[1024,896]{1,0:T(8,128)(2,1)S(1)}, bf16[1024,896]{1,0:T(8,128)(2,1)}, u32[]{:S(2)}) copy-start(bf16[1024,896]{1,0:T(8,128)(2,1)} %change_ref.1) | copy-start | bytes 5505028
  80.0 2.2 %copy-start = (f32[1024,896]{1,0:T(8,128)S(1)}, f32[1024,896]{1,0:T(8,128)}, u32[]{:S(2)}) copy-start(f32[1024,896]{1,0:T(8,128)} %error_ref.1) | copy-start | bytes 11010052
  84.7 6.5 %collective-permute-start.6 = (bf16[16,64,128]{2,1,0:T(8,128)(2,1)S(1)}, bf16[16,64,128]{2,1,0:T(8,128)(2,1)S(1)}, u32[]{:S(2)}, u32[]{:S(2)}) collective-permute-start(bf16[16,64,128]{2,1,0:T(8,128)(2,1)S(1)} %all-to-all-done.3), channel_id=1, source_target_pairs={{0,1},{1,0},{2,3},{3,2},{4,5},{5,4},{6,7},{7,6},{8,9},{9,8},{10,11... | collective-permute-start | bytes 786440 | tf_op jit(solution)/shard_map/ppermute | solution.py:341

commit v8 on v7

--- a/solution.py
+++ b/solution.py
@@ -30,7 +30,12 @@
     for z in range(8)
     for q in range(4)
 ]
-SWAP = [(r * COLS + 4 * z + q, z * COLS + 4 * r + q) for r in range(ROWS) for z in range(8) for q in range(4)]
+FANOUT = [
+    (r * COLS + 4 * z + q, t * COLS + 4 * r + q)
+    for r in range(ROWS)
+    for t, z in partners(r).items()
+    for q in range(4)
+]
 SAME_CORE = [
     [row * COLS + 4 * SLOTS[row][b] + 2 * half + core for b in range(ROWS) for half in range(2)]
     for row in range(ROWS)
@@ -131,7 +136,7 @@
     )(parts)
 
 
-def right_kernel(total_ref, left_ref, rows_ref, out_ref):
+def right_kernel(total_ref, left_ref, out_ref):
     left = jnp.concatenate([left_ref[:, i].reshape(R, -1) for i in range(4)], 1)
     both = dot(jnp.concatenate(split(left), 0), total_ref[...], 1, 0)
     right = both[:R] + both[R:]
@@ -144,21 +149,19 @@
     for b in range(BLOCKS):
         out_ref[b, R : GRAM_END, :R] = gram[: R // 2]
         out_ref[b, R : GRAM_END, R:] = gram[R // 2 :]
-        for i in range(rows_ref.shape[1] // LANES):
-            out_ref[b, GRAM_END + 8 * i : GRAM_END + 8 * i + 8] = rows_ref[:, i * LANES : (i + 1) * LANES]
-
-
-def right_part(total, left, some_rows):
+
+
+def right_part(total, left):
     rows, units = total.shape
     return pl.pallas_call(
         right_kernel,
-        in_specs=[VMEM, VMEM, VMEM],
+        in_specs=[VMEM, VMEM],
         out_specs=VMEM,
-        out_shape=jax.ShapeDtypeStruct((BLOCKS, GRAM_END + some_rows.size // LANES, LANES), jnp.float32),
+        out_shape=jax.ShapeDtypeStruct((BLOCKS, GRAM_END, LANES), jnp.float32),
         compiler_params=grant(12),
         cost_estimate=pl.CostEstimate(flops=4 * rows * units * R, bytes_accessed=2 * rows * units, transcendentals=0),
         name="right_part",
-    )(total, left, some_rows)
+    )(total, left)
 
 
 def inverse_factor(gram):
@@ -197,28 +200,22 @@
     return jnp.concatenate(out, 0)
 
 
-def settle_kernel(parts_ref, block_ref, gram_ref, rows_ref):
-    got = parts_ref[0, :GRAM_END]
+def settle_kernel(parts_ref, block_ref, gram_ref):
+    got = parts_ref[0]
     for b in range(1, BLOCKS):
-        got = got + parts_ref[b, :GRAM_END]
+        got = got + parts_ref[b]
     block_ref[...] = got[:R]
     gram_ref[...] = got[R:]
-    for b in range(BLOCKS):
-        for i in range(rows_ref.shape[1] // LANES):
-            piece = parts_ref[b, GRAM_END + 8 * i : GRAM_END + 8 * i + 8]
-            rows_ref[8 * b : 8 * b + 8, i * LANES : (i + 1) * LANES] = piece
 
 
 def settle(parts):
-    width = (parts.shape[1] - GRAM_END) // 8 * LANES
     return pl.pallas_call(
         settle_kernel,
         in_specs=[VMEM],
-        out_specs=[VMEM, VMEM, VMEM],
+        out_specs=[VMEM, VMEM],
         out_shape=[
             jax.ShapeDtypeStruct((R, LANES), jnp.float32),
             jax.ShapeDtypeStruct((R // 2, LANES), jnp.float32),
-            jax.ShapeDtypeStruct((R, width), jnp.float32),
         ],
         compiler_params=grant(6),
         name="settle",
@@ -283,7 +280,7 @@
     for q in range(4):
         first, second = (near_ref, other_ref) if q % 2 == 0 else (other_ref, near_ref)
         blocks = [jnp.where(even, first[b, q // 2], second[b, q // 2]) for b in range(width // LANES)]
-        delta = dot(left_ref[...], jnp.concatenate(blocks, 1), 1, 0)
+        delta = dot(left_ref[...], jnp.concatenate(blocks, 1), 0, 0)
         buf[q] = (weight_ref[q].astype(jnp.float32) + delta).astype(jnp.bfloat16)
         copy = pltpu.make_async_copy(buf.at[q], out_ref.at[:, pl.ds(q * width, width)], sem.at[q])
         copy.start()
@@ -310,18 +307,15 @@
 
 def local(weight_change, error_buffer, basis, rollout_weight):
     row = lax.axis_index("row")
-    core = lax.axis_index("col") % 2
+    q = lax.axis_index("col") % 4
     rows, units = weight_change.shape
     part = left_part(weight_change, error_buffer, basis.T)
     part, change, error = lax.optimization_barrier((part, weight_change, error_buffer))
     total = (change.astype(jnp.float32) + error).astype(jnp.bfloat16)
     parts = exchange(part.reshape(COLS, 8, rows // 4), "col")
     parts, total = lax.optimization_barrier((parts, total))
-    chunks = sum_share(parts)
-    some_rows = lax.ppermute(chunks[0], AXES, SWAP)
-    left = exchange(chunks, "col").reshape(8, 4, 8, rows // 4)
-    parts = exchange(right_part(total, left, some_rows), "row")
-    block, gram, far_left = settle(parts)
+    left = exchange(sum_share(parts), "col").reshape(8, 4, 8, rows // 4)
+    block, gram = settle(exchange(right_part(total, left), "row"))
     far = lax.ppermute(block, AXES, SPREAD)
     other_block = lax.ppermute(block, "row", [(r, r ^ 1) for r in range(ROWS)])
     inverse, copies = factor(gram)
@@ -329,18 +323,19 @@
     pair = jnp.concatenate([jnp.where(odd, other_block, block), jnp.where(odd, block, other_block)], 1)
     pairs = [lax.ppermute(pair, "row", [(r, (r + 2 * k) % ROWS) for r in range(ROWS)]) for k in (1, 2, 3)]
     far_round = dot(copies, far, 1, 0, HIGH).astype(jnp.bfloat16).reshape(COLS // 2, R, LANES)
-    far_round, inverse, weight = lax.optimization_barrier((far_round, inverse, rollout_weight))
+    mine = lax.dynamic_index_in_dim(left, q, 1, keepdims=False).reshape(R, rows // 4)
+    far_round, inverse, weight, mine = lax.optimization_barrier((far_round, inverse, rollout_weight, mine))
+    far_left = lax.ppermute(dot(inverse, mine, 1, 0, HIGH).astype(jnp.bfloat16), AXES, FANOUT)
     near = exchange(far_round, AXES, SAME_CORE)
     weight = jnp.stack([weight[:, i * units : (i + 1) * units] for i in range(4)])
     left_rows = left.transpose(0, 2, 1, 3).reshape(R, rows)
     left_round = dot(inverse, left_rows, 1, 0, HIGH).astype(jnp.bfloat16)
-    far_left = dot(far_left, inverse, 0, 1, HIGH).astype(jnp.bfloat16)
     new_basis, right_round = basis_part(row.astype(jnp.int32).reshape(1), inverse, [pair] + pairs, units)
     new_error = weight_change.astype(jnp.float32) + error_buffer - dot(left_round, right_round, 0, 0)
-    near, far_left, new_error, weight = lax.optimization_barrier((near, far_left, new_error, weight))
+    near, new_error, weight, far_left = lax.optimization_barrier((near, new_error, weight, far_left))
     other = lax.ppermute(near, "col", PAIR)
     halves = (BLOCKS, 2, R, LANES)
-    core = core.astype(jnp.int32).reshape(1)
+    core = (q % 2).astype(jnp.int32).reshape(1)
     new_rollout = rollout(core, far_left, near.reshape(halves), other.reshape(halves), weight)
     return (new_error, new_basis.T, new_rollout)
 

time: 94.4 us -> 93 us (0.985); the launches traced: 92.7 us -> 92.6 us
  blocking collectives: 12.8 us -> 16.9 us
  waiting for transfers between devices: 22.7 us -> 19.2 us
    all_to_all x1, blocking collectives: 12.8 us -> 16.9 us  [exchange(): return lax.all_to_all(parts, axis, 0, 0, axis_index_groups=groups)]
    all_to_all x3, waiting for transfers between devices: 21.5 us -> 18.1 us  [exchange(): return lax.all_to_all(parts, axis, 0, 0, axis_index_groups=groups)]
    ppermute x1, starting transfers between devices: 5.3 us -> 4.01 us  [local(): other = lax.ppermute(near, 'col', PAIR)]
  transfers between devices with their start and end apart: 10 -> 10, of which waited for: 3 -> 3; matrix products, arithmetic and copies ran while one was open for 11% -> 10% of each run, Pallas kernels for 3% -> 3%
where the time goes in v8:
time: 93 us; the launch traced here: 92.6 us
  starting transfers between devices  35.6 us (38%)
  waiting for transfers between devices  19.2 us (21%)
  blocking collectives  16.9 us (18%)
  Pallas kernels  10.3 us (11%)
  matrix products  3.99 us (4%)
  other arithmetic  3.26 us (4%)
  local copies, waits for them, and re-layouts  2.56 us (3%)
    all_to_all x3, starting transfers between devices, exchange(): return lax.all_to_all(parts, axis, 0, 0, axis_index_groups=groups)  25.1 us
    all_to_all x3, waiting for transfers between devices, exchange(): return lax.all_to_all(parts, axis, 0, 0, axis_index_groups=groups)  18.1 us
    all_to_all x1, blocking collectives, exchange(): return lax.all_to_all(parts, axis, 0, 0, axis_index_groups=groups)  16.9 us
    pallas_call x1, Pallas kernels, left_part(): pl.pallas_call(left_kernel, in_specs=[ANY, ANY, ANY], out_specs=VMEM, out...  4.24 us
    ppermute x1, starting transfers between devices, local(): other = lax.ppermute(near, 'col', PAIR)  4.01 us
    dot_general x4, matrix products, dot(): lax.dot_general(a, b, (((ca,), (cb,)), ((), ())), precision=precision, pr...  3.99 us
    ppermute x3, starting transfers between devices, local(): lax.ppermute(pair, 'row', [(r, (r + 2 * k) % ROWS) for r in range(ROWS)])  3.06 us
    convert_element_type x1, other arithmetic, local(): total = (change.astype(jnp.float32) + error).astype(jnp.bfloat16)  2.95 us
  transfers between devices with their start and end apart: 10, of which 3 were waited for; matrix products, arithmetic and copies ran while one was open for 10% of the time, Pallas kernels for 3%

profile of v8, /device:TPU:1, one launch (start us, length us, event | category | flops | bytes accessed | tf_op | source)
XLA Modules:
  0.0 92.6 jit_solution(15791482728282912755)
XLA Ops:
  0.6 4.2 %left_part.1 = f32[8,4,8,256]{3,2,1,0:T(8,128)} custom-call(bf16[1024,896]{1,0:T(8,128)(2,1)} %change_ref.1, f32[1024,896]{1,0:T(8,128)} %error_ref.1, f32[64,896]{1,0:T(8,128)} %bitcast.37), custom_call_target="tpu_custom_call" | custom-call | flops 352321536 | bytes 5505024 | tf_op jit(solution)/shard_map/left_part/pallas_call | solution.py:102
  4.9 12.6 %all-to-all-start = ((f32[32,8,256]{2,1,0:T(8,128)}), f32[32,8,256]{2,1,0:T(8,128)S(1)}, u32[]{:S(2)}, u32[]{:S(2)}) async-start(f32[32,8,256]{2,1,0:T(8,128)} %bitcast.36), calls=%async_computation | async-start | bytes 524288 | tf_op jit(solution)/shard_map/all_to_all | solution.py:59
  17.5 3.0 %add_convert_fusion.total_ref = bf16[1024,896]{1,0:T(8,128)(2,1)S(1)} fusion(f32[1024,896]{1,0:T(8,128)} %error_ref.1, bf16[1024,896]{1,0:T(8,128)(2,1)} %change_ref.1), kind=kLoop, calls=%fused_computation.1 | loop fusion | flops 2752512 | bytes 7340032 | tf_op jit(solution)/shard_map/convert_element_type | solution.py:314
  20.4 10.0 %all-to-all-done.parts_ref = f32[32,8,256]{2,1,0:T(8,128)S(1)} async-done(((f32[32,8,256]{2,1,0:T(8,128)}), f32[32,8,256]{2,1,0:T(8,128)S(1)}, u32[]{:S(2)}, u32[]{:S(2)}) %all-to-all-start) | async-done | bytes 262176 | tf_op jit(solution)/shard_map/all_to_all | solution.py:59
  30.4 0.1 sum_share.1
  30.5 16.9 %all_to_all.20 = f32[32,8,256]{2,1,0:T(8,128)S(1)} all-to-all(f32[32,8,256]{2,1,0:T(8,128)S(1)} %sum_share.1), channel_id=1, replica_groups=mesh['row'=8,'col'=32] {'col'}, dimensions={0} | all-to-all | bytes 524288 | tf_op jit(solution)/shard_map/all_to_all | solution.py:59
  47.3 1.5 %right_part.1 = f32[8,96,128]{2,1,0:T(8,128)} custom-call(bf16[1024,896]{1,0:T(8,128)(2,1)S(1)} %add_convert_fusion.total_ref, f32[8,4,8,256]{3,2,1,0:T(8,128)S(1)} %bitcast.31), custom_call_target="tpu_custom_call" | custom-call | flops 234881024 | bytes 1835008 | tf_op jit(solution)/shard_map/right_part/pallas_call | solution.py:156
  48.8 4.2 %all-to-all-start.2 = ((f32[8,96,128]{2,1,0:T(8,128)}), f32[8,96,128]{2,1,0:T(8,128)S(1)}, u32[]{:S(2)}, u32[]{:S(2)}) async-start(f32[8,96,128]{2,1,0:T(8,128)} %right_part.1), calls=%async_computation.2 | async-start | bytes 786432 | tf_op jit(solution)/shard_map/all_to_all | solution.py:59
  53.0 8.1 %all-to-all-done.2.parts_ref = f32[8,96,128]{2,1,0:T(8,128)S(1)} async-done(((f32[8,96,128]{2,1,0:T(8,128)}), f32[8,96,128]{2,1,0:T(8,128)S(1)}, u32[]{:S(2)}, u32[]{:S(2)}) %all-to-all-start.2) | async-done | bytes 393248 | tf_op jit(solution)/shard_map/all_to_all | solution.py:59
  61.1 0.4 collective-permute-start.1
  61.6 1.8 %collective-permute-start = (f32[64,128]{1,0:T(8,128)S(1)}, f32[64,128]{1,0:T(8,128)S(1)}, u32[]{:S(2)}, u32[]{:S(2)}) collective-permute-start(f32[64,128]{1,0:T(8,128)S(1)} %get-tuple-element.29), channel_id=1, source_target_pairs={{0,16},{1,17},{2,18},{3,19},{4,48},{5,49},{6,50},{7,51},{8,84},{9,... | collective-permute-start | bytes 98312 | tf_op jit(solution)/shard_map/ppermute | solution.py:319
  63.4 1.9 %factor.1 = (f32[64,64]{1,0:T(8,128)S(1)}, f32[1024,64]{1,0:T(8,128)S(1)}) custom-call(f32[32,128]{1,0:T(8,128)S(1)} %get-tuple-element.27.gram_ref), custom_call_target="tpu_custom_call" | custom-call | flops 1 | bytes 1 | tf_op jit(solution)/shard_map/factor/pallas_call | solution.py:234
  65.3 1.5 %collective-permute-start.4 = (f32[64,256]{1,0:T(8,128)S(1)}, f32[64,256]{1,0:T(8,128)S(1)}, u32[]{:S(2)}, u32[]{:S(2)}) collective-permute-start(f32[64,256]{1,0:T(8,128)S(1)} %pad_maximum_fusion.1.pair0_ref), channel_id=1, source_target_pairs={{0,192},{32,224},{64,0},{96,32},{128,64},{160,96},{192,128},{224,1... | collective-permute-start | bytes 196616 | tf_op jit(solution)/shard_map/ppermute | solution.py:324
  66.8 1.6 %collective-permute-start.3 = (f32[64,256]{1,0:T(8,128)S(1)}, f32[64,256]{1,0:T(8,128)S(1)}, u32[]{:S(2)}, u32[]{:S(2)}) collective-permute-start(f32[64,256]{1,0:T(8,128)S(1)} %pad_maximum_fusion.1.pair0_ref), channel_id=1, source_target_pairs={{0,128},{32,160},{64,192},{96,224},{128,0},{160,32},{192,64},{224,... | collective-permute-start | bytes 196616 | tf_op jit(solution)/shard_map/ppermute | solution.py:324
  68.4 1.1 %convolution_convert_fusion = bf16[1024,128]{1,0:T(8,128)(2,1)} fusion(f32[1024,64]{1,0:T(8,128)S(1)} %get-tuple-element.28, f32[64,128]{1,0:T(8,128)S(1)} %collective-permute-done), kind=kOutput, calls=%fused_computation.3 | convolution fusion | flops 50462720 | bytes 557056 | tf_op jit(solution)/shard_map/dot_general | solution.py:48
  69.4 8.3 %all-to-all-start.3 = ((bf16[16,64,128]{2,1,0:T(8,128)(2,1)}), bf16[16,64,128]{2,1,0:T(8,128)(2,1)S(1)}, u32[]{:S(2)}, u32[]{:S(2)}) async-start(bf16[16,64,128]{2,1,0:T(8,128)(2,1)} %bitcast.3), calls=%async_computation.3 | async-start | bytes 524288 | tf_op jit(solution)/shard_map/all_to_all | solution.py:59
  77.7 0.3 convolution_convert_fusion.1
  78.0 0.2 convolution_convert_fusion.2
  78.1 1.2 %collective-permute-start.5 = (bf16[64,256]{1,0:T(8,128)(2,1)S(1)}, bf16[64,256]{1,0:T(8,128)(2,1)S(1)}, u32[]{:S(2)}, u32[]{:S(2)}) collective-permute-start(bf16[64,256]{1,0:T(8,128)(2,1)S(1)} %convolution_convert_fusion.2), channel_id=1, source_target_pairs={{16,0},{17,1},{18,2},{19,3},{12,32},{13,33},{14,34},{15,35},{20,64... | collective-permute-start | bytes 98312 | tf_op jit(solution)/shard_map/ppermute | solution.py:328
  79.4 1.7 %slice_bitcast_fusion.3 = (bf16[1,256,896]{2,1,0:T(8,128)(2,1)S(1)}, bf16[1,256,896]{2,1,0:T(8,128)(2,1)S(1)}, bf16[1,256,896]{2,1,0:T(8,128)(2,1)S(1)}, bf16[1,256,896]{2,1,0:T(8,128)(2,1)S(1)}) fusion(bf16[256,3584]{1,0:T(8,128)(2,1)} %param.7), kind=kLoop, calls=%fused_computation.9 | loop fusion | bytes 3670016 | tf_op jit(solution)/shard_map/stack | solution.py:330
  81.1 0.0 copy-start
  81.1 0.3 pad_maximum_fusion.weight_ref
  81.4 0.0 collective-permute-done.4.pair3_ref
  81.4 0.0 collective-permute-done.3.pair2_ref
  81.4 1.1 %basis_part.1 = (f32[64,896]{1,0:T(8,128)}, bf16[64,896]{1,0:T(8,128)(2,1)S(1)}) custom-call(s32[1]{0:T(128)} %bitcast.7.row_ref, f32[64,64]{1,0:T(8,128)S(1)} %get-tuple-element.32.inverse_ref, f32[64,256]{1,0:T(8,128)S(1)} %pad_maximum_fusion.1.pair0_ref, f32[64,256]{1,0:T(8,128)S(1)} %collective-permute-done.2.pair1_ref, ...), custom_call_target="tpu_custom_call" | custom-call | tf_op jit(solution)/shard_map/basis_part/pallas_call | solution.py:263
  82.5 0.8 copy-done
  83.3 2.5 %add_subtract_fusion = f32[1024,896]{1,0:T(8,128)} fusion(f32[1024,896]{1,0:T(8,128)S(1)} %copy-done, bf16[1024,896]{1,0:T(8,128)(2,1)S(1)} %copy-done.1, bf16[64,1024]{1,0:T(8,128)(2,1)S(1)} %convolution_convert_fusion.1, bf16[64,896]{1,0:T(8,128)(2,1)S(1)} %get-tuple-element.33), kind=kOutput, calls=%fused_computation | convolution fusion | flops 120193024 | bytes 9420800 | tf_op jit(solution)/shard_map/dot_general | solution.py:48
  85.8 0.0 collective-permute-done.5.left_ref
  85.8 0.0 all-to-all-done.3
  85.8 4.0 %collective-permute-start.6 = (bf16[16,64,128]{2,1,0:T(8,128)(2,1)S(1)}, bf16[16,64,128]{2,1,0:T(8,128)(2,1)S(1)}, u32[]{:S(2)}, u32[]{:S(2)}) collective-permute-start(bf16[16,64,128]{2,1,0:T(8,128)(2,1)S(1)} %all-to-all-done.3), channel_id=1, source_target_pairs={{0,1},{1,0},{2,3},{3,2},{4,5},{5,4},{6,7},{7,6},{8,9},{9,8},{10,11... | collective-permute-start | bytes 786440 | tf_op jit(solution)/shard_map/ppermute | solution.py:336
  89.9 1.2 %collective-permute-done.6 = bf16[16,64,128]{2,1,0:T(8,128)(2,1)S(1)} collective-permute-done((bf16[16,64,128]{2,1,0:T(8,128)(2,1)S(1)}, bf16[16,64,128]{2,1,0:T(8,128)(2,1)S(1)}, u32[]{:S(2)}, u32[]{:S(2)}) %collective-permute-start.6) | collective-permute-done | bytes 262176 | tf_op jit(solution)/shard_map/ppermute | solution.py:336
  91.0 1.6 %rollout.1 = bf16[256,3584]{1,0:T(8,128)(2,1)} custom-call(s32[1]{0:T(128)} %bitcast.13.core_ref, bf16[64,256]{1,0:T(8,128)(2,1)S(1)} %collective-permute-done.5.left_ref, bf16[8,2,64,128]{3,2,1,0:T(8,128)(2,1)S(1)} %bitcast.34, bf16[8,2,64,128]{3,2,1,0:T(8,128)(2,1)S(1)} %bitcast.35, bf16[4,256,896]{2,1,0:T(8,128)(2,1)S(1)} %pad_maximum_fusion.weight_ref), custom_call_target="tpu_custom_call" | custom-call | tf_op jit(solution)/shard_map/rollout/pallas_call | solution.py:294
  (10 shorter events, 0.1 us)
Async XLA Ops:
  4.9 25.5 %all-to-all-start = ((f32[32,8,256]{2,1,0:T(8,128)}), f32[32,8,256]{2,1,0:T(8,128)S(1)}, u32[]{:S(2)}, u32[]{:S(2)}) async-start(f32[32,8,256]{2,1,0:T(8,128)} %bitcast.36), calls=%async_computation | async-start | bytes 524288 | tf_op jit(solution)/shard_map/all_to_all | solution.py:59
  48.8 12.3 %all-to-all-start.2 = ((f32[8,96,128]{2,1,0:T(8,128)}), f32[8,96,128]{2,1,0:T(8,128)S(1)}, u32[]{:S(2)}, u32[]{:S(2)}) async-start(f32[8,96,128]{2,1,0:T(8,128)} %right_part.1), calls=%async_computation.2 | async-start | bytes 786432 | tf_op jit(solution)/shard_map/all_to_all | solution.py:59
  61.1 4.1 %collective-permute-start.1 = (f32[64,128]{1,0:T(8,128)S(1)}, f32[64,128]{1,0:T(8,128)S(1)}, u32[]{:S(2)}, u32[]{:S(2)}) collective-permute-start(f32[64,128]{1,0:T(8,128)S(1)} %get-tuple-element.29), channel_id=1, source_target_pairs={{0,32},{32,0},{64,96},{96,64},{128,160},{160,128},{192,224},{224,1... | collective-permute-start | bytes 98312 | tf_op jit(solution)/shard_map/ppermute | solution.py:320
  61.6 6.8 %collective-permute-start = (f32[64,128]{1,0:T(8,128)S(1)}, f32[64,128]{1,0:T(8,128)S(1)}, u32[]{:S(2)}, u32[]{:S(2)}) collective-permute-start(f32[64,128]{1,0:T(8,128)S(1)} %get-tuple-element.29), channel_id=1, source_target_pairs={{0,16},{1,17},{2,18},{3,19},{4,48},{5,49},{6,50},{7,51},{8,84},{9,... | collective-permute-start | bytes 98312 | tf_op jit(solution)/shard_map/ppermute | solution.py:319
  65.3 16.1 %collective-permute-start.4 = (f32[64,256]{1,0:T(8,128)S(1)}, f32[64,256]{1,0:T(8,128)S(1)}, u32[]{:S(2)}, u32[]{:S(2)}) collective-permute-start(f32[64,256]{1,0:T(8,128)S(1)} %pad_maximum_fusion.1.pair0_ref), channel_id=1, source_target_pairs={{0,192},{32,224},{64,0},{96,32},{128,64},{160,96},{192,128},{224,1... | collective-permute-start | bytes 196616 | tf_op jit(solution)/shard_map/ppermute | solution.py:324
  66.8 14.6 %collective-permute-start.3 = (f32[64,256]{1,0:T(8,128)S(1)}, f32[64,256]{1,0:T(8,128)S(1)}, u32[]{:S(2)}, u32[]{:S(2)}) collective-permute-start(f32[64,256]{1,0:T(8,128)S(1)} %pad_maximum_fusion.1.pair0_ref), channel_id=1, source_target_pairs={{0,128},{32,160},{64,192},{96,224},{128,0},{160,32},{192,64},{224,... | collective-permute-start | bytes 196616 | tf_op jit(solution)/shard_map/ppermute | solution.py:324
  68.4 13.1 %collective-permute-start.2 = (f32[64,256]{1,0:T(8,128)S(1)}, f32[64,256]{1,0:T(8,128)S(1)}, u32[]{:S(2)}, u32[]{:S(2)}) collective-permute-start(f32[64,256]{1,0:T(8,128)S(1)} %pad_maximum_fusion.1.pair0_ref), channel_id=1, source_target_pairs={{0,64},{32,96},{64,128},{96,160},{128,192},{160,224},{192,0},{224,... | collective-permute-start | bytes 196616 | tf_op jit(solution)/shard_map/ppermute | solution.py:324
  69.4 16.4 %all-to-all-start.3 = ((bf16[16,64,128]{2,1,0:T(8,128)(2,1)}), bf16[16,64,128]{2,1,0:T(8,128)(2,1)S(1)}, u32[]{:S(2)}, u32[]{:S(2)}) async-start(bf16[16,64,128]{2,1,0:T(8,128)(2,1)} %bitcast.3), calls=%async_computation.3 | async-start | bytes 524288 | tf_op jit(solution)/shard_map/all_to_all | solution.py:59
  78.1 7.7 %collective-permute-start.5 = (bf16[64,256]{1,0:T(8,128)(2,1)S(1)}, bf16[64,256]{1,0:T(8,128)(2,1)S(1)}, u32[]{:S(2)}, u32[]{:S(2)}) collective-permute-start(bf16[64,256]{1,0:T(8,128)(2,1)S(1)} %convolution_convert_fusion.2), channel_id=1, source_target_pairs={{16,0},{17,1},{18,2},{19,3},{12,32},{13,33},{14,34},{15,35},{20,64... | collective-permute-start | bytes 98312 | tf_op jit(solution)/shard_map/ppermute | solution.py:328
  79.4 3.1 %copy-start.1 = (bf16[1024,896]{1,0:T(8,128)(2,1)S(1)}, bf16[1024,896]{1,0:T(8,128)(2,1)}, u32[]{:S(2)}) copy-start(bf16[1024,896]{1,0:T(8,128)(2,1)} %change_ref.1) | copy-start | bytes 5505028
  81.1 2.2 %copy-start = (f32[1024,896]{1,0:T(8,128)S(1)}, f32[1024,896]{1,0:T(8,128)}, u32[]{:S(2)}) copy-start(f32[1024,896]{1,0:T(8,128)} %error_ref.1) | copy-start | bytes 11010052
  85.8 5.2 %collective-permute-start.6 = (bf16[16,64,128]{2,1,0:T(8,128)(2,1)S(1)}, bf16[16,64,128]{2,1,0:T(8,128)(2,1)S(1)}, u32[]{:S(2)}, u32[]{:S(2)}) collective-permute-start(bf16[16,64,128]{2,1,0:T(8,128)(2,1)S(1)} %all-to-all-done.3), channel_id=1, source_target_pairs={{0,1},{1,0},{2,3},{3,2},{4,5},{5,4},{6,7},{7,6},{8,9},{9,8},{10,11... | collective-permute-start | bytes 786440 | tf_op jit(solution)/shard_map/ppermute | solution.py:336

commit v9 on v8

--- a/solution.py
+++ b/solution.py
@@ -323,8 +323,8 @@
     pair = jnp.concatenate([jnp.where(odd, other_block, block), jnp.where(odd, block, other_block)], 1)
     pairs = [lax.ppermute(pair, "row", [(r, (r + 2 * k) % ROWS) for r in range(ROWS)]) for k in (1, 2, 3)]
     far_round = dot(copies, far, 1, 0, HIGH).astype(jnp.bfloat16).reshape(COLS // 2, R, LANES)
+    far_round, inverse, weight, left = lax.optimization_barrier((far_round, inverse, rollout_weight, left))
     mine = lax.dynamic_index_in_dim(left, q, 1, keepdims=False).reshape(R, rows // 4)
-    far_round, inverse, weight, mine = lax.optimization_barrier((far_round, inverse, rollout_weight, mine))
     far_left = lax.ppermute(dot(inverse, mine, 1, 0, HIGH).astype(jnp.bfloat16), AXES, FANOUT)
     near = exchange(far_round, AXES, SAME_CORE)
     weight = jnp.stack([weight[:, i * units : (i + 1) * units] for i in range(4)])

time: 93 us -> 92 us (0.989)
  blocking collectives: 16.9 us -> 28.8 us
  waiting for transfers between devices: 19.2 us -> 11.2 us
  starting transfers between devices: 35.6 us -> 31.6 us
    all_to_all x1 -> x2, blocking collectives: 16.9 us -> 28.8 us  [exchange(): return lax.all_to_all(parts, axis, 0, 0, axis_index_groups=groups)]
    all_to_all x3 -> x2, waiting for transfers between devices: 18.1 us -> 9.98 us  [exchange(): return lax.all_to_all(parts, axis, 0, 0, axis_index_groups=groups)]
    all_to_all x3 -> x2, starting transfers between devices: 25.1 us -> 20.5 us  [exchange(): return lax.all_to_all(parts, axis, 0, 0, axis_index_groups=groups)]
  transfers between devices with their start and end apart: 10 -> 9, of which waited for: 3 -> 2; matrix products, arithmetic and copies ran while one was open for 10% -> 10% of each run, Pallas kernels for 3% -> 3%
where the time goes in v9:
time: 92 us; the launch traced here: 91.6 us
  starting transfers between devices  31.6 us (34%)
  blocking collectives  28.8 us (31%)
  waiting for transfers between devices  11.2 us (12%)
  Pallas kernels  9.57 us (10%)
  matrix products  3.99 us (4%)
  other arithmetic  3.26 us (4%)
  local copies, waits for them, and re-layouts  2.55 us (3%)
    all_to_all x2, blocking collectives, exchange(): return lax.all_to_all(parts, axis, 0, 0, axis_index_groups=groups)  28.8 us
    all_to_all x2, starting transfers between devices, exchange(): return lax.all_to_all(parts, axis, 0, 0, axis_index_groups=groups)  20.5 us
    all_to_all x2, waiting for transfers between devices, exchange(): return lax.all_to_all(parts, axis, 0, 0, axis_index_groups=groups)  9.98 us
    pallas_call x1, Pallas kernels, left_part(): pl.pallas_call(left_kernel, in_specs=[ANY, ANY, ANY], out_specs=VMEM, out...  4.24 us
    dot_general x4, matrix products, dot(): lax.dot_general(a, b, (((ca,), (cb,)), ((), ())), precision=precision, pr...  3.99 us
    ppermute x1, starting transfers between devices, local(): other = lax.ppermute(near, 'col', PAIR)  3.94 us
    convert_element_type x1, other arithmetic, local(): total = (change.astype(jnp.float32) + error).astype(jnp.bfloat16)  2.95 us
    ppermute x3, starting transfers between devices, local(): lax.ppermute(pair, 'row', [(r, (r + 2 * k) % ROWS) for r in range(ROWS)])  2.75 us
  transfers between devices with their start and end apart: 9, of which 2 were waited for; matrix products, arithmetic and copies ran while one was open for 10% of the time, Pallas kernels for 3%

profile of v9, /device:TPU:1, one launch (start us, length us, event | category | flops | bytes accessed | tf_op | source)
XLA Modules:
  0.0 91.6 jit_solution(10554957443647500089)
XLA Ops:
  0.6 4.2 %left_part.1 = f32[8,4,8,256]{3,2,1,0:T(8,128)} custom-call(bf16[1024,896]{1,0:T(8,128)(2,1)} %change_ref.1, f32[1024,896]{1,0:T(8,128)} %error_ref.1, f32[64,896]{1,0:T(8,128)} %bitcast.36), custom_call_target="tpu_custom_call" | custom-call | flops 352321536 | bytes 5505024 | tf_op jit(solution)/shard_map/left_part/pallas_call | solution.py:102
  4.9 12.6 %all-to-all-start = ((f32[32,8,256]{2,1,0:T(8,128)}), f32[32,8,256]{2,1,0:T(8,128)S(1)}, u32[]{:S(2)}, u32[]{:S(2)}) async-start(f32[32,8,256]{2,1,0:T(8,128)} %bitcast.35), calls=%async_computation | async-start | bytes 524288 | tf_op jit(solution)/shard_map/all_to_all | solution.py:59
  17.5 3.0 %add_convert_fusion.total_ref = bf16[1024,896]{1,0:T(8,128)(2,1)S(1)} fusion(f32[1024,896]{1,0:T(8,128)} %error_ref.1, bf16[1024,896]{1,0:T(8,128)(2,1)} %change_ref.1), kind=kLoop, calls=%fused_computation.1 | loop fusion | flops 2752512 | bytes 7340032 | tf_op jit(solution)/shard_map/convert_element_type | solution.py:314
  20.4 10.0 %all-to-all-done.parts_ref = f32[32,8,256]{2,1,0:T(8,128)S(1)} async-done(((f32[32,8,256]{2,1,0:T(8,128)}), f32[32,8,256]{2,1,0:T(8,128)S(1)}, u32[]{:S(2)}, u32[]{:S(2)}) %all-to-all-start) | async-done | bytes 262176 | tf_op jit(solution)/shard_map/all_to_all | solution.py:59
  30.4 0.1 sum_share.1
  30.5 16.9 %all_to_all.20 = f32[32,8,256]{2,1,0:T(8,128)S(1)} all-to-all(f32[32,8,256]{2,1,0:T(8,128)S(1)} %sum_share.1), channel_id=1, replica_groups=mesh['row'=8,'col'=32] {'col'}, dimensions={0} | all-to-all | bytes 524288 | tf_op jit(solution)/shard_map/all_to_all | solution.py:59
  47.3 0.7 right_part.1
  48.1 11.9 %all_to_all.21.parts_ref = f32[8,96,128]{2,1,0:T(8,128)S(1)} all-to-all(f32[8,96,128]{2,1,0:T(8,128)S(1)} %right_part.1), channel_id=1, replica_groups=mesh['row'=8,'col'=32] {'row'}, dimensions={0} | all-to-all | bytes 786432 | tf_op jit(solution)/shard_map/all_to_all | solution.py:59
  60.0 1.2 %collective-permute-start.1 = (f32[64,128]{1,0:T(8,128)S(1)}, f32[64,128]{1,0:T(8,128)S(1)}, u32[]{:S(2)}, u32[]{:S(2)}) collective-permute-start(f32[64,128]{1,0:T(8,128)S(1)} %get-tuple-element.29), channel_id=1, source_target_pairs={{0,32},{32,0},{64,96},{96,64},{128,160},{160,128},{192,224},{224,1... | collective-permute-start | bytes 98312 | tf_op jit(solution)/shard_map/ppermute | solution.py:320
  61.2 1.8 %collective-permute-start = (f32[64,128]{1,0:T(8,128)S(1)}, f32[64,128]{1,0:T(8,128)S(1)}, u32[]{:S(2)}, u32[]{:S(2)}) collective-permute-start(f32[64,128]{1,0:T(8,128)S(1)} %get-tuple-element.29), channel_id=1, source_target_pairs={{0,16},{1,17},{2,18},{3,19},{4,48},{5,49},{6,50},{7,51},{8,84},{9,... | collective-permute-start | bytes 98312 | tf_op jit(solution)/shard_map/ppermute | solution.py:319
  63.0 1.9 %factor.1 = (f32[64,64]{1,0:T(8,128)S(1)}, f32[1024,64]{1,0:T(8,128)S(1)}) custom-call(f32[32,128]{1,0:T(8,128)S(1)} %get-tuple-element.27.gram_ref), custom_call_target="tpu_custom_call" | custom-call | flops 1 | bytes 1 | tf_op jit(solution)/shard_map/factor/pallas_call | solution.py:234
  64.9 0.0 collective-permute-done.1
  64.9 0.6 collective-permute-start.4
  65.6 2.1 %collective-permute-start.3 = (f32[64,256]{1,0:T(8,128)S(1)}, f32[64,256]{1,0:T(8,128)S(1)}, u32[]{:S(2)}, u32[]{:S(2)}) collective-permute-start(f32[64,256]{1,0:T(8,128)S(1)} %pad_maximum_fusion.1.pair0_ref), channel_id=1, source_target_pairs={{0,128},{32,160},{64,192},{96,224},{128,0},{160,32},{192,64},{224,... | collective-permute-start | bytes 196616 | tf_op jit(solution)/shard_map/ppermute | solution.py:324
  67.7 0.0 collective-permute-start.2
  67.7 1.1 %convolution_convert_fusion = bf16[1024,128]{1,0:T(8,128)(2,1)} fusion(f32[1024,64]{1,0:T(8,128)S(1)} %get-tuple-element.28, f32[64,128]{1,0:T(8,128)S(1)} %collective-permute-done), kind=kOutput, calls=%fused_computation.3 | convolution fusion | flops 50462720 | bytes 557056 | tf_op jit(solution)/shard_map/dot_general | solution.py:48
  68.7 7.9 %all-to-all-start.3 = ((bf16[16,64,128]{2,1,0:T(8,128)(2,1)}), bf16[16,64,128]{2,1,0:T(8,128)(2,1)S(1)}, u32[]{:S(2)}, u32[]{:S(2)}) async-start(bf16[16,64,128]{2,1,0:T(8,128)(2,1)} %bitcast.3), calls=%async_computation.3 | async-start | bytes 524288 | tf_op jit(solution)/shard_map/all_to_all | solution.py:59
  76.6 0.2 convolution_convert_fusion.2
  76.8 0.2 convolution_convert_fusion.1
  77.1 1.4 %collective-permute-start.5 = (bf16[64,256]{1,0:T(8,128)(2,1)S(1)}, bf16[64,256]{1,0:T(8,128)(2,1)S(1)}, u32[]{:S(2)}, u32[]{:S(2)}) collective-permute-start(bf16[64,256]{1,0:T(8,128)(2,1)S(1)} %convolution_convert_fusion.2), channel_id=1, source_target_pairs={{16,0},{17,1},{18,2},{19,3},{12,32},{13,33},{14,34},{15,35},{20,64... | collective-permute-start | bytes 98312 | tf_op jit(solution)/shard_map/ppermute | solution.py:328
  78.5 1.7 %slice_bitcast_fusion.3 = (bf16[1,256,896]{2,1,0:T(8,128)(2,1)S(1)}, bf16[1,256,896]{2,1,0:T(8,128)(2,1)S(1)}, bf16[1,256,896]{2,1,0:T(8,128)(2,1)S(1)}, bf16[1,256,896]{2,1,0:T(8,128)(2,1)S(1)}) fusion(bf16[256,3584]{1,0:T(8,128)(2,1)} %param.7), kind=kLoop, calls=%fused_computation.9 | loop fusion | bytes 3670016 | tf_op jit(solution)/shard_map/stack | solution.py:330
  80.2 0.0 copy-start
  80.2 0.3 pad_maximum_fusion.weight_ref
  80.5 0.0 collective-permute-done.4.pair3_ref
  80.5 0.0 collective-permute-done.3.pair2_ref
  80.5 1.1 %basis_part.1 = (f32[64,896]{1,0:T(8,128)}, bf16[64,896]{1,0:T(8,128)(2,1)S(1)}) custom-call(s32[1]{0:T(128)} %bitcast.6.row_ref, f32[64,64]{1,0:T(8,128)S(1)} %get-tuple-element.32.inverse_ref, f32[64,256]{1,0:T(8,128)S(1)} %pad_maximum_fusion.1.pair0_ref, f32[64,256]{1,0:T(8,128)S(1)} %collective-permute-done.2.pair1_ref, ...), custom_call_target="tpu_custom_call" | custom-call | tf_op jit(solution)/shard_map/basis_part/pallas_call | solution.py:263
  81.6 0.8 copy-done
  82.4 2.5 %add_subtract_fusion = f32[1024,896]{1,0:T(8,128)} fusion(f32[1024,896]{1,0:T(8,128)S(1)} %copy-done, bf16[1024,896]{1,0:T(8,128)(2,1)S(1)} %copy-done.1, bf16[64,1024]{1,0:T(8,128)(2,1)S(1)} %convolution_convert_fusion.1, bf16[64,896]{1,0:T(8,128)(2,1)S(1)} %get-tuple-element.34), kind=kOutput, calls=%fused_computation | convolution fusion | flops 120193024 | bytes 9420800 | tf_op jit(solution)/shard_map/dot_general | solution.py:48
  84.9 0.0 collective-permute-done.5.left_ref
  84.9 3.9 %collective-permute-start.6 = (bf16[16,64,128]{2,1,0:T(8,128)(2,1)S(1)}, bf16[16,64,128]{2,1,0:T(8,128)(2,1)S(1)}, u32[]{:S(2)}, u32[]{:S(2)}) collective-permute-start(bf16[16,64,128]{2,1,0:T(8,128)(2,1)S(1)} %all-to-all-done.3), channel_id=1, source_target_pairs={{0,1},{1,0},{2,3},{3,2},{4,5},{5,4},{6,7},{7,6},{8,9},{9,8},{10,11... | collective-permute-start | bytes 786440 | tf_op jit(solution)/shard_map/ppermute | solution.py:336
  88.9 1.2 %collective-permute-done.6 = bf16[16,64,128]{2,1,0:T(8,128)(2,1)S(1)} collective-permute-done((bf16[16,64,128]{2,1,0:T(8,128)(2,1)S(1)}, bf16[16,64,128]{2,1,0:T(8,128)(2,1)S(1)}, u32[]{:S(2)}, u32[]{:S(2)}) %collective-permute-start.6) | collective-permute-done | bytes 262176 | tf_op jit(solution)/shard_map/ppermute | solution.py:336
  90.0 1.6 %rollout.1 = bf16[256,3584]{1,0:T(8,128)(2,1)} custom-call(s32[1]{0:T(128)} %bitcast.13.core_ref, bf16[64,256]{1,0:T(8,128)(2,1)S(1)} %collective-permute-done.5.left_ref, bf16[8,2,64,128]{3,2,1,0:T(8,128)(2,1)S(1)} %bitcast.33, bf16[8,2,64,128]{3,2,1,0:T(8,128)(2,1)S(1)} %bitcast.34, bf16[4,256,896]{2,1,0:T(8,128)(2,1)S(1)} %pad_maximum_fusion.weight_ref), custom_call_target="tpu_custom_call" | custom-call | tf_op jit(solution)/shard_map/rollout/pallas_call | solution.py:294
  (8 shorter events, 0.1 us)
Async XLA Ops:
  4.9 25.5 %all-to-all-start = ((f32[32,8,256]{2,1,0:T(8,128)}), f32[32,8,256]{2,1,0:T(8,128)S(1)}, u32[]{:S(2)}, u32[]{:S(2)}) async-start(f32[32,8,256]{2,1,0:T(8,128)} %bitcast.35), calls=%async_computation | async-start | bytes 524288 | tf_op jit(solution)/shard_map/all_to_all | solution.py:59
  60.0 4.9 %collective-permute-start.1 = (f32[64,128]{1,0:T(8,128)S(1)}, f32[64,128]{1,0:T(8,128)S(1)}, u32[]{:S(2)}, u32[]{:S(2)}) collective-permute-start(f32[64,128]{1,0:T(8,128)S(1)} %get-tuple-element.29), channel_id=1, source_target_pairs={{0,32},{32,0},{64,96},{96,64},{128,160},{160,128},{192,224},{224,1... | collective-permute-start | bytes 98312 | tf_op jit(solution)/shard_map/ppermute | solution.py:320
  61.2 6.5 %collective-permute-start = (f32[64,128]{1,0:T(8,128)S(1)}, f32[64,128]{1,0:T(8,128)S(1)}, u32[]{:S(2)}, u32[]{:S(2)}) collective-permute-start(f32[64,128]{1,0:T(8,128)S(1)} %get-tuple-element.29), channel_id=1, source_target_pairs={{0,16},{1,17},{2,18},{3,19},{4,48},{5,49},{6,50},{7,51},{8,84},{9,... | collective-permute-start | bytes 98312 | tf_op jit(solution)/shard_map/ppermute | solution.py:319
  64.9 15.6 %collective-permute-start.4 = (f32[64,256]{1,0:T(8,128)S(1)}, f32[64,256]{1,0:T(8,128)S(1)}, u32[]{:S(2)}, u32[]{:S(2)}) collective-permute-start(f32[64,256]{1,0:T(8,128)S(1)} %pad_maximum_fusion.1.pair0_ref), channel_id=1, source_target_pairs={{0,192},{32,224},{64,0},{96,32},{128,64},{160,96},{192,128},{224,1... | collective-permute-start | bytes 196616 | tf_op jit(solution)/shard_map/ppermute | solution.py:324
  65.6 15.0 %collective-permute-start.3 = (f32[64,256]{1,0:T(8,128)S(1)}, f32[64,256]{1,0:T(8,128)S(1)}, u32[]{:S(2)}, u32[]{:S(2)}) collective-permute-start(f32[64,256]{1,0:T(8,128)S(1)} %pad_maximum_fusion.1.pair0_ref), channel_id=1, source_target_pairs={{0,128},{32,160},{64,192},{96,224},{128,0},{160,32},{192,64},{224,... | collective-permute-start | bytes 196616 | tf_op jit(solution)/shard_map/ppermute | solution.py:324
  67.7 12.9 %collective-permute-start.2 = (f32[64,256]{1,0:T(8,128)S(1)}, f32[64,256]{1,0:T(8,128)S(1)}, u32[]{:S(2)}, u32[]{:S(2)}) collective-permute-start(f32[64,256]{1,0:T(8,128)S(1)} %pad_maximum_fusion.1.pair0_ref), channel_id=1, source_target_pairs={{0,64},{32,96},{64,128},{96,160},{128,192},{160,224},{192,0},{224,... | collective-permute-start | bytes 196616 | tf_op jit(solution)/shard_map/ppermute | solution.py:324
  68.7 16.2 %all-to-all-start.3 = ((bf16[16,64,128]{2,1,0:T(8,128)(2,1)}), bf16[16,64,128]{2,1,0:T(8,128)(2,1)S(1)}, u32[]{:S(2)}, u32[]{:S(2)}) async-start(bf16[16,64,128]{2,1,0:T(8,128)(2,1)} %bitcast.3), calls=%async_computation.3 | async-start | bytes 524288 | tf_op jit(solution)/shard_map/all_to_all | solution.py:59
  77.1 7.9 %collective-permute-start.5 = (bf16[64,256]{1,0:T(8,128)(2,1)S(1)}, bf16[64,256]{1,0:T(8,128)(2,1)S(1)}, u32[]{:S(2)}, u32[]{:S(2)}) collective-permute-start(bf16[64,256]{1,0:T(8,128)(2,1)S(1)} %convolution_convert_fusion.2), channel_id=1, source_target_pairs={{16,0},{17,1},{18,2},{19,3},{12,32},{13,33},{14,34},{15,35},{20,64... | collective-permute-start | bytes 98312 | tf_op jit(solution)/shard_map/ppermute | solution.py:328
  78.5 3.1 %copy-start.1 = (bf16[1024,896]{1,0:T(8,128)(2,1)S(1)}, bf16[1024,896]{1,0:T(8,128)(2,1)}, u32[]{:S(2)}) copy-start(bf16[1024,896]{1,0:T(8,128)(2,1)} %change_ref.1) | copy-start | bytes 5505028
  80.2 2.2 %copy-start = (f32[1024,896]{1,0:T(8,128)S(1)}, f32[1024,896]{1,0:T(8,128)}, u32[]{:S(2)}) copy-start(f32[1024,896]{1,0:T(8,128)} %error_ref.1) | copy-start | bytes 11010052
  84.9 5.1 %collective-permute-start.6 = (bf16[16,64,128]{2,1,0:T(8,128)(2,1)S(1)}, bf16[16,64,128]{2,1,0:T(8,128)(2,1)S(1)}, u32[]{:S(2)}, u32[]{:S(2)}) collective-permute-start(bf16[16,64,128]{2,1,0:T(8,128)(2,1)S(1)} %all-to-all-done.3), channel_id=1, source_target_pairs={{0,1},{1,0},{2,3},{3,2},{4,5},{5,4},{6,7},{7,6},{8,9},{9,8},{10,11... | collective-permute-start | bytes 786440 | tf_op jit(solution)/shard_map/ppermute | solution.py:336

commit v10 on v9

--- a/solution.py
+++ b/solution.py
@@ -325,9 +325,10 @@
     far_round = dot(copies, far, 1, 0, HIGH).astype(jnp.bfloat16).reshape(COLS // 2, R, LANES)
     far_round, inverse, weight, left = lax.optimization_barrier((far_round, inverse, rollout_weight, left))
     mine = lax.dynamic_index_in_dim(left, q, 1, keepdims=False).reshape(R, rows // 4)
-    far_left = lax.ppermute(dot(inverse, mine, 1, 0, HIGH).astype(jnp.bfloat16), AXES, FANOUT)
     near = exchange(far_round, AXES, SAME_CORE)
     weight = jnp.stack([weight[:, i * units : (i + 1) * units] for i in range(4)])
+    weight, mine = lax.optimization_barrier((weight, mine))
+    far_left = lax.ppermute(dot(inverse, mine, 1, 0, HIGH).astype(jnp.bfloat16), AXES, FANOUT)
     left_rows = left.transpose(0, 2, 1, 3).reshape(R, rows)
     left_round = dot(inverse, left_rows, 1, 0, HIGH).astype(jnp.bfloat16)
     new_basis, right_round = basis_part(row.astype(jnp.int32).reshape(1), inverse, [pair] + pairs, units)

time: 92 us -> 93.5 us (1.016)
  waiting for transfers between devices: 11.2 us -> 13.5 us
    ppermute x1, waiting for transfers between devices: 0.01 us -> 2.32 us  [local(): lax.ppermute(dot(inverse, mine, 1, 0, HIGH).astype(jnp.bfloat16), AXES, F...]
  transfers between devices with their start and end apart: 9 -> 9, of which waited for: 2 -> 3; matrix products, arithmetic and copies ran while one was open for 10% -> 10% of each run, Pallas kernels for 3% -> 3%
where the time goes in v10:
time: 93.5 us; the launch traced here: 93.1 us
  starting transfers between devices  31.6 us (34%)
  blocking collectives  28.8 us (31%)
  waiting for transfers between devices  13.5 us (14%)
  Pallas kernels  9.56 us (10%)
  matrix products  3.99 us (4%)
  other arithmetic  3.26 us (3%)
  local copies, waits for them, and re-layouts  1.75 us (2%)
    all_to_all x2, blocking collectives, exchange(): return lax.all_to_all(parts, axis, 0, 0, axis_index_groups=groups)  28.8 us
    all_to_all x2, starting transfers between devices, exchange(): return lax.all_to_all(parts, axis, 0, 0, axis_index_groups=groups)  20.5 us
    all_to_all x2, waiting for transfers between devices, exchange(): return lax.all_to_all(parts, axis, 0, 0, axis_index_groups=groups)  9.98 us
    pallas_call x1, Pallas kernels, left_part(): pl.pallas_call(left_kernel, in_specs=[ANY, ANY, ANY], out_specs=VMEM, out...  4.24 us
    dot_general x4, matrix products, dot(): lax.dot_general(a, b, (((ca,), (cb,)), ((), ())), precision=precision, pr...  3.99 us
    ppermute x1, starting transfers between devices, local(): other = lax.ppermute(near, 'col', PAIR)  3.97 us
    convert_element_type x1, other arithmetic, local(): total = (change.astype(jnp.float32) + error).astype(jnp.bfloat16)  2.95 us
    ppermute x3, starting transfers between devices, local(): lax.ppermute(pair, 'row', [(r, (r + 2 * k) % ROWS) for r in range(ROWS)])  2.75 us
  transfers between devices with their start and end apart: 9, of which 3 were waited for; matrix products, arithmetic and copies ran while one was open for 10% of the time, Pallas kernels for 3%

profile of v10, /device:TPU:1, one launch (start us, length us, event | category | flops | bytes accessed | tf_op | source)
XLA Modules:
  0.0 93.1 jit_solution(5130940004581167542)
XLA Ops:
  0.6 4.2 %left_part.1 = f32[8,4,8,256]{3,2,1,0:T(8,128)} custom-call(bf16[1024,896]{1,0:T(8,128)(2,1)} %change_ref.1, f32[1024,896]{1,0:T(8,128)} %error_ref.1, f32[64,896]{1,0:T(8,128)} %bitcast.36), custom_call_target="tpu_custom_call" | custom-call | flops 352321536 | bytes 5505024 | tf_op jit(solution)/shard_map/left_part/pallas_call | solution.py:102
  4.9 12.6 %all-to-all-start = ((f32[32,8,256]{2,1,0:T(8,128)}), f32[32,8,256]{2,1,0:T(8,128)S(1)}, u32[]{:S(2)}, u32[]{:S(2)}) async-start(f32[32,8,256]{2,1,0:T(8,128)} %bitcast.35), calls=%async_computation | async-start | bytes 524288 | tf_op jit(solution)/shard_map/all_to_all | solution.py:59
  17.5 3.0 %add_convert_fusion.total_ref = bf16[1024,896]{1,0:T(8,128)(2,1)S(1)} fusion(f32[1024,896]{1,0:T(8,128)} %error_ref.1, bf16[1024,896]{1,0:T(8,128)(2,1)} %change_ref.1), kind=kLoop, calls=%fused_computation.1 | loop fusion | flops 2752512 | bytes 7340032 | tf_op jit(solution)/shard_map/convert_element_type | solution.py:314
  20.4 10.0 %all-to-all-done.parts_ref = f32[32,8,256]{2,1,0:T(8,128)S(1)} async-done(((f32[32,8,256]{2,1,0:T(8,128)}), f32[32,8,256]{2,1,0:T(8,128)S(1)}, u32[]{:S(2)}, u32[]{:S(2)}) %all-to-all-start) | async-done | bytes 262176 | tf_op jit(solution)/shard_map/all_to_all | solution.py:59
  30.4 0.1 sum_share.1
  30.5 16.9 %all_to_all.20 = f32[32,8,256]{2,1,0:T(8,128)S(1)} all-to-all(f32[32,8,256]{2,1,0:T(8,128)S(1)} %sum_share.1), channel_id=1, replica_groups=mesh['row'=8,'col'=32] {'col'}, dimensions={0} | all-to-all | bytes 524288 | tf_op jit(solution)/shard_map/all_to_all | solution.py:59
  47.3 0.7 right_part.1
  48.1 11.9 %all_to_all.21.parts_ref = f32[8,96,128]{2,1,0:T(8,128)S(1)} all-to-all(f32[8,96,128]{2,1,0:T(8,128)S(1)} %right_part.1), channel_id=1, replica_groups=mesh['row'=8,'col'=32] {'row'}, dimensions={0} | all-to-all | bytes 786432 | tf_op jit(solution)/shard_map/all_to_all | solution.py:59
  60.0 1.2 %collective-permute-start.1 = (f32[64,128]{1,0:T(8,128)S(1)}, f32[64,128]{1,0:T(8,128)S(1)}, u32[]{:S(2)}, u32[]{:S(2)}) collective-permute-start(f32[64,128]{1,0:T(8,128)S(1)} %get-tuple-element.31), channel_id=1, source_target_pairs={{0,32},{32,0},{64,96},{96,64},{128,160},{160,128},{192,224},{224,1... | collective-permute-start | bytes 98312 | tf_op jit(solution)/shard_map/ppermute | solution.py:320
  61.2 1.8 %collective-permute-start = (f32[64,128]{1,0:T(8,128)S(1)}, f32[64,128]{1,0:T(8,128)S(1)}, u32[]{:S(2)}, u32[]{:S(2)}) collective-permute-start(f32[64,128]{1,0:T(8,128)S(1)} %get-tuple-element.31), channel_id=1, source_target_pairs={{0,16},{1,17},{2,18},{3,19},{4,48},{5,49},{6,50},{7,51},{8,84},{9,... | collective-permute-start | bytes 98312 | tf_op jit(solution)/shard_map/ppermute | solution.py:319
  63.0 1.9 %factor.1 = (f32[64,64]{1,0:T(8,128)S(1)}, f32[1024,64]{1,0:T(8,128)S(1)}) custom-call(f32[32,128]{1,0:T(8,128)S(1)} %get-tuple-element.29.gram_ref), custom_call_target="tpu_custom_call" | custom-call | flops 1 | bytes 1 | tf_op jit(solution)/shard_map/factor/pallas_call | solution.py:234
  64.9 0.6 collective-permute-start.4
  65.6 2.1 %collective-permute-start.3 = (f32[64,256]{1,0:T(8,128)S(1)}, f32[64,256]{1,0:T(8,128)S(1)}, u32[]{:S(2)}, u32[]{:S(2)}) collective-permute-start(f32[64,256]{1,0:T(8,128)S(1)} %pad_maximum_fusion.1.pair0_ref), channel_id=1, source_target_pairs={{0,128},{32,160},{64,192},{96,224},{128,0},{160,32},{192,64},{224,... | collective-permute-start | bytes 196616 | tf_op jit(solution)/shard_map/ppermute | solution.py:324
  67.7 0.0 collective-permute-start.2
  67.7 0.0 collective-permute-done
  67.7 1.1 %convolution_convert_fusion = bf16[1024,128]{1,0:T(8,128)(2,1)} fusion(f32[1024,64]{1,0:T(8,128)S(1)} %get-tuple-element.30, f32[64,128]{1,0:T(8,128)S(1)} %collective-permute-done), kind=kOutput, calls=%fused_computation.3 | convolution fusion | flops 50462720 | bytes 557056 | tf_op jit(solution)/shard_map/dot_general | solution.py:48
  68.7 7.9 %all-to-all-start.3 = ((bf16[16,64,128]{2,1,0:T(8,128)(2,1)}), bf16[16,64,128]{2,1,0:T(8,128)(2,1)S(1)}, u32[]{:S(2)}, u32[]{:S(2)}) async-start(bf16[16,64,128]{2,1,0:T(8,128)(2,1)} %bitcast.3), calls=%async_computation.3 | async-start | bytes 524288 | tf_op jit(solution)/shard_map/all_to_all | solution.py:59
  76.7 1.7 %slice_bitcast_fusion.3 = (bf16[1,256,896]{2,1,0:T(8,128)(2,1)S(1)}, bf16[1,256,896]{2,1,0:T(8,128)(2,1)S(1)}, bf16[1,256,896]{2,1,0:T(8,128)(2,1)S(1)}, bf16[1,256,896]{2,1,0:T(8,128)(2,1)S(1)}) fusion(bf16[256,3584]{1,0:T(8,128)(2,1)} %param.7), kind=kLoop, calls=%fused_computation.9 | loop fusion | bytes 3670016 | tf_op jit(solution)/shard_map/stack | solution.py:329
  78.4 0.0 copy-start
  78.4 0.3 pad_maximum_fusion.weight_ref
  78.7 0.3 convolution_convert_fusion.1
  79.0 0.2 convolution_convert_fusion.2
  79.1 1.4 %collective-permute-start.5 = (bf16[64,256]{1,0:T(8,128)(2,1)S(1)}, bf16[64,256]{1,0:T(8,128)(2,1)S(1)}, u32[]{:S(2)}, u32[]{:S(2)}) collective-permute-start(bf16[64,256]{1,0:T(8,128)(2,1)S(1)} %convolution_convert_fusion.2), channel_id=1, source_target_pairs={{16,0},{17,1},{18,2},{19,3},{12,32},{13,33},{14,34},{15,35},{20,64... | collective-permute-start | bytes 98312 | tf_op jit(solution)/shard_map/ppermute | solution.py:331
  80.5 0.0 collective-permute-done.4.pair3_ref
  80.5 0.0 collective-permute-done.3.pair2_ref
  80.5 0.0 collective-permute-done.2.pair1_ref
  80.5 1.0 %basis_part.1 = (f32[64,896]{1,0:T(8,128)}, bf16[64,896]{1,0:T(8,128)(2,1)S(1)}) custom-call(s32[1]{0:T(128)} %bitcast.6.row_ref, f32[64,64]{1,0:T(8,128)S(1)} %get-tuple-element.34.inverse_ref, f32[64,256]{1,0:T(8,128)S(1)} %pad_maximum_fusion.1.pair0_ref, f32[64,256]{1,0:T(8,128)S(1)} %collective-permute-done.2.pair1_ref, ...), custom_call_target="tpu_custom_call" | custom-call | tf_op jit(solution)/shard_map/basis_part/pallas_call | solution.py:263
  81.6 2.5 %add_subtract_fusion = f32[1024,896]{1,0:T(8,128)} fusion(f32[1024,896]{1,0:T(8,128)S(1)} %copy-done, bf16[1024,896]{1,0:T(8,128)(2,1)S(1)} %copy-done.1, bf16[64,1024]{1,0:T(8,128)(2,1)S(1)} %convolution_convert_fusion.1, bf16[64,896]{1,0:T(8,128)(2,1)S(1)} %get-tuple-element.36), kind=kOutput, calls=%fused_computation | convolution fusion | flops 120193024 | bytes 9420800 | tf_op jit(solution)/shard_map/dot_general | solution.py:48
  84.1 2.3 %collective-permute-done.5.left_ref = bf16[64,256]{1,0:T(8,128)(2,1)S(1)} collective-permute-done((bf16[64,256]{1,0:T(8,128)(2,1)S(1)}, bf16[64,256]{1,0:T(8,128)(2,1)S(1)}, u32[]{:S(2)}, u32[]{:S(2)}) %collective-permute-start.5) | collective-permute-done | bytes 32800 | tf_op jit(solution)/shard_map/ppermute | solution.py:331
  86.4 4.0 %collective-permute-start.6 = (bf16[16,64,128]{2,1,0:T(8,128)(2,1)S(1)}, bf16[16,64,128]{2,1,0:T(8,128)(2,1)S(1)}, u32[]{:S(2)}, u32[]{:S(2)}) collective-permute-start(bf16[16,64,128]{2,1,0:T(8,128)(2,1)S(1)} %all-to-all-done.3), channel_id=1, source_target_pairs={{0,1},{1,0},{2,3},{3,2},{4,5},{5,4},{6,7},{7,6},{8,9},{9,8},{10,11... | collective-permute-start | bytes 786440 | tf_op jit(solution)/shard_map/ppermute | solution.py:337
  90.4 1.2 %collective-permute-done.6 = bf16[16,64,128]{2,1,0:T(8,128)(2,1)S(1)} collective-permute-done((bf16[16,64,128]{2,1,0:T(8,128)(2,1)S(1)}, bf16[16,64,128]{2,1,0:T(8,128)(2,1)S(1)}, u32[]{:S(2)}, u32[]{:S(2)}) %collective-permute-start.6) | collective-permute-done | bytes 262176 | tf_op jit(solution)/shard_map/ppermute | solution.py:337
  91.6 1.6 %rollout.1 = bf16[256,3584]{1,0:T(8,128)(2,1)} custom-call(s32[1]{0:T(128)} %bitcast.13.core_ref, bf16[64,256]{1,0:T(8,128)(2,1)S(1)} %collective-permute-done.5.left_ref, bf16[8,2,64,128]{3,2,1,0:T(8,128)(2,1)S(1)} %bitcast.33, bf16[8,2,64,128]{3,2,1,0:T(8,128)(2,1)S(1)} %bitcast.34, bf16[4,256,896]{2,1,0:T(8,128)(2,1)S(1)} %pad_maximum_fusion.weight_ref), custom_call_target="tpu_custom_call" | custom-call | tf_op jit(solution)/shard_map/rollout/pallas_call | solution.py:294
  (9 shorter events, 0.1 us)
Async XLA Ops:
  4.9 25.5 %all-to-all-start = ((f32[32,8,256]{2,1,0:T(8,128)}), f32[32,8,256]{2,1,0:T(8,128)S(1)}, u32[]{:S(2)}, u32[]{:S(2)}) async-start(f32[32,8,256]{2,1,0:T(8,128)} %bitcast.35), calls=%async_computation | async-start | bytes 524288 | tf_op jit(solution)/shard_map/all_to_all | solution.py:59
  60.0 4.9 %collective-permute-start.1 = (f32[64,128]{1,0:T(8,128)S(1)}, f32[64,128]{1,0:T(8,128)S(1)}, u32[]{:S(2)}, u32[]{:S(2)}) collective-permute-start(f32[64,128]{1,0:T(8,128)S(1)} %get-tuple-element.31), channel_id=1, source_target_pairs={{0,32},{32,0},{64,96},{96,64},{128,160},{160,128},{192,224},{224,1... | collective-permute-start | bytes 98312 | tf_op jit(solution)/shard_map/ppermute | solution.py:320
  61.2 6.5 %collective-permute-start = (f32[64,128]{1,0:T(8,128)S(1)}, f32[64,128]{1,0:T(8,128)S(1)}, u32[]{:S(2)}, u32[]{:S(2)}) collective-permute-start(f32[64,128]{1,0:T(8,128)S(1)} %get-tuple-element.31), channel_id=1, source_target_pairs={{0,16},{1,17},{2,18},{3,19},{4,48},{5,49},{6,50},{7,51},{8,84},{9,... | collective-permute-start | bytes 98312 | tf_op jit(solution)/shard_map/ppermute | solution.py:319
  64.9 15.6 %collective-permute-start.4 = (f32[64,256]{1,0:T(8,128)S(1)}, f32[64,256]{1,0:T(8,128)S(1)}, u32[]{:S(2)}, u32[]{:S(2)}) collective-permute-start(f32[64,256]{1,0:T(8,128)S(1)} %pad_maximum_fusion.1.pair0_ref), channel_id=1, source_target_pairs={{0,192},{32,224},{64,0},{96,32},{128,64},{160,96},{192,128},{224,1... | collective-permute-start | bytes 196616 | tf_op jit(solution)/shard_map/ppermute | solution.py:324
  65.6 15.0 %collective-permute-start.3 = (f32[64,256]{1,0:T(8,128)S(1)}, f32[64,256]{1,0:T(8,128)S(1)}, u32[]{:S(2)}, u32[]{:S(2)}) collective-permute-start(f32[64,256]{1,0:T(8,128)S(1)} %pad_maximum_fusion.1.pair0_ref), channel_id=1, source_target_pairs={{0,128},{32,160},{64,192},{96,224},{128,0},{160,32},{192,64},{224,... | collective-permute-start | bytes 196616 | tf_op jit(solution)/shard_map/ppermute | solution.py:324
  67.7 12.9 %collective-permute-start.2 = (f32[64,256]{1,0:T(8,128)S(1)}, f32[64,256]{1,0:T(8,128)S(1)}, u32[]{:S(2)}, u32[]{:S(2)}) collective-permute-start(f32[64,256]{1,0:T(8,128)S(1)} %pad_maximum_fusion.1.pair0_ref), channel_id=1, source_target_pairs={{0,64},{32,96},{64,128},{96,160},{128,192},{160,224},{192,0},{224,... | collective-permute-start | bytes 196616 | tf_op jit(solution)/shard_map/ppermute | solution.py:324
  68.7 17.7 %all-to-all-start.3 = ((bf16[16,64,128]{2,1,0:T(8,128)(2,1)}), bf16[16,64,128]{2,1,0:T(8,128)(2,1)S(1)}, u32[]{:S(2)}, u32[]{:S(2)}) async-start(bf16[16,64,128]{2,1,0:T(8,128)(2,1)} %bitcast.3), calls=%async_computation.3 | async-start | bytes 524288 | tf_op jit(solution)/shard_map/all_to_all | solution.py:59
  76.6 5.0 %copy-start.1 = (bf16[1024,896]{1,0:T(8,128)(2,1)S(1)}, bf16[1024,896]{1,0:T(8,128)(2,1)}, u32[]{:S(2)}) copy-start(bf16[1024,896]{1,0:T(8,128)(2,1)} %change_ref.1) | copy-start | bytes 5505028
  78.4 3.2 %copy-start = (f32[1024,896]{1,0:T(8,128)S(1)}, f32[1024,896]{1,0:T(8,128)}, u32[]{:S(2)}) copy-start(f32[1024,896]{1,0:T(8,128)} %error_ref.1) | copy-start | bytes 11010052
  79.1 7.3 %collective-permute-start.5 = (bf16[64,256]{1,0:T(8,128)(2,1)S(1)}, bf16[64,256]{1,0:T(8,128)(2,1)S(1)}, u32[]{:S(2)}, u32[]{:S(2)}) collective-permute-start(bf16[64,256]{1,0:T(8,128)(2,1)S(1)} %convolution_convert_fusion.2), channel_id=1, source_target_pairs={{16,0},{17,1},{18,2},{19,3},{12,32},{13,33},{14,34},{15,35},{20,64... | collective-permute-start | bytes 98312 | tf_op jit(solution)/shard_map/ppermute | solution.py:331
  86.4 5.1 %collective-permute-start.6 = (bf16[16,64,128]{2,1,0:T(8,128)(2,1)S(1)}, bf16[16,64,128]{2,1,0:T(8,128)(2,1)S(1)}, u32[]{:S(2)}, u32[]{:S(2)}) collective-permute-start(bf16[16,64,128]{2,1,0:T(8,128)(2,1)S(1)} %all-to-all-done.3), channel_id=1, source_target_pairs={{0,1},{1,0},{2,3},{3,2},{4,5},{5,4},{6,7},{7,6},{8,9},{9,8},{10,11... | collective-permute-start | bytes 786440 | tf_op jit(solution)/shard_map/ppermute | solution.py:337
